TPU v7x, 32 devices: a whole 2x2x4 slice. The times are simulated.
32 devices in a mesh: sub: 2 (over x), dev: 16 (over z, y, core).
Axes of the slice: x: 2, y: 2, z: 4, core: 2. Of those that a mesh axis runs over, the one named last changes fastest.
Arguments:
- root_rhs: bfloat16 [256, 16384], P('dev', 'sub'), may hold values from -6 to 6
- root_inverse: bfloat16 [128, 128, 128], P('sub')
- level_rhs: bfloat16 [256, 4096], P(None, ('sub', 'dev')), may hold values from -6 to 6
- level_inverse: bfloat16 [32, 128, 128], P(('sub', 'dev'))
- level_panels: bfloat16 [32, 16, 128, 128], P(('sub', 'dev')), may hold values from -0.125 to 0.125
- level_columns: int32 [32, 16], P(('sub', 'dev')), may hold values from 0 to 127, as said below
- leaf_rhs: bfloat16 [256, 262144], P(None, ('sub', 'dev')), may hold values from -6 to 6
- leaf_inverse: bfloat16 [2048, 128, 128], P(('sub', 'dev'))
- leaf_panels: bfloat16 [2048, 6, 128, 128], P(('sub', 'dev')), may hold values from -0.21875 to 0.21875
- leaf_columns: int32 [2048, 6], P(('sub', 'dev')), may hold values from 0 to 143, as said below
- slab_order: int32 [32, 64], P(('sub', 'dev')), may hold values from 0 to 63, each once within a row
Outputs:
- slab_adjoint: bfloat16 [256, 262144], P(None, ('sub', 'dev'))
Inputs may be any that keep to these rules, and one draw needn't show every extreme that they name: `level_columns`: entries of one row are distinct. `leaf_columns`: entries of one row are distinct; values under 128 name top-separator blocks, the others second-level blocks of the device's own subcube. `slab_order`: each row is a permutation.
All inputs are finite; a program needn't handle non-finite values.
Results may differ from a plain program's by a relative error of at most 0.0059.
Values may be sent and summed in bfloat16 or wider, within the bound.
No kernel may reach another device: no remote copies, remote signals or barrier semaphores. Data moves between devices by JAX's collectives and lax.ppermute only.
A program may use at most 256 MiB of HBM per device.

v0:
```python
import jax
import jax.numpy as jnp
from jax import lax
from jax.sharding import PartitionSpec as P


def apply_inverse(inverse, vector):
    row_count = vector.shape[0]
    block_count = inverse.shape[0]
    block_width = inverse.shape[1]
    pieces = vector.reshape(row_count, block_count, block_width)
    result = jnp.einsum("rnj,nij->rni", pieces, inverse, preferred_element_type=jnp.float32)
    return result.reshape(row_count, block_count * block_width)


def pick_blocks(source, columns, block_width):
    row_count = source.shape[0]
    blocks = source.reshape(row_count, -1, block_width)
    picked = jnp.take(blocks, columns.reshape(-1), axis=1)
    return picked.reshape(row_count, columns.shape[0], columns.shape[1], block_width)


def panel_product(picked, panels):
    result = jnp.einsum("rnkj,nkij->rni", picked, panels, preferred_element_type=jnp.float32)
    return result.reshape(picked.shape[0], picked.shape[1] * picked.shape[3])


def solve_leaves(picked, leaf_rhs, leaf_panels, leaf_inverse):
    leaf_part = panel_product(picked, leaf_panels)
    leaf_residue = (leaf_rhs.astype(jnp.float32) - leaf_part).astype(jnp.bfloat16)
    return apply_inverse(leaf_inverse, leaf_residue).astype(jnp.bfloat16)


def slab_outgoing(leaf_sol, slab_order, peers, block_width):
    row_count = leaf_sol.shape[0]
    tile_count = slab_order.shape[1]
    tile_set = leaf_sol.reshape(row_count, tile_count, block_width)
    ordered = jnp.take(tile_set, slab_order[0], axis=1)
    return ordered.reshape(row_count, peers, tile_count // peers * block_width)


def on_device(
    root_rhs,
    root_inverse,
    level_rhs,
    level_inverse,
    level_panels,
    level_columns,
    leaf_rhs,
    leaf_inverse,
    leaf_panels,
    leaf_columns,
    slab_order,
):
    block_width = leaf_panels.shape[2]
    root_piece = apply_inverse(root_inverse, root_rhs).astype(jnp.bfloat16)
    partial_root = lax.all_gather(root_piece, "dev", axis=0, tiled=True)
    root_sol = lax.all_gather(partial_root, "sub", axis=1, tiled=True)
    level_picked = pick_blocks(root_sol, level_columns, block_width)
    level_part = panel_product(level_picked, level_panels)
    level_residue = (level_rhs.astype(jnp.float32) - level_part).astype(jnp.bfloat16)
    level_block = apply_inverse(level_inverse, level_residue).astype(jnp.bfloat16)
    level_sol = lax.all_gather(level_block, "dev", axis=1, tiled=True)
    source = jnp.concatenate([root_sol, level_sol], axis=1)
    picked = pick_blocks(source, leaf_columns, block_width)
    peers = lax.axis_size("dev")
    row_count = picked.shape[0]
    tile_count = leaf_panels.shape[0]
    leaf_sol = solve_leaves(picked, leaf_rhs, leaf_panels, leaf_inverse)
    outgoing = slab_outgoing(leaf_sol, slab_order, peers, block_width)
    arrived = lax.all_to_all(outgoing, "dev", split_axis=1, concat_axis=1, tiled=True)
    return arrived.reshape(row_count, tile_count * block_width)


def solution(mesh):
    in_specs = (
        P("dev", "sub"),
        P("sub", None, None),
        P(None, ("sub", "dev")),
        P(("sub", "dev"), None, None),
        P(("sub", "dev"), None, None, None),
        P(("sub", "dev"), None),
        P(None, ("sub", "dev")),
        P(("sub", "dev"), None, None),
        P(("sub", "dev"), None, None, None),
        P(("sub", "dev"), None),
        P(("sub", "dev"), None),
    )
    out_specs = P(None, ("sub", "dev"))
    return jax.shard_map(
        on_device, mesh=mesh, in_specs=in_specs, out_specs=out_specs, check_vma=False
    )
```

profile of v0, /device:TPU:13, one launch (start us, length us, event | category | flops | bytes accessed | tf_op | source)
XLA Modules:
  0.0 446.6 jit_solution(2605876743018431121)
XLA Ops:
  6.5 2.9 fusion.10
  9.5 0.8 copy.53
  10.2 0.0 all-gather.6.cloned.1.call-start
  10.3 51.3 %all-gather.4.cloned.1.call-done = bf16[256,8192]{1,0:T(8,128)(2,1)} async-done(((bf16[16,8192]{1,0:T(8,128)(2,1)}), bf16[256,8192]{1,0:T(8,128)(2,1)}) %all-gather.4.cloned.1.call-update) | async-done | bytes 4194320 | tf_op jit(solution)/shard_map/all_gather | solution.py:57
  61.6 0.0 all-gather.8.cloned.1.call-start
  61.6 0.7 fusion.28
  62.3 0.7 compare_and_fusion.2
  63.0 103.2 %all-gather.6.cloned.1.call-done = bf16[256,16384]{1,0:T(8,128)(2,1)} async-done(((bf16[256,8192]{1,0:T(8,128)(2,1)}), bf16[256,16384]{1,0:T(8,128)(2,1)}) %all-gather.6.cloned.1.call-update) | async-done | bytes 8388624 | tf_op jit(solution)/shard_map/all_gather | solution.py:58
  166.1 12.0 %copy.27 = bf16[256,16384]{0,1:T(8,128)(2,1)} copy(bf16[256,16384]{1,0:T(8,128)(2,1)} %all-gather.6.cloned.1.call-done) | data formatting | bytes 16777216 | tf_op jit(solution)/shard_map/all_gather | solution.py:58
  178.1 12.0 %copy.28 = bf16[256,128,128]{2,0,1:T(8,128)(2,1)} copy(bf16[256,128,128]{0,2,1:T(8,128)(2,1)} %bitcast.77) | data formatting | bytes 16777216 | tf_op jit(solution)/shard_map/reshape | solution.py:18
  190.2 4.1 gather_fusion
  194.3 2.3 convolution_convert_fusion.1
  196.7 0.1 copy.30
  196.8 0.1 reshape.164
  196.9 0.1 copy.24
  197.1 0.6 broadcast.127
  197.6 0.7 reduce.5
  198.3 0.1 squeeze.5
  198.4 0.1 broadcast_in_dim.34
  198.6 35.4 %all-gather.8.cloned.1.call-done = bf16[256,2048]{1,0:T(8,128)(2,1)} async-done(((bf16[256,128]{1,0:T(8,128)(2,1)}), bf16[256,2048]{1,0:T(8,128)(2,1)}) %all-gather.8.cloned.1.call-update) | async-done | bytes 1048592 | tf_op jit(solution)/shard_map/all_gather | solution.py:63
  234.0 10.4 %pad_maximum_fusion = bf16[256,18432]{1,0:T(8,128)(2,1)} fusion(bf16[256,2048]{1,0:T(8,128)(2,1)} %all-gather.8.cloned.1.call-done, bf16[256,16384]{1,0:T(8,128)(2,1)} %all-gather.6.cloned.1.call-done), kind=kLoop, calls=%fused_computation.7 | loop fusion | flops 18874368 | bytes 18874368 | tf_op jit(solution)/shard_map/concatenate | solution.py:64
  244.5 12.6 %copy.29 = bf16[256,18432]{0,1:T(8,128)(2,1)} copy(bf16[256,18432]{1,0:T(8,128)(2,1)} %pad_maximum_fusion) | data formatting | bytes 18874368 | tf_op jit(solution)/shard_map/concatenate | solution.py:64
  257.1 12.3 %copy.31 = bf16[256,144,128]{2,0,1:T(8,128)(2,1)} copy(bf16[256,144,128]{0,2,1:T(8,128)(2,1)} %bitcast.76) | data formatting | bytes 18874368 | tf_op jit(solution)/shard_map/reshape | solution.py:18
  269.5 16.7 %gather_fusion.1 = bf16[384,256,128]{2,1,0:T(8,128)(2,1)} fusion(bf16[256,144,128]{2,0,1:T(8,128)(2,1)} %copy.31, s32[1024]{0:T(1024)S(1)} %pad_clamp_fusion.1), kind=kCustom, calls=%fused_computation.1 | custom fusion | bytes 50333184 | tf_op jit(solution)/shard_map/jit(_take)/gather | solution.py:19
  286.1 18.2 %fusion = f32[64,256,128,1]{1,2,3,0:T(8,128)} fusion(bf16[64,6,128,128]{3,2,1,0:T(8,128)(2,1)} %param.19, bf16[256,64,6,128]{3,0,2,1:T(8,128)(2,1)} %bitcast.78, pred[64,6]{1,0:T(8,128)(4,1)S(1)} %copy.24), kind=kOutput, calls=%fused_computation.3 | convolution fusion | flops 3233808384 | bytes 46137728 | tf_op jit(solution)/shard_map/rnkj,nkij->rni/dot_general | solution.py:24
  304.3 8.9 %copy.32 = f32[256,8192]{1,0:T(8,128)} copy(f32[256,8192]{0,1:T(8,128)} %bitcast.82) | data formatting | bytes 16777216 | tf_op jit(solution)/shard_map/reshape | solution.py:25
  313.3 7.9 %convert_bitcast_fusion = bf16[256,64,128]{2,0,1:T(8,128)(2,1)} fusion(bf16[64,128,128]{2,1,0:T(8,128)(2,1)S(1)} %copy-done, f32[256,8192]{1,0:T(8,128)} %copy.32, bf16[256,8192]{1,0:T(8,128)(2,1)} %param.17), kind=kOutput, calls=%fused_computation.14 | convolution fusion | flops 545259520 | bytes 18874368 | tf_op jit(solution)/shard_map/rnj,nij->rni/dot_general | solution.py:12
  321.1 5.2 %gather_fusion.2 = bf16[64,256,128]{2,1,0:T(8,128)(2,1)} fusion(bf16[256,64,128]{2,0,1:T(8,128)(2,1)} %convert_bitcast_fusion, s32[1024]{0:T(1024)S(1)} %pad_clamp_fusion), kind=kCustom, calls=%fused_computation.2 | custom fusion | bytes 8388864 | tf_op jit(solution)/shard_map/jit(_take)/gather | solution.py:38
  326.3 6.4 %copy.34 = bf16[256,64,128]{0,2,1:T(8,128)(2,1)} copy(bf16[256,64,128]{2,0,1:T(8,128)(2,1)} %bitcast.80) | data formatting | bytes 8388608 | tf_op jit(solution)/shard_map/jit(_take)/gather | solution.py:38
  332.7 4.4 bitcast_select_fusion
  337.1 96.7 %all_to_all.5 = bf16[256,16,512]{0,2,1:T(8,128)(2,1)} all-to-all(bf16[256,16,512]{0,2,1:T(8,128)(2,1)S(1)} %bitcast_select_fusion), channel_id=1, replica_groups=mesh['sub'=2,'dev'=16] {'dev'}, dimensions={1} | all-to-all | bytes 8388608 | tf_op jit(solution)/shard_map/all_to_all | solution.py:71
  433.8 6.3 %copy.35 = bf16[256,8192]{1,0:T(8,128)(2,1)} copy(bf16[256,8192]{0,1:T(8,128)(2,1)} %bitcast.81) | data formatting | bytes 8388608 | tf_op jit(solution)/shard_map/reshape | solution.py:72
  (22 shorter events, 0.1 us)
Async XLA Ops:
  6.5 306.7 %copy-start = (bf16[64,128,128]{2,1,0:T(8,128)(2,1)S(1)}, bf16[64,128,128]{2,1,0:T(8,128)(2,1)}, u32[]{:S(2)}) copy-start(bf16[64,128,128]{2,1,0:T(8,128)(2,1)} %param.18) | copy-start | bytes 6291460
  6.5 55.0 %all-gather.4.cloned.1.call-start = ((), (), s32[]{:S(2)}) async-start(), calls=%async_computation.1 | async-start | bytes 4456448 | tf_op jit(solution)/shard_map/all_gather | solution.py:57
  10.2 155.9 %all-gather.6.cloned.1.call-start = ((), (), s32[]{:S(2)}) async-start(), calls=%async_computation.2 | async-start | bytes 12582912 | tf_op jit(solution)/shard_map/all_gather | solution.py:58
  61.6 172.4 %all-gather.8.cloned.1.call-start = ((), (), s32[]{:S(2)}) async-start(), calls=%async_computation.3 | async-start | bytes 1114112 | tf_op jit(solution)/shard_map/all_gather | solution.py:63
  178.1 16.2 %copy-start.2 = (bf16[256,128]{1,0:T(8,128)(2,1)S(1)}, bf16[256,128]{1,0:T(8,128)(2,1)}, u32[]{:S(2)}) copy-start(bf16[256,128]{1,0:T(8,128)(2,1)} %param.13) | copy-start | bytes 196612
  178.1 16.2 %copy-start.3 = (bf16[1,128,128]{2,1,0:T(8,128)(2,1)S(1)}, bf16[1,128,128]{2,1,0:T(8,128)(2,1)}, u32[]{:S(2)}) copy-start(bf16[1,128,128]{2,1,0:T(8,128)(2,1)} %param.14) | copy-start | bytes 98308
  178.1 18.6 %copy-start.1 = (s32[64,6]{0,1:T(8,128)S(1)}, s32[64,6]{0,1:T(8,128)}, u32[]{:S(2)}) copy-start(s32[64,6]{0,1:T(8,128)} %param.20) | copy-start | bytes 4612
  178.1 19.5 %copy-start.4 = (s32[1,64]{1,0:T(1,128)S(1)}, s32[1,64]{1,0:T(1,128)}, u32[]{:S(2)}) copy-start(s32[1,64]{1,0:T(1,128)} %param.21) | copy-start | bytes 772
Sparse Core Ops, SparseCore 0:
  10.4 51.1 all-gather.3
  63.1 102.9 all-gather.5
  196.8 37.1 all-gather.7
where the time goes:
time: 450 us; the launch traced here: 447 us
  waiting for transfers between devices  190 us (42%)
  local copies, waits for them, and re-layouts  98.4 us (22%)
  blocking collectives  96.7 us (21%)
  matrix products  31.3 us (7%)
  other arithmetic  17 us (4%)
  between operations  13.2 us (3%)
    all_gather x1, waiting for transfers between devices, on_device(): root_sol = lax.all_gather(partial_root, 'sub', axis=1, tiled=True)  103 us
    all_to_all x1, blocking collectives, on_device(): lax.all_to_all(outgoing, 'dev', split_axis=1, concat_axis=1, tiled=True)  96.7 us
    all_gather x1, waiting for transfers between devices, on_device(): partial_root = lax.all_gather(root_piece, 'dev', axis=0, tiled=True)  51.3 us
    all_gather x1, waiting for transfers between devices, on_device(): level_sol = lax.all_gather(level_block, 'dev', axis=1, tiled=True)  35.4 us
    reshape x2, local copies, waits for them, and re-layouts, pick_blocks(): blocks = source.reshape(row_count, -1, block_width)  24.4 us
    gather x2, local copies, waits for them, and re-layouts, pick_blocks(): picked = jnp.take(blocks, columns.reshape(-1), axis=1)  20.8 us
    dot_general x1, matrix products, panel_product(): jnp.einsum('rnkj,nkij->rni', picked, panels, preferred_element_type=jnp.f...  18.2 us
    dot_general x3, matrix products, apply_inverse(): jnp.einsum('rnj,nij->rni', pieces, inverse, preferred_element_type=jnp.fl...  13.1 us
  transfers between devices with their start and end apart: 3, of which 3 were waited for; matrix products, arithmetic and copies ran while one was open for 1% of the time, Pallas kernels for 0%

commit v1 on v0

v1 whole, which is shorter than its diff:
```python
import functools

import jax
import jax.numpy as jnp
from jax import lax
from jax.experimental import pallas as pl
from jax.experimental.pallas import tpu as pltpu
from jax.sharding import PartitionSpec as P

NT = (((1,), (1,)), ((), ()))


def load_source(copies):
    for copy in copies:
        copy.start()
    for copy in copies:
        copy.wait()


def pick_product(source, columns, panels):
    groups, _, rows, width = source.shape
    picked = [source[:, col].reshape(groups * rows, width) for col in columns]
    total = None
    step = 2 if len(picked) % 2 == 0 else 1
    for k in range(0, len(picked), step):
        left = jnp.concatenate(picked[k : k + step], axis=1)
        right = jnp.concatenate(panels[k : k + step], axis=1)
        term = lax.dot_general(left, right, NT, preferred_element_type=jnp.float32)
        total = term if total is None else total + term
    return total


def solve_block(rhs, part, inverse):
    residue = (rhs.astype(jnp.float32) - part).astype(jnp.bfloat16)
    return lax.dot_general(
        residue, inverse, NT, preferred_element_type=jnp.float32
    ).astype(jnp.bfloat16)


def level_kernel(columns, root_hbm, rhs, panels, inverse, out, source, sems):
    subs, groups, blocks = root_hbm.shape[:3]
    copies = []
    for s in range(subs):
        for e in range(groups):
            copies.append(
                pltpu.make_async_copy(
                    root_hbm.at[s, e],
                    source.at[e, pl.ds(s * blocks, blocks)],
                    sems.at[s * groups + e],
                )
            )
    load_source(copies)
    tiles = panels.shape[1]
    part = pick_product(
        source,
        [columns[0, k] for k in range(tiles)],
        [panels[0, k] for k in range(tiles)],
    )
    shape = rhs.shape
    solved = solve_block(rhs[...].reshape(part.shape), part, inverse[0])
    out[...] = solved.reshape(shape)


def level_solve(root, rhs, panels, inverse, columns):
    subs, groups, blocks, rows, width = root.shape
    vmem = pl.BlockSpec(memory_space=pltpu.VMEM)
    return pl.pallas_call(
        level_kernel,
        out_shape=jax.ShapeDtypeStruct((groups, rows, width), jnp.bfloat16),
        in_specs=[
            pl.BlockSpec(memory_space=pltpu.SMEM),
            pl.BlockSpec(memory_space=pl.ANY),
            vmem,
            vmem,
            vmem,
        ],
        out_specs=vmem,
        scratch_shapes=[
            pltpu.VMEM((groups, subs * blocks, rows, width), jnp.bfloat16),
            pltpu.SemaphoreType.DMA((subs * groups,)),
        ],
        compiler_params=pltpu.CompilerParams(vmem_limit_bytes=40 * 2**20),
        name="level_solve",
    )(columns, root, rhs.reshape(groups, rows, width), panels, inverse)


def leaf_kernel(per_step, order, columns, root_hbm, level_hbm, *refs):
    rhs = refs[:per_step]
    panels = refs[per_step : 2 * per_step]
    inverse = refs[2 * per_step : 3 * per_step]
    out, source, sems = refs[3 * per_step :]
    subs, groups, blocks = root_hbm.shape[:3]
    level_blocks = level_hbm.shape[0]
    step = pl.program_id(0)

    @pl.when(step == 0)
    def _():
        copies = []
        for s in range(subs):
            for e in range(groups):
                copies.append(
                    pltpu.make_async_copy(
                        root_hbm.at[s, e],
                        source.at[e, pl.ds(s * blocks, blocks)],
                        sems.at[s * groups + e],
                    )
                )
        for j in range(level_blocks):
            copies.append(
                pltpu.make_async_copy(
                    level_hbm.at[j],
                    source.at[:, subs * blocks + j],
                    sems.at[subs * groups + j],
                )
            )
        load_source(copies)

    depth = panels[0].shape[1]
    groups, _, rows, width = source.shape
    for q in range(per_step):
        tile = order[0, step * per_step + q]
        part = pick_product(
            source,
            [columns[tile, k] for k in range(depth)],
            [panels[q][0, k] for k in range(depth)],
        )
        solved = solve_block(rhs[q][...].reshape(part.shape), part, inverse[q][0])
        out[0, :, :, q * width : (q + 1) * width] = solved.reshape(groups, rows, width)


def leaf_solve(root, level, rhs, panels, inverse, order, columns, peers):
    subs, groups, blocks, rows, width = root.shape
    tiles, depth = panels.shape[:2]
    per_step = tiles // peers
    level_blocks = level.shape[0]
    rhs = rhs.reshape(groups, rows, tiles * width)

    def tile_of(q):
        return lambda i, order, columns: order[0, i * per_step + q]

    def spec(shape, index):
        return [
            pl.BlockSpec(shape, functools.partial(index, q)) for q in range(per_step)
        ]

    def rhs_index(q, i, order, columns):
        return (0, 0, order[0, i * per_step + q])

    def panel_index(q, i, order, columns):
        return (order[0, i * per_step + q], 0, 0, 0)

    def inverse_index(q, i, order, columns):
        return (order[0, i * per_step + q], 0, 0)

    return pl.pallas_call(
        functools.partial(leaf_kernel, per_step),
        out_shape=jax.ShapeDtypeStruct(
            (peers, groups, rows, per_step * width), jnp.bfloat16
        ),
        grid_spec=pltpu.PrefetchScalarGridSpec(
            num_scalar_prefetch=2,
            grid=(peers,),
            in_specs=[pl.BlockSpec(memory_space=pl.ANY)] * 2
            + spec((groups, rows, width), rhs_index)
            + spec((1, depth, width, width), panel_index)
            + spec((1, width, width), inverse_index),
            out_specs=pl.BlockSpec(
                (1, groups, rows, per_step * width),
                lambda i, order, columns: (i, 0, 0, 0),
            ),
            scratch_shapes=[
                pltpu.VMEM(
                    (groups, subs * blocks + level_blocks, rows, width), jnp.bfloat16
                ),
                pltpu.SemaphoreType.DMA((subs * groups + level_blocks,)),
            ],
        ),
        compiler_params=pltpu.CompilerParams(vmem_limit_bytes=48 * 2**20),
        name="leaf_solve",
    )(
        order,
        columns,
        root,
        level,
        *([rhs] * per_step),
        *([panels] * per_step),
        *([inverse] * per_step),
    )


def on_device(
    root_rhs,
    root_inverse,
    level_rhs,
    level_inverse,
    level_panels,
    level_columns,
    leaf_rhs,
    leaf_inverse,
    leaf_panels,
    leaf_columns,
    slab_order,
):
    width = leaf_panels.shape[2]
    subs, peers = lax.axis_size("sub"), lax.axis_size("dev")
    row_count = leaf_rhs.shape[0]
    piece_rows = root_rhs.shape[0]
    blocks = root_inverse.shape[0]
    piece = jnp.einsum(
        "rnj,nij->nri",
        root_rhs.reshape(piece_rows, blocks, width),
        root_inverse,
        preferred_element_type=jnp.float32,
    ).astype(jnp.bfloat16)
    root = lax.all_gather(piece, ("sub", "dev"), axis=0, tiled=False)
    root = root.reshape(subs, peers, blocks, piece_rows, width)
    if piece_rows % 16:
        root = root.transpose(0, 2, 1, 3, 4).reshape(subs, 1, blocks, row_count, width)
    level = level_solve(root, level_rhs, level_panels, level_inverse, level_columns)
    level = lax.all_gather(level, "dev", axis=0, tiled=False)
    outgoing = leaf_solve(
        root, level, leaf_rhs, leaf_panels, leaf_inverse, slab_order, leaf_columns, peers
    )
    outgoing = outgoing.reshape(peers, row_count, -1)
    arrived = lax.all_to_all(outgoing, "dev", split_axis=0, concat_axis=0, tiled=True)
    return arrived.transpose(1, 0, 2).reshape(row_count, -1)


def solution(mesh):
    in_specs = (
        P("dev", "sub"),
        P("sub", None, None),
        P(None, ("sub", "dev")),
        P(("sub", "dev"), None, None),
        P(("sub", "dev"), None, None, None),
        P(("sub", "dev"), None),
        P(None, ("sub", "dev")),
        P(("sub", "dev"), None, None),
        P(("sub", "dev"), None, None, None),
        P(("sub", "dev"), None),
        P(("sub", "dev"), None),
    )
    out_specs = P(None, ("sub", "dev"))
    return jax.shard_map(
        on_device, mesh=mesh, in_specs=in_specs, out_specs=out_specs, check_vma=False
    )
```

time: 450 us -> 279 us (0.62)
  local copies, waits for them, and re-layouts: 98.4 us -> 13.8 us
  waiting for transfers between devices: 190 us -> 115 us
  Pallas kernels: 0 us -> 34.8 us
  matrix products: 31.3 us -> 2.86 us
  other arithmetic: 17 us -> 0 us
    all_gather x3 -> x2, waiting for transfers between devices: 190 us -> 115 us  [the longest x1 79.2 us: on_device(): root = lax.all_gather(piece, ('sub', 'dev'), axis=0, tiled=False)]
    reshape x5 -> x1, local copies, waits for them, and re-layouts: 39.7 us -> 2.57 us  [on_device(): return arrived.transpose(1, 0, 2).reshape(row_count, -1)]
    pallas_call x0 -> x2, Pallas kernels: none -> 34.8 us  [the longest x1 32.1 us: leaf_solve(): pl.pallas_call(functools.partial(leaf_kernel, per_step), out_shape=jax.Sh...]
    gather x4 -> x0, local copies, waits for them, and re-layouts: 32.3 us -> none  [the longest x2 20.8 us: pick_blocks(): picked = jnp.take(blocks, columns.reshape(-1), axis=1)]
    dot_general x4 -> x1, matrix products: 31.3 us -> 2.86 us  [on_device(): jnp.einsum('rnj,nij->nri', root_rhs.reshape(piece_rows, blocks, width), r...]
    concatenate x1 -> x0, local copies, waits for them, and re-layouts: 12.6 us -> none  [on_device(): source = jnp.concatenate([root_sol, level_sol], axis=1)]
    all_gather x1 -> x0, local copies, waits for them, and re-layouts: 12 us -> none  [on_device(): root_sol = lax.all_gather(partial_root, 'sub', axis=1, tiled=True)]
    unnamed x13 -> x21, local copies, waits for them, and re-layouts: 0.7 us -> 11.2 us
  transfers between devices with their start and end apart: 3 -> 2, of which waited for: 3 -> 2; matrix products, arithmetic and copies ran while one was open for 1% -> 0% of each run, Pallas kernels for 0% -> 0%
where the time goes in v1:
time: 279 us; the launch traced here: 277 us
  waiting for transfers between devices  115 us (41%)
  blocking collectives  97.5 us (35%)
  Pallas kernels  34.8 us (12%)
  local copies, waits for them, and re-layouts  13.8 us (5%)
  between operations  13.4 us (5%)
  matrix products  2.86 us (1%)
    all_to_all x1, blocking collectives, on_device(): lax.all_to_all(outgoing, 'dev', split_axis=0, concat_axis=0, tiled=True)  97.5 us
    all_gather x1, waiting for transfers between devices, on_device(): root = lax.all_gather(piece, ('sub', 'dev'), axis=0, tiled=False)  79.2 us
    all_gather x1, waiting for transfers between devices, on_device(): level = lax.all_gather(level, 'dev', axis=0, tiled=False)  35.3 us
    pallas_call x1, Pallas kernels, leaf_solve(): pl.pallas_call(functools.partial(leaf_kernel, per_step), out_shape=jax.Sh...  32.1 us
    unnamed x21, local copies, waits for them, and re-layouts  11.2 us
  transfers between devices with their start and end apart: 2, of which 2 were waited for; matrix products, arithmetic and copies ran while one was open for 0% of the time, Pallas kernels for 0%

profile of v1, /device:TPU:13, one launch (start us, length us, event | category | flops | bytes accessed | tf_op | source)
XLA Modules:
  0.0 276.9 jit_solution(7025664714923598613)
XLA Ops:
  6.5 0.0 copy-start
  6.5 0.0 all-gather.5.cloned.1.call-start
  6.5 1.6 copy-done
  8.1 2.9 %convolution_convert_fusion = bf16[64,16,128]{2,1,0:T(8,128)(2,1)} fusion(bf16[64,128,128]{2,1,0:T(8,128)(2,1)S(1)} %copy-done, bf16[16,8192]{1,0:T(8,128)(2,1)} %param.11), kind=kOutput, calls=%fused_computation | convolution fusion | flops 33685504 | bytes 2621440 | tf_op jit(solution)/shard_map/rnj,nij->nri/dot_general | solution.py:209
  11.0 0.0 all-gather.5.cloned.1.call-update
  11.0 0.0 all-gather.7.cloned.1.call-start
  11.1 79.2 %all-gather.5.cloned.1.call-done = bf16[2048,16,128]{2,1,0:T(8,128)(2,1)} async-done(((bf16[64,16,128]{2,1,0:T(8,128)(2,1)}), bf16[2048,16,128]{2,1,0:T(8,128)(2,1)}) %all-gather.5.cloned.1.call-update) | async-done | bytes 8388624 | tf_op jit(solution)/shard_map/all_gather | solution.py:215
  90.3 0.0 copy-start.2
  90.3 3.4 %copy-done.2 = bf16[2048,16,128]{2,1,0:T(8,128)(2,1)S(1)} copy-done((bf16[2048,16,128]{2,1,0:T(8,128)(2,1)S(1)}, bf16[2048,16,128]{2,1,0:T(8,128)(2,1)}, u32[]{:S(2)}) %copy-start.2) | copy-done | bytes 8388632
  93.7 0.0 copy-start.4
  93.7 1.0 copy-done.4
  94.7 0.0 copy-start.5
  94.7 0.8 copy-done.5
  95.6 0.0 copy-start.6
  95.6 0.8 copy-done.6
  96.3 0.0 copy-start.7
  96.3 0.7 copy-done.7
  97.0 0.0 copy-start.9
  97.0 0.0 copy-start.8
  97.0 2.7 level_solve.1
  99.7 0.0 all-gather.7.cloned.1.call-update
  99.7 0.0 copy-done.9
  99.7 0.1 copy.16.columns
  99.8 35.3 %all-gather.7.cloned.1.call-done = bf16[256,16,128]{2,1,0:T(8,128)(2,1)} async-done(((bf16[16,16,128]{2,1,0:T(8,128)(2,1)}), bf16[256,16,128]{2,1,0:T(8,128)(2,1)}) %all-gather.7.cloned.1.call-update) | async-done | bytes 1048592 | tf_op jit(solution)/shard_map/all_gather | solution.py:220
  135.1 0.0 copy-done.8
  135.1 0.0 copy-start.1
  135.1 1.6 copy-done.1
  136.7 0.0 copy-start.3
  136.7 1.2 copy-done.3
  137.9 32.1 %leaf_solve.1 = bf16[16,16,16,512]{3,2,1,0:T(8,128)(2,1)} custom-call(s32[1,64]{1,0:T(1,128)S(1)} %copy-done.8, s32[64,6]{1,0:T(8,128)S(1)} %copy.16.columns, bf16[2,16,64,16,128]{4,3,2,1,0:T(8,128)(2,1)} %bitcast.16, bf16[16,16,16,128]{3,2,1,0:T(8,128)(2,1)S(1)} %bitcast.18, bf16[16,16,8192]{2,1,0:T(8,128)(2,1)} %bitcast.20, ...), custom_call_target="tpu_custom_call" | custom-call | tf_op jit(solution)/shard_map/leaf_solve/pallas_call | solution.py:155
  170.0 97.5 %all_to_all.5 = bf16[16,256,512]{2,1,0:T(8,128)(2,1)S(1)} all-to-all(bf16[16,256,512]{2,1,0:T(8,128)(2,1)} %bitcast.24), channel_id=1, replica_groups=mesh['sub'=2,'dev'=16] {'dev'}, dimensions={0} | all-to-all | bytes 8388608 | tf_op jit(solution)/shard_map/all_to_all | solution.py:225
  267.5 2.6 copy.19
Async XLA Ops:
  6.5 1.6 copy-start
  6.5 83.8 %all-gather.5.cloned.1.call-start = ((), (), s32[]{:S(2)}) async-start(), calls=%async_computation.1 | async-start | bytes 8650752 | tf_op jit(solution)/shard_map/all_gather | solution.py:215
  11.0 124.1 %all-gather.7.cloned.1.call-start = ((), (), s32[]{:S(2)}) async-start(), calls=%async_computation.2 | async-start | bytes 1114112 | tf_op jit(solution)/shard_map/all_gather | solution.py:220
  90.3 3.4 %copy-start.2 = (bf16[2048,16,128]{2,1,0:T(8,128)(2,1)S(1)}, bf16[2048,16,128]{2,1,0:T(8,128)(2,1)}, u32[]{:S(2)}) copy-start(bf16[2048,16,128]{2,1,0:T(8,128)(2,1)} %all-gather.5.cloned.1.call-done) | copy-start | bytes 25165828
  93.7 1.0 copy-start.4
  94.7 0.8 copy-start.5
  95.6 0.8 copy-start.6
  96.3 0.7 copy-start.7
  97.0 2.7 copy-start.9
  97.0 38.1 %copy-start.8 = (s32[1,64]{1,0:T(1,128)S(1)}, s32[1,64]{1,0:T(1,128)}, u32[]{:S(2)}) copy-start(s32[1,64]{1,0:T(1,128)} %order.1) | copy-start | bytes 772
  135.1 1.6 copy-start.1
  136.7 1.2 copy-start.3
Sparse Core Ops, SparseCore 0:
  11.1 79.1 all-gather.4
  99.8 35.2 all-gather.6

commit v2 on v1

--- a/solution.py
+++ b/solution.py
@@ -8,13 +8,10 @@
 from jax.sharding import PartitionSpec as P
 
 NT = (((1,), (1,)), ((), ()))
-
-
-def load_source(copies):
-    for copy in copies:
-        copy.start()
-    for copy in copies:
-        copy.wait()
+ANY = pl.BlockSpec(memory_space=pltpu.HBM)
+SMEM = pl.BlockSpec(memory_space=pltpu.SMEM)
+VMEM_LIMIT = 60 * 2**20
+SMALL = pl.CostEstimate(flops=1000, bytes_accessed=1000, transcendentals=0)
 
 
 def pick_product(source, columns, panels):
@@ -37,7 +34,342 @@
     ).astype(jnp.bfloat16)
 
 
-def level_kernel(columns, root_hbm, rhs, panels, inverse, out, source, sems):
+def run_copies(pairs, sems):
+    copies = [
+        pltpu.make_async_copy(src, dst, sems.at[i]) for i, (src, dst) in enumerate(pairs)
+    ]
+    for copy in copies:
+        copy.start()
+    for copy in copies:
+        copy.wait()
+
+
+def flat_permute(value, dx=0, dz=0, dy=0, dc=0):
+    step = dx * 16 + dz * 4 + dy * 2 + dc
+    return lax.ppermute(value, ("sub", "dev"), [(i, i ^ step) for i in range(32)])
+
+
+def after(values, event):
+    return lax.optimization_barrier((values, event))[0]
+
+
+SIDES = ((0, 0), (1, 0), (0, 1), (1, 1))
+
+
+def gather_root(piece):
+    found = {}
+
+    def plane(dz, base):
+        found[0, dz, 0, 0] = base
+        for dx, dy in SIDES[1:]:
+            found[dx, dz, dy, 0] = flat_permute(base, dx=dx, dy=dy)
+        return [found[dx, dz, dy, 0] for dx, dy in SIDES]
+
+    def chip(dz):
+        for dx, dy in SIDES:
+            found[dx, dz, dy, 1] = flat_permute(found[dx, dz, dy, 0], dc=1)
+
+    near = flat_permute(piece, dz=1)
+    far = flat_permute(piece, dz=2)
+    own_plane = plane(0, piece)
+    last = flat_permute(after(piece, near), dz=3)
+    near_plane = plane(1, after(near, own_plane))
+    chip(0)
+    plane(2, after(far, own_plane))
+    chip(1)
+    plane(3, after(last, near_plane))
+    chip(2)
+    chip(3)
+    return found
+
+
+def piece_pairs(keys, pieces, source, groups):
+    me_sub, me_dev = lax.axis_index("sub"), lax.axis_index("dev")
+    pairs = []
+    for (dx, dz, dy, dc), piece in zip(keys, pieces):
+        blocks = piece.shape[0]
+        group = (me_dev ^ (dz * 4 + dy * 2 + dc)) % groups
+        pairs.append((piece, source.at[group, pl.ds((me_sub ^ dx) * blocks, blocks)]))
+    return pairs
+
+
+def level_kernel(keys, columns, *refs):
+    count = len(keys)
+    pieces = refs[:count]
+    rhs, panels, inverse, out, source, sems = refs[count:]
+    run_copies(piece_pairs(keys, pieces, source, source.shape[0]), sems)
+    tiles = panels.shape[1]
+    part = pick_product(
+        source,
+        [columns[0, k] for k in range(tiles)],
+        [panels[0, k] for k in range(tiles)],
+    )
+    solved = solve_block(rhs[...], part, inverse[0])
+    out[...] = solved.reshape(out.shape)
+
+
+def level_block(found, rhs, panels, inverse, columns):
+    keys = tuple(sorted(found))
+    pieces = [found[key] for key in keys]
+    blocks, rows, width = pieces[0].shape
+    vmem = pl.BlockSpec(memory_space=pltpu.VMEM)
+    return pl.pallas_call(
+        functools.partial(level_kernel, keys),
+        out_shape=jax.ShapeDtypeStruct((16, rows, width), jnp.bfloat16),
+        in_specs=[SMEM] + [ANY] * len(keys) + [vmem] * 3,
+        out_specs=vmem,
+        scratch_shapes=[
+            pltpu.VMEM((16, 2 * blocks, rows, width), jnp.bfloat16),
+            pltpu.SemaphoreType.DMA((len(keys),)),
+        ],
+        compiler_params=pltpu.CompilerParams(vmem_limit_bytes=VMEM_LIMIT),
+        cost_estimate=SMALL,
+        name="level_block",
+    )(columns, *pieces, rhs, panels, inverse)
+
+
+def swap_cores(value):
+    return lax.ppermute(value, "dev", [(i, i ^ 1) for i in range(16)])
+
+
+def stack_kernel(*refs):
+    for i, ref in enumerate(refs[:-1]):
+        refs[-1][i] = ref[...]
+
+
+def gather_level(block):
+    found = [block]
+    for k in range(2, 16, 2):
+        found.append(lax.ppermute(block, "dev", [(i, i ^ k) for i in range(16)]))
+    vmem = pl.BlockSpec(memory_space=pltpu.VMEM)
+    mine = pl.pallas_call(
+        stack_kernel,
+        out_shape=jax.ShapeDtypeStruct((8,) + block.shape, block.dtype),
+        in_specs=[vmem] * 8,
+        out_specs=vmem,
+        cost_estimate=SMALL,
+        name="stack_level",
+    )(*found)
+    return mine, swap_cores(mine)
+
+
+def leaf_kernel(part_index, keys, order, columns, *refs):
+    count = len(keys)
+    pieces = refs[:count]
+    level, sibling, rhs_hbm, inverse_hbm, panels_hbm = refs[count : count + 5]
+    out, source, rhs, inverse, panels, solved, sems, panel_sems, out_sems = refs[
+        count + 5 :
+    ]
+    steps = out.shape[0]
+    me_dev = lax.axis_index("dev")
+    chip, core = me_dev // 2, me_dev % 2
+    first = source.shape[1] - steps
+
+    def tile_at(step, q):
+        return order[0, step * 4 + q]
+
+    def panel_copy(step, q):
+        spot = step * 4 + q
+        return pltpu.make_async_copy(
+            panels_hbm.at[tile_at(step, q)], panels.at[spot], panel_sems.at[spot]
+        )
+
+    groups, _, rows, width = source.shape
+    half = (me_dev // groups) ^ part_index
+    mine = pl.ds(half * groups, groups)
+    pairs = piece_pairs(keys, pieces, source, groups)
+    for i in range(level.shape[0]):
+        owner = first + (chip ^ i) * 2
+        pairs.append((level.at[i, mine], source.at[:, owner + core]))
+        pairs.append((sibling.at[i, mine], source.at[:, owner + 1 - core]))
+    pairs.append((rhs_hbm.at[half], rhs))
+    pairs.append((inverse_hbm, inverse))
+    copies = [
+        pltpu.make_async_copy(src, dst, sems.at[i]) for i, (src, dst) in enumerate(pairs)
+    ]
+    for copy in copies:
+        copy.start()
+
+    @pl.loop(0, steps)
+    def _(step):
+        for q in range(4):
+            panel_copy(step, q).start()
+
+    for copy in copies:
+        copy.wait()
+
+    depth = panels.shape[1]
+
+    @pl.loop(0, steps)
+    def _(step):
+        slot = lax.rem(step, 2)
+
+        @pl.when(step >= 2)
+        def _():
+            pltpu.make_async_copy(
+                solved.at[slot], out.at[step], out_sems.at[slot]
+            ).wait()
+
+        for q in range(4):
+            panel_copy(step, q).wait()
+        tiles = [tile_at(step, q) for q in range(4)]
+        parts = [
+            pick_product(
+                source,
+                [columns[tile, k] for k in range(depth)],
+                [panels[step * 4 + q, k] for k in range(depth)],
+            )
+            for q, tile in enumerate(tiles)
+        ]
+        for q, tile in enumerate(tiles):
+            own = rhs[:, :, pl.ds(pl.multiple_of(tile * width, width), width)]
+            done = solve_block(own.reshape(parts[q].shape), parts[q], inverse[tile])
+            solved[slot, :, :, q * width : (q + 1) * width] = done.reshape(
+                groups, rows, width
+            )
+        pltpu.make_async_copy(solved.at[slot], out.at[step], out_sems.at[slot]).start()
+
+    for i in range(2):
+        pltpu.make_async_copy(solved.at[i], out.at[i], out_sems.at[i]).wait()
+
+
+def leaf_part(
+    part_index, found, level, rhs, panels, inverse, order, columns
+):
+    keys = tuple(sorted(key for key in found if key[1] // 2 == part_index))
+    pieces = [found[key] for key in keys]
+    blocks, rows, width = pieces[0].shape
+    groups = 8
+    tiles, depth = panels.shape[:2]
+    level_blocks = 16
+    return pl.pallas_call(
+        functools.partial(leaf_kernel, part_index, keys),
+        out_shape=jax.ShapeDtypeStruct(
+            (level_blocks, groups, rows, 4 * width), jnp.bfloat16
+        ),
+        in_specs=[SMEM] * 2 + [ANY] * (len(keys) + 5),
+        out_specs=ANY,
+        scratch_shapes=[
+            pltpu.VMEM((groups, 2 * blocks + level_blocks, rows, width), jnp.bfloat16),
+            pltpu.VMEM((groups, rows, tiles * width), jnp.bfloat16),
+            pltpu.VMEM((tiles, width, width), jnp.bfloat16),
+            pltpu.VMEM((tiles, depth, width, width), jnp.bfloat16),
+            pltpu.VMEM((2, groups, rows, 4 * width), jnp.bfloat16),
+            pltpu.SemaphoreType.DMA((len(keys) + level_blocks + 2,)),
+            pltpu.SemaphoreType.DMA((tiles,)),
+            pltpu.SemaphoreType.DMA((2,)),
+        ],
+        compiler_params=pltpu.CompilerParams(vmem_limit_bytes=VMEM_LIMIT),
+        cost_estimate=SMALL,
+        name="leaf_part",
+    )(
+        order,
+        columns,
+        *pieces,
+        *level,
+        rhs.reshape(2, groups, rows, tiles * width),
+        inverse,
+        panels,
+    )
+
+
+def place_kernel(part_index, arrived, *refs):
+    out, held, in_sems, out_sems = refs[-4:]
+    count, groups, _, span = arrived.shape
+    inward = [
+        pltpu.make_async_copy(arrived.at[k], held.at[k], in_sems.at[k])
+        for k in range(count)
+    ]
+    for copy in inward:
+        copy.start()
+    outward = [
+        pltpu.make_async_copy(
+            held.at[k],
+            out.at[(k // groups) ^ part_index, :, :, pl.ds(k * span, span)],
+            out_sems.at[k],
+        )
+        for k in range(count)
+    ]
+    for k in range(count):
+        inward[k].wait()
+        outward[k].start()
+    for copy in outward:
+        copy.wait()
+
+
+def place_part(part_index, arrived, before):
+    count, groups, rows, span = arrived.shape
+    extra = [] if before is None else [before]
+    return pl.pallas_call(
+        functools.partial(place_kernel, part_index),
+        out_shape=jax.ShapeDtypeStruct((2, groups, rows, count * span), jnp.bfloat16),
+        in_specs=[ANY] * (1 + len(extra)),
+        out_specs=ANY,
+        scratch_shapes=[
+            pltpu.VMEM((count, groups, rows, span), jnp.bfloat16),
+            pltpu.SemaphoreType.DMA((count,)),
+            pltpu.SemaphoreType.DMA((count,)),
+        ],
+        input_output_aliases={} if before is None else {1: 0},
+        compiler_params=pltpu.CompilerParams(vmem_limit_bytes=VMEM_LIMIT),
+        cost_estimate=SMALL,
+        name="place_part",
+    )(arrived, *extra)
+
+
+def on_device_pairs(
+    root_rhs,
+    root_inverse,
+    level_rhs,
+    level_inverse,
+    level_panels,
+    level_columns,
+    leaf_rhs,
+    leaf_inverse,
+    leaf_panels,
+    leaf_columns,
+    slab_order,
+):
+    width = leaf_panels.shape[2]
+    piece = jnp.einsum(
+        "rnj,nij->nri",
+        root_rhs.reshape(root_rhs.shape[0], root_inverse.shape[0], width),
+        root_inverse,
+        preferred_element_type=jnp.float32,
+    ).astype(jnp.bfloat16)
+    found = gather_root(piece)
+    block = level_block(found, level_rhs, level_panels, level_inverse, level_columns)
+    level = gather_level(block)
+
+    def leaf_of(part_index):
+        return leaf_part(
+            part_index,
+            found,
+            level,
+            leaf_rhs,
+            leaf_panels,
+            leaf_inverse,
+            slab_order,
+            leaf_columns,
+        )
+
+    def exchange(value):
+        return lax.all_to_all(value, "dev", split_axis=0, concat_axis=0, tiled=True)
+
+    out = None
+    for part_index in range(2):
+        out = place_part(part_index, exchange(leaf_of(part_index)), out)
+    return out.reshape(leaf_rhs.shape)
+
+
+def load_source(copies):
+    for copy in copies:
+        copy.start()
+    for copy in copies:
+        copy.wait()
+
+
+def level_kernel_any(columns, root_hbm, rhs, panels, inverse, out, source, sems):
     subs, groups, blocks = root_hbm.shape[:3]
     copies = []
     for s in range(subs):
@@ -65,7 +397,7 @@
     subs, groups, blocks, rows, width = root.shape
     vmem = pl.BlockSpec(memory_space=pltpu.VMEM)
     return pl.pallas_call(
-        level_kernel,
+        level_kernel_any,
         out_shape=jax.ShapeDtypeStruct((groups, rows, width), jnp.bfloat16),
         in_specs=[
             pl.BlockSpec(memory_space=pltpu.SMEM),
@@ -84,7 +416,7 @@
     )(columns, root, rhs.reshape(groups, rows, width), panels, inverse)
 
 
-def leaf_kernel(per_step, order, columns, root_hbm, level_hbm, *refs):
+def leaf_kernel_any(per_step, order, columns, root_hbm, level_hbm, *refs):
     rhs = refs[:per_step]
     panels = refs[per_step : 2 * per_step]
     inverse = refs[2 * per_step : 3 * per_step]
@@ -153,7 +485,7 @@
         return (order[0, i * per_step + q], 0, 0)
 
     return pl.pallas_call(
-        functools.partial(leaf_kernel, per_step),
+        functools.partial(leaf_kernel_any, per_step),
         out_shape=jax.ShapeDtypeStruct(
             (peers, groups, rows, per_step * width), jnp.bfloat16
         ),
@@ -188,7 +520,7 @@
     )
 
 
-def on_device(
+def on_device_any(
     root_rhs,
     root_inverse,
     level_rhs,
@@ -241,6 +573,8 @@
         P(("sub", "dev"), None),
     )
     out_specs = P(None, ("sub", "dev"))
+    fits = mesh.shape["sub"] == 2 and mesh.shape["dev"] == 16
+    on_device = on_device_pairs if fits else on_device_any
     return jax.shard_map(
         on_device, mesh=mesh, in_specs=in_specs, out_specs=out_specs, check_vma=False
     )

time: 279 us -> 223 us (0.80)
  blocking collectives: 97.5 us -> 0 us
  starting transfers between devices: 0.04 us -> 49.1 us
  between operations: 13.4 us -> 0.28 us
  Pallas kernels: 34.8 us -> 44.3 us
  local copies, waits for them, and re-layouts: 13.8 us -> 4.95 us
  waiting for transfers between devices: 115 us -> 122 us
    all_gather x2 -> x0, waiting for transfers between devices: 115 us -> none  [the longest x1 79.2 us: on_device(): root = lax.all_gather(piece, ('sub', 'dev'), axis=0, tiled=False)]
    all_to_all x1 -> x0, blocking collectives: 97.5 us -> none  [on_device(): lax.all_to_all(outgoing, 'dev', split_axis=0, concat_axis=0, tiled=True)]
    all_to_all x0 -> x2, waiting for transfers between devices: none -> 76.9 us  [exchange(): return lax.all_to_all(value, 'dev', split_axis=0, concat_axis=0, tiled=True)]
    ppermute x0 -> x39, waiting for transfers between devices: none -> 44.8 us  [the longest x31 36 us: flat_permute(): lax.ppermute(value, ('sub', 'dev'), [(i, i ^ step) for i in range(32)])]
    ppermute x0 -> x39, starting transfers between devices: none -> 37.2 us  [the longest x31 28.3 us: flat_permute(): lax.ppermute(value, ('sub', 'dev'), [(i, i ^ step) for i in range(32)])]
    all_to_all x0 -> x2, starting transfers between devices: none -> 11.9 us  [exchange(): return lax.all_to_all(value, 'dev', split_axis=0, concat_axis=0, tiled=True)]
    pallas_call x2 -> x6, Pallas kernels: 34.8 us -> 44.3 us  [the longest x2 31.2 us: leaf_part(): pl.pallas_call(functools.partial(leaf_kernel, part_index, keys), out_shap...]
    unnamed x21 -> x83, local copies, waits for them, and re-layouts: 11.2 us -> 4.95 us
  transfers between devices with their start and end apart: 2 -> 41, of which waited for: 2 -> 19; matrix products, arithmetic and copies ran while one was open for 0% -> 0% of each run, Pallas kernels for 0% -> 8%
where the time goes in v2:
time: 223 us; the launch traced here: 222 us
  waiting for transfers between devices  122 us (55%)
  starting transfers between devices  49.1 us (22%)
  Pallas kernels  44.3 us (20%)
  local copies, waits for them, and re-layouts  4.95 us (2%)
    all_to_all x2, waiting for transfers between devices, exchange(): return lax.all_to_all(value, 'dev', split_axis=0, concat_axis=0, tiled=True)  76.9 us
    ppermute x31, waiting for transfers between devices, flat_permute(): lax.ppermute(value, ('sub', 'dev'), [(i, i ^ step) for i in range(32)])  36 us
    pallas_call x2, Pallas kernels, leaf_part(): pl.pallas_call(functools.partial(leaf_kernel, part_index, keys), out_shap...  31.2 us
    ppermute x31, starting transfers between devices, flat_permute(): lax.ppermute(value, ('sub', 'dev'), [(i, i ^ step) for i in range(32)])  28.3 us
    all_to_all x2, starting transfers between devices, exchange(): return lax.all_to_all(value, 'dev', split_axis=0, concat_axis=0, tiled=True)  11.9 us
    ppermute x7, waiting for transfers between devices, gather_level(): found.append(lax.ppermute(block, 'dev', [(i, i ^ k) for i in range(16)]))  7.74 us
    ppermute x7, starting transfers between devices, gather_level(): found.append(lax.ppermute(block, 'dev', [(i, i ^ k) for i in range(16)]))  7.18 us
    pallas_call x1, Pallas kernels, level_block(): pl.pallas_call(functools.partial(level_kernel, keys), out_shape=jax.Shape...  6.04 us
  transfers between devices with their start and end apart: 41, of which 19 were waited for; matrix products, arithmetic and copies ran while one was open for 0% of the time, Pallas kernels for 8%

profile of v2, /device:TPU:13, one launch (start us, length us, event | category | flops | bytes accessed | tf_op | source)
XLA Modules:
  0.0 222.5 jit_solution(2044880107985407349)
XLA Ops:
  0.0 1.6 copy-done
  1.6 2.1 convolution_convert_fusion.refs_0_
  6.6 1.8 collective-permute-start.23
  8.4 2.6 %collective-permute-done.7.refs_4_ = bf16[64,16,128]{2,1,0:T(8,128)(2,1)S(1)} collective-permute-done((bf16[64,16,128]{2,1,0:T(8,128)(2,1)S(1)}, bf16[64,16,128]{2,1,0:T(8,128)(2,1)S(1)}, u32[]{:S(2)}, u32[]{:S(2)}) %collective-permute-start.7) | collective-permute-done | bytes 262176 | tf_op jit(solution)/shard_map/ppermute | solution.py:49
  11.0 2.3 %collective-permute-start = (bf16[64,16,128]{2,1,0:T(8,128)(2,1)S(1)}, bf16[64,16,128]{2,1,0:T(8,128)(2,1)S(1)}, u32[]{:S(2)}, u32[]{:S(2)}) collective-permute-start(bf16[64,16,128]{2,1,0:T(8,128)(2,1)S(1)} %convolution_convert_fusion.refs_0_), channel_id=1, source_target_pairs={{0,8},{1,9},{2,10},{3,11},{4,12},{5,13},{6,14},{7,15},{8,0},{9,1},... | collective-permute-start | bytes 786440 | tf_op jit(solution)/shard_map/ppermute | solution.py:49
  14.2 4.5 %collective-permute-done.2.refs_2_ = bf16[64,16,128]{2,1,0:T(8,128)(2,1)S(1)} collective-permute-done((bf16[64,16,128]{2,1,0:T(8,128)(2,1)S(1)}, bf16[64,16,128]{2,1,0:T(8,128)(2,1)S(1)}, u32[]{:S(2)}, u32[]{:S(2)}) %collective-permute-start.2) | collective-permute-done | bytes 262176 | tf_op jit(solution)/shard_map/ppermute | solution.py:49
  20.9 9.5 %collective-permute-done.refs_8_.refs_0_ = bf16[64,16,128]{2,1,0:T(8,128)(2,1)S(1)} collective-permute-done((bf16[64,16,128]{2,1,0:T(8,128)(2,1)S(1)}, bf16[64,16,128]{2,1,0:T(8,128)(2,1)S(1)}, u32[]{:S(2)}, u32[]{:S(2)}) %collective-permute-start) | collective-permute-done | bytes 262176 | tf_op jit(solution)/shard_map/ppermute | solution.py:49
  31.6 4.4 %collective-permute-done.8.refs_12_.refs_4_ = bf16[64,16,128]{2,1,0:T(8,128)(2,1)S(1)} collective-permute-done((bf16[64,16,128]{2,1,0:T(8,128)(2,1)S(1)}, bf16[64,16,128]{2,1,0:T(8,128)(2,1)S(1)}, u32[]{:S(2)}, u32[]{:S(2)}) %collective-permute-start.8) | collective-permute-done | bytes 262176 | tf_op jit(solution)/shard_map/ppermute | solution.py:49
  41.3 4.6 %collective-permute-done.17.refs_26_.refs_10_ = bf16[64,16,128]{2,1,0:T(8,128)(2,1)S(1)} collective-permute-done((bf16[64,16,128]{2,1,0:T(8,128)(2,1)S(1)}, bf16[64,16,128]{2,1,0:T(8,128)(2,1)S(1)}, u32[]{:S(2)}, u32[]{:S(2)}) %collective-permute-start.17) | collective-permute-done | bytes 262176 | tf_op jit(solution)/shard_map/ppermute | solution.py:49
  47.2 3.4 %collective-permute-done.15.refs_24_.refs_8_ = bf16[64,16,128]{2,1,0:T(8,128)(2,1)S(1)} collective-permute-done((bf16[64,16,128]{2,1,0:T(8,128)(2,1)S(1)}, bf16[64,16,128]{2,1,0:T(8,128)(2,1)S(1)}, u32[]{:S(2)}, u32[]{:S(2)}) %collective-permute-start.15) | collective-permute-done | bytes 262176 | tf_op jit(solution)/shard_map/ppermute | solution.py:49
  50.6 2.1 collective-permute-start.21
  53.3 1.7 collective-permute-start.12
  55.1 3.4 %collective-permute-done.21.refs_30_.refs_14_ = bf16[64,16,128]{2,1,0:T(8,128)(2,1)S(1)} collective-permute-done((bf16[64,16,128]{2,1,0:T(8,128)(2,1)S(1)}, bf16[64,16,128]{2,1,0:T(8,128)(2,1)S(1)}, u32[]{:S(2)}, u32[]{:S(2)}) %collective-permute-start.21) | collective-permute-done | bytes 262176 | tf_op jit(solution)/shard_map/ppermute | solution.py:49
  58.5 3.1 %collective-permute-start.18 = (bf16[64,16,128]{2,1,0:T(8,128)(2,1)S(1)}, bf16[64,16,128]{2,1,0:T(8,128)(2,1)S(1)}, u32[]{:S(2)}, u32[]{:S(2)}) collective-permute-start(bf16[64,16,128]{2,1,0:T(8,128)(2,1)S(1)} %collective-permute-done.17.refs_26_.refs_10_), channel_id=1, source_target_pairs={{0,1},{1,0},{2,3},{3,2},{4,5},{5,4},{6,7},{7,6},{8,9},{9,8},{10,11... | collective-permute-start | bytes 786440 | tf_op jit(solution)/shard_map/ppermute | solution.py:49
  61.6 2.5 %collective-permute-done.19.refs_28_.refs_12_ = bf16[64,16,128]{2,1,0:T(8,128)(2,1)S(1)} collective-permute-done((bf16[64,16,128]{2,1,0:T(8,128)(2,1)S(1)}, bf16[64,16,128]{2,1,0:T(8,128)(2,1)S(1)}, u32[]{:S(2)}, u32[]{:S(2)}) %collective-permute-start.19) | collective-permute-done | bytes 262176 | tf_op jit(solution)/shard_map/ppermute | solution.py:49
  64.1 1.8 collective-permute-start.16
  69.3 6.0 %level_block.1.refs_0_ = bf16[16,16,128]{2,1,0:T(8,128)(2,1)} custom-call(s32[1,16]{1,0:T(1,128)} %columns.3, bf16[64,16,128]{2,1,0:T(8,128)(2,1)} %copy-done.1, bf16[64,16,128]{2,1,0:T(8,128)(2,1)} %copy-done.9, bf16[64,16,128]{2,1,0:T(8,128)(2,1)} %copy-done.6, bf16[64,16,128]{2,1,0:T(8,128)(2,1)} %copy-done.14, bf16[64,16,128]{2,1,0:T(8,128)(2,1)} %copy-done.3, ...), custom_call_target="tpu_custom_call" | custom-call | flops 1000 | bytes 1000 | tf_op jit(solution)/shard_map/level_block/pallas_call | solution.py:116
  75.3 2.8 %collective-permute-start.37 = (bf16[16,16,128]{2,1,0:T(8,128)(2,1)}, bf16[16,16,128]{2,1,0:T(8,128)(2,1)S(1)}, u32[]{:S(2)}, u32[]{:S(2)}) collective-permute-start(bf16[16,16,128]{2,1,0:T(8,128)(2,1)} %level_block.1.refs_0_), channel_id=1, source_target_pairs={{0,14},{1,15},{2,12},{3,13},{4,10},{5,11},{6,8},{7,9},{8,6},{9,7},... | collective-permute-start | bytes 196616 | tf_op jit(solution)/shard_map/ppermute | solution.py:143
  78.1 2.5 %collective-permute-start.35 = (bf16[16,16,128]{2,1,0:T(8,128)(2,1)}, bf16[16,16,128]{2,1,0:T(8,128)(2,1)S(1)}, u32[]{:S(2)}, u32[]{:S(2)}) collective-permute-start(bf16[16,16,128]{2,1,0:T(8,128)(2,1)} %level_block.1.refs_0_), channel_id=1, source_target_pairs={{0,10},{1,11},{2,8},{3,9},{4,14},{5,15},{6,12},{7,13},{8,2},{9,3},... | collective-permute-start | bytes 196616 | tf_op jit(solution)/shard_map/ppermute | solution.py:143
  81.7 3.3 %collective-permute-done.37.refs_7_ = bf16[16,16,128]{2,1,0:T(8,128)(2,1)S(1)} collective-permute-done((bf16[16,16,128]{2,1,0:T(8,128)(2,1)}, bf16[16,16,128]{2,1,0:T(8,128)(2,1)S(1)}, u32[]{:S(2)}, u32[]{:S(2)}) %collective-permute-start.37) | collective-permute-done | bytes 65568 | tf_op jit(solution)/shard_map/ppermute | solution.py:143
  85.0 1.9 collective-permute-done.36.refs_6_
  88.4 1.5 collective-permute-done.34.refs_4_
  91.1 1.9 stack_level.1.refs_16_
  93.0 1.7 collective-permute-start.38
  97.3 15.6 %leaf_part.3 = bf16[16,8,16,512]{3,2,1,0:T(8,128)(2,1)} custom-call(s32[1,64]{1,0:T(1,128)} %order.3, s32[64,6]{1,0:T(8,128)} %copy.14.columns, bf16[64,16,128]{2,1,0:T(8,128)(2,1)} %copy-done.1, bf16[64,16,128]{2,1,0:T(8,128)(2,1)} %copy-done.9, bf16[64,16,128]{2,1,0:T(8,128)(2,1)} %copy-done.6, bf16[64,16,128]{2,1,0:T(8,128)(2,1)} %copy-done.14, ...), custom_call_target="tpu_custom_call" | custom-call | flops 1000 | bytes 1000 | tf_op jit(solution)/shard_map/leaf_part/pallas_call | solution.py:245
  112.9 7.0 %all-to-all-start.1 = ((bf16[16,8,16,512]{3,2,1,0:T(8,128)(2,1)}), bf16[16,8,16,512]{3,2,1,0:T(8,128)(2,1)}, u32[]{:S(2)}, u32[]{:S(2)}) async-start(bf16[16,8,16,512]{3,2,1,0:T(8,128)(2,1)} %leaf_part.3), calls=%async_computation.1 | async-start | bytes 4194304 | tf_op jit(solution)/shard_map/all_to_all | solution.py:357
  119.9 15.6 %leaf_part.2 = bf16[16,8,16,512]{3,2,1,0:T(8,128)(2,1)} custom-call(s32[1,64]{1,0:T(1,128)} %order.3, s32[64,6]{1,0:T(8,128)} %copy.14.columns, bf16[64,16,128]{2,1,0:T(8,128)(2,1)} %copy-done.4, bf16[64,16,128]{2,1,0:T(8,128)(2,1)} %copy-done.20, bf16[64,16,128]{2,1,0:T(8,128)(2,1)} %copy-done.19, bf16[64,16,128]{2,1,0:T(8,128)(2,1)} %copy-done.30, ...), custom_call_target="tpu_custom_call" | custom-call | flops 1000 | bytes 1000 | tf_op jit(solution)/shard_map/leaf_part/pallas_call | solution.py:245
  135.5 31.9 %all-to-all-done.1.arrived = bf16[16,8,16,512]{3,2,1,0:T(8,128)(2,1)} async-done(((bf16[16,8,16,512]{3,2,1,0:T(8,128)(2,1)}), bf16[16,8,16,512]{3,2,1,0:T(8,128)(2,1)}, u32[]{:S(2)}, u32[]{:S(2)}) %all-to-all-start.1) | async-done | bytes 2097184 | tf_op jit(solution)/shard_map/all_to_all | solution.py:357
  167.5 4.9 %all-to-all-start = ((bf16[16,8,16,512]{3,2,1,0:T(8,128)(2,1)}), bf16[16,8,16,512]{3,2,1,0:T(8,128)(2,1)}, u32[]{:S(2)}, u32[]{:S(2)}) async-start(bf16[16,8,16,512]{3,2,1,0:T(8,128)(2,1)} %leaf_part.2), calls=%async_computation | async-start | bytes 4194304 | tf_op jit(solution)/shard_map/all_to_all | solution.py:357
  172.4 2.6 %place_part.2.refs_0_ = bf16[2,8,16,8192]{3,2,1,0:T(8,128)(2,1)} custom-call(bf16[16,8,16,512]{3,2,1,0:T(8,128)(2,1)} %all-to-all-done.1.arrived), custom_call_target="tpu_custom_call" | custom-call | flops 1000 | bytes 1000 | tf_op jit(solution)/shard_map/place_part/pallas_call | solution.py:303
  174.9 44.9 %all-to-all-done.arrived = bf16[16,8,16,512]{3,2,1,0:T(8,128)(2,1)} async-done(((bf16[16,8,16,512]{3,2,1,0:T(8,128)(2,1)}), bf16[16,8,16,512]{3,2,1,0:T(8,128)(2,1)}, u32[]{:S(2)}, u32[]{:S(2)}) %all-to-all-start) | async-done | bytes 2097184 | tf_op jit(solution)/shard_map/all_to_all | solution.py:357
  219.9 2.6 %place_part.3 = bf16[2,8,16,8192]{3,2,1,0:T(8,128)(2,1)} custom-call(bf16[16,8,16,512]{3,2,1,0:T(8,128)(2,1)} %all-to-all-done.arrived, bf16[2,8,16,8192]{3,2,1,0:T(8,128)(2,1)} %place_part.2.refs_0_), custom_call_target="tpu_custom_call", output_to_operand_aliasing={{}: (1, {})} | custom-call | flops 1000 | bytes 1000 | tf_op jit(solution)/shard_map/place_part/pallas_call | solution.py:303
  (140 shorter events, 23.8 us)
Async XLA Ops:
  3.7 7.2 %collective-permute-start.7 = (bf16[64,16,128]{2,1,0:T(8,128)(2,1)S(1)}, bf16[64,16,128]{2,1,0:T(8,128)(2,1)S(1)}, u32[]{:S(2)}, u32[]{:S(2)}) collective-permute-start(bf16[64,16,128]{2,1,0:T(8,128)(2,1)S(1)} %convolution_convert_fusion.refs_0_), channel_id=1, source_target_pairs={{0,4},{1,5},{2,6},{3,7},{4,0},{5,1},{6,2},{7,3},{8,12},{9,13},{10,... | collective-permute-start | bytes 786440 | tf_op jit(solution)/shard_map/ppermute | solution.py:49
  4.0 9.3 %collective-permute-start.3 = (bf16[64,16,128]{2,1,0:T(8,128)(2,1)S(1)}, bf16[64,16,128]{2,1,0:T(8,128)(2,1)S(1)}, u32[]{:S(2)}, u32[]{:S(2)}) collective-permute-start(bf16[64,16,128]{2,1,0:T(8,128)(2,1)S(1)} %convolution_convert_fusion.refs_0_), channel_id=1, source_target_pairs={{0,18},{1,19},{2,16},{3,17},{4,22},{5,23},{6,20},{7,21},{8,26},{9,... | collective-permute-start | bytes 786440 | tf_op jit(solution)/shard_map/ppermute | solution.py:49
  5.1 13.6 %collective-permute-start.2 = (bf16[64,16,128]{2,1,0:T(8,128)(2,1)S(1)}, bf16[64,16,128]{2,1,0:T(8,128)(2,1)S(1)}, u32[]{:S(2)}, u32[]{:S(2)}) collective-permute-start(bf16[64,16,128]{2,1,0:T(8,128)(2,1)S(1)} %convolution_convert_fusion.refs_0_), channel_id=1, source_target_pairs={{0,2},{1,3},{2,0},{3,1},{4,6},{5,7},{6,4},{7,5},{8,10},{9,11},{10,... | collective-permute-start | bytes 786440 | tf_op jit(solution)/shard_map/ppermute | solution.py:49
  6.4 12.4 %collective-permute-start.1 = (bf16[64,16,128]{2,1,0:T(8,128)(2,1)S(1)}, bf16[64,16,128]{2,1,0:T(8,128)(2,1)S(1)}, u32[]{:S(2)}, u32[]{:S(2)}) collective-permute-start(bf16[64,16,128]{2,1,0:T(8,128)(2,1)S(1)} %convolution_convert_fusion.refs_0_), channel_id=1, source_target_pairs={{0,16},{1,17},{2,18},{3,19},{4,20},{5,21},{6,22},{7,23},{8,24},{9,... | collective-permute-start | bytes 786440 | tf_op jit(solution)/shard_map/ppermute | solution.py:49
  6.6 13.9 %collective-permute-start.23 = (bf16[64,16,128]{2,1,0:T(8,128)(2,1)S(1)}, bf16[64,16,128]{2,1,0:T(8,128)(2,1)S(1)}, u32[]{:S(2)}, u32[]{:S(2)}) collective-permute-start(bf16[64,16,128]{2,1,0:T(8,128)(2,1)S(1)} %convolution_convert_fusion.refs_0_), channel_id=1, source_target_pairs={{0,1},{1,0},{2,3},{3,2},{4,5},{5,4},{6,7},{7,6},{8,9},{9,8},{10,11... | collective-permute-start | bytes 786440 | tf_op jit(solution)/shard_map/ppermute | solution.py:49
  11.0 19.5 %collective-permute-start = (bf16[64,16,128]{2,1,0:T(8,128)(2,1)S(1)}, bf16[64,16,128]{2,1,0:T(8,128)(2,1)S(1)}, u32[]{:S(2)}, u32[]{:S(2)}) collective-permute-start(bf16[64,16,128]{2,1,0:T(8,128)(2,1)S(1)} %convolution_convert_fusion.refs_0_), channel_id=1, source_target_pairs={{0,8},{1,9},{2,10},{3,11},{4,12},{5,13},{6,14},{7,15},{8,0},{9,1},... | collective-permute-start | bytes 786440 | tf_op jit(solution)/shard_map/ppermute | solution.py:49
  13.3 22.8 %collective-permute-start.8 = (bf16[64,16,128]{2,1,0:T(8,128)(2,1)S(1)}, bf16[64,16,128]{2,1,0:T(8,128)(2,1)S(1)}, u32[]{:S(2)}, u32[]{:S(2)}) collective-permute-start(bf16[64,16,128]{2,1,0:T(8,128)(2,1)S(1)} %convolution_convert_fusion.refs_0_), channel_id=1, source_target_pairs={{0,12},{1,13},{2,14},{3,15},{4,8},{5,9},{6,10},{7,11},{8,4},{9,5},... | collective-permute-start | bytes 786440 | tf_op jit(solution)/shard_map/ppermute | solution.py:49
  18.7 17.8 %collective-permute-start.28 = (bf16[64,16,128]{2,1,0:T(8,128)(2,1)S(1)}, bf16[64,16,128]{2,1,0:T(8,128)(2,1)S(1)}, u32[]{:S(2)}, u32[]{:S(2)}) collective-permute-start(bf16[64,16,128]{2,1,0:T(8,128)(2,1)S(1)} %collective-permute-done.3.refs_18_.refs_10_), channel_id=1, source_target_pairs={{0,1},{1,0},{2,3},{3,2},{4,5},{5,4},{6,7},{7,6},{8,9},{9,8},{10,11... | collective-permute-start | bytes 786440 | tf_op jit(solution)/shard_map/ppermute | solution.py:49
  19.3 17.4 %collective-permute-start.11 = (bf16[64,16,128]{2,1,0:T(8,128)(2,1)S(1)}, bf16[64,16,128]{2,1,0:T(8,128)(2,1)S(1)}, u32[]{:S(2)}, u32[]{:S(2)}) collective-permute-start(bf16[64,16,128]{2,1,0:T(8,128)(2,1)S(1)} %collective-permute-done.7.refs_4_), channel_id=1, source_target_pairs={{0,18},{1,19},{2,16},{3,17},{4,22},{5,23},{6,20},{7,21},{8,26},{9,... | collective-permute-start | bytes 786440 | tf_op jit(solution)/shard_map/ppermute | solution.py:49
  20.5 16.6 %collective-permute-start.10 = (bf16[64,16,128]{2,1,0:T(8,128)(2,1)S(1)}, bf16[64,16,128]{2,1,0:T(8,128)(2,1)S(1)}, u32[]{:S(2)}, u32[]{:S(2)}) collective-permute-start(bf16[64,16,128]{2,1,0:T(8,128)(2,1)S(1)} %collective-permute-done.7.refs_4_), channel_id=1, source_target_pairs={{0,2},{1,3},{2,0},{3,1},{4,6},{5,7},{6,4},{7,5},{8,10},{9,11},{10,... | collective-permute-start | bytes 786440 | tf_op jit(solution)/shard_map/ppermute | solution.py:49
  30.4 7.8 %collective-permute-start.9 = (bf16[64,16,128]{2,1,0:T(8,128)(2,1)S(1)}, bf16[64,16,128]{2,1,0:T(8,128)(2,1)S(1)}, u32[]{:S(2)}, u32[]{:S(2)}) collective-permute-start(bf16[64,16,128]{2,1,0:T(8,128)(2,1)S(1)} %collective-permute-done.7.refs_4_), channel_id=1, source_target_pairs={{0,16},{1,17},{2,18},{3,19},{4,20},{5,21},{6,22},{7,23},{8,24},{9,... | collective-permute-start | bytes 786440 | tf_op jit(solution)/shard_map/ppermute | solution.py:49
  36.6 4.5 %collective-permute-start.27 = (bf16[64,16,128]{2,1,0:T(8,128)(2,1)S(1)}, bf16[64,16,128]{2,1,0:T(8,128)(2,1)S(1)}, u32[]{:S(2)}, u32[]{:S(2)}) collective-permute-start(bf16[64,16,128]{2,1,0:T(8,128)(2,1)S(1)} %collective-permute-done.1.refs_16_.refs_8_), channel_id=1, source_target_pairs={{0,1},{1,0},{2,3},{3,2},{4,5},{5,4},{6,7},{7,6},{8,9},{9,8},{10,11... | collective-permute-start | bytes 786440 | tf_op jit(solution)/shard_map/ppermute | solution.py:49
  37.1 8.8 %collective-permute-start.17 = (bf16[64,16,128]{2,1,0:T(8,128)(2,1)S(1)}, bf16[64,16,128]{2,1,0:T(8,128)(2,1)S(1)}, u32[]{:S(2)}, u32[]{:S(2)}) collective-permute-start(bf16[64,16,128]{2,1,0:T(8,128)(2,1)S(1)} %collective-permute-done.refs_8_.refs_0_), channel_id=1, source_target_pairs={{0,18},{1,19},{2,16},{3,17},{4,22},{5,23},{6,20},{7,21},{8,26},{9,... | collective-permute-start | bytes 786440 | tf_op jit(solution)/shard_map/ppermute | solution.py:49
  38.2 12.4 %collective-permute-start.15 = (bf16[64,16,128]{2,1,0:T(8,128)(2,1)S(1)}, bf16[64,16,128]{2,1,0:T(8,128)(2,1)S(1)}, u32[]{:S(2)}, u32[]{:S(2)}) collective-permute-start(bf16[64,16,128]{2,1,0:T(8,128)(2,1)S(1)} %collective-permute-done.refs_8_.refs_0_), channel_id=1, source_target_pairs={{0,16},{1,17},{2,18},{3,19},{4,20},{5,21},{6,22},{7,23},{8,24},{9,... | collective-permute-start | bytes 786440 | tf_op jit(solution)/shard_map/ppermute | solution.py:49
  38.9 13.8 %collective-permute-start.5 = (bf16[64,16,128]{2,1,0:T(8,128)(2,1)S(1)}, bf16[64,16,128]{2,1,0:T(8,128)(2,1)S(1)}, u32[]{:S(2)}, u32[]{:S(2)}) collective-permute-start(bf16[64,16,128]{2,1,0:T(8,128)(2,1)S(1)} %collective-permute-done.refs_8_.refs_0_), channel_id=1, source_target_pairs={{0,2},{1,3},{2,0},{3,1},{4,6},{5,7},{6,4},{7,5},{8,10},{9,11},{10,... | collective-permute-start | bytes 786440 | tf_op jit(solution)/shard_map/ppermute | solution.py:49
  39.7 13.3 %collective-permute-start.4 = (bf16[64,16,128]{2,1,0:T(8,128)(2,1)S(1)}, bf16[64,16,128]{2,1,0:T(8,128)(2,1)S(1)}, u32[]{:S(2)}, u32[]{:S(2)}) collective-permute-start(bf16[64,16,128]{2,1,0:T(8,128)(2,1)S(1)} %collective-permute-done.refs_8_.refs_0_), channel_id=1, source_target_pairs={{0,1},{1,0},{2,3},{3,2},{4,5},{5,4},{6,7},{7,6},{8,9},{9,8},{10,11... | collective-permute-start | bytes 786440 | tf_op jit(solution)/shard_map/ppermute | solution.py:49
  41.2 12.1 %collective-permute-start.30 = (bf16[64,16,128]{2,1,0:T(8,128)(2,1)S(1)}, bf16[64,16,128]{2,1,0:T(8,128)(2,1)S(1)}, u32[]{:S(2)}, u32[]{:S(2)}) collective-permute-start(bf16[64,16,128]{2,1,0:T(8,128)(2,1)S(1)} %collective-permute-done.11.refs_22_.refs_14_), channel_id=1, source_target_pairs={{0,1},{1,0},{2,3},{3,2},{4,5},{5,4},{6,7},{7,6},{8,9},{9,8},{10,11... | collective-permute-start | bytes 786440 | tf_op jit(solution)/shard_map/ppermute | solution.py:49
  45.9 9.1 %collective-permute-start.26 = (bf16[64,16,128]{2,1,0:T(8,128)(2,1)S(1)}, bf16[64,16,128]{2,1,0:T(8,128)(2,1)S(1)}, u32[]{:S(2)}, u32[]{:S(2)}) collective-permute-start(bf16[64,16,128]{2,1,0:T(8,128)(2,1)S(1)} %collective-permute-done.10.refs_6_), channel_id=1, source_target_pairs={{0,1},{1,0},{2,3},{3,2},{4,5},{5,4},{6,7},{7,6},{8,9},{9,8},{10,11... | collective-permute-start | bytes 786440 | tf_op jit(solution)/shard_map/ppermute | solution.py:49
  50.6 7.9 %collective-permute-start.21 = (bf16[64,16,128]{2,1,0:T(8,128)(2,1)S(1)}, bf16[64,16,128]{2,1,0:T(8,128)(2,1)S(1)}, u32[]{:S(2)}, u32[]{:S(2)}) collective-permute-start(bf16[64,16,128]{2,1,0:T(8,128)(2,1)S(1)} %collective-permute-done.8.refs_12_.refs_4_), channel_id=1, source_target_pairs={{0,18},{1,19},{2,16},{3,17},{4,22},{5,23},{6,20},{7,21},{8,26},{9,... | collective-permute-start | bytes 786440 | tf_op jit(solution)/shard_map/ppermute | solution.py:49
  52.7 11.4 %collective-permute-start.19 = (bf16[64,16,128]{2,1,0:T(8,128)(2,1)S(1)}, bf16[64,16,128]{2,1,0:T(8,128)(2,1)S(1)}, u32[]{:S(2)}, u32[]{:S(2)}) collective-permute-start(bf16[64,16,128]{2,1,0:T(8,128)(2,1)S(1)} %collective-permute-done.8.refs_12_.refs_4_), channel_id=1, source_target_pairs={{0,16},{1,17},{2,18},{3,19},{4,20},{5,21},{6,22},{7,23},{8,24},{9,... | collective-permute-start | bytes 786440 | tf_op jit(solution)/shard_map/ppermute | solution.py:49
  53.0 12.8 %collective-permute-start.13 = (bf16[64,16,128]{2,1,0:T(8,128)(2,1)S(1)}, bf16[64,16,128]{2,1,0:T(8,128)(2,1)S(1)}, u32[]{:S(2)}, u32[]{:S(2)}) collective-permute-start(bf16[64,16,128]{2,1,0:T(8,128)(2,1)S(1)} %collective-permute-done.8.refs_12_.refs_4_), channel_id=1, source_target_pairs={{0,2},{1,3},{2,0},{3,1},{4,6},{5,7},{6,4},{7,5},{8,10},{9,11},{10,... | collective-permute-start | bytes 786440 | tf_op jit(solution)/shard_map/ppermute | solution.py:49
  53.3 12.7 %collective-permute-start.12 = (bf16[64,16,128]{2,1,0:T(8,128)(2,1)S(1)}, bf16[64,16,128]{2,1,0:T(8,128)(2,1)S(1)}, u32[]{:S(2)}, u32[]{:S(2)}) collective-permute-start(bf16[64,16,128]{2,1,0:T(8,128)(2,1)S(1)} %collective-permute-done.8.refs_12_.refs_4_), channel_id=1, source_target_pairs={{0,1},{1,0},{2,3},{3,2},{4,5},{5,4},{6,7},{7,6},{8,9},{9,8},{10,11... | collective-permute-start | bytes 786440 | tf_op jit(solution)/shard_map/ppermute | solution.py:49
  55.0 11.5 %collective-permute-start.29 = (bf16[64,16,128]{2,1,0:T(8,128)(2,1)S(1)}, bf16[64,16,128]{2,1,0:T(8,128)(2,1)S(1)}, u32[]{:S(2)}, u32[]{:S(2)}) collective-permute-start(bf16[64,16,128]{2,1,0:T(8,128)(2,1)S(1)} %collective-permute-done.9.refs_20_.refs_12_), channel_id=1, source_target_pairs={{0,1},{1,0},{2,3},{3,2},{4,5},{5,4},{6,7},{7,6},{8,9},{9,8},{10,11... | collective-permute-start | bytes 786440 | tf_op jit(solution)/shard_map/ppermute | solution.py:49
  58.5 8.1 %collective-permute-start.18 = (bf16[64,16,128]{2,1,0:T(8,128)(2,1)S(1)}, bf16[64,16,128]{2,1,0:T(8,128)(2,1)S(1)}, u32[]{:S(2)}, u32[]{:S(2)}) collective-permute-start(bf16[64,16,128]{2,1,0:T(8,128)(2,1)S(1)} %collective-permute-done.17.refs_26_.refs_10_), channel_id=1, source_target_pairs={{0,1},{1,0},{2,3},{3,2},{4,5},{5,4},{6,7},{7,6},{8,9},{9,8},{10,11... | collective-permute-start | bytes 786440 | tf_op jit(solution)/shard_map/ppermute | solution.py:49
  75.3 9.7 %collective-permute-start.37 = (bf16[16,16,128]{2,1,0:T(8,128)(2,1)}, bf16[16,16,128]{2,1,0:T(8,128)(2,1)S(1)}, u32[]{:S(2)}, u32[]{:S(2)}) collective-permute-start(bf16[16,16,128]{2,1,0:T(8,128)(2,1)} %level_block.1.refs_0_), channel_id=1, source_target_pairs={{0,14},{1,15},{2,12},{3,13},{4,10},{5,11},{6,8},{7,9},{8,6},{9,7},... | collective-permute-start | bytes 196616 | tf_op jit(solution)/shard_map/ppermute | solution.py:143
  78.1 8.8 %collective-permute-start.36 = (bf16[16,16,128]{2,1,0:T(8,128)(2,1)}, bf16[16,16,128]{2,1,0:T(8,128)(2,1)S(1)}, u32[]{:S(2)}, u32[]{:S(2)}) collective-permute-start(bf16[16,16,128]{2,1,0:T(8,128)(2,1)} %level_block.1.refs_0_), channel_id=1, source_target_pairs={{0,12},{1,13},{2,14},{3,15},{4,8},{5,9},{6,10},{7,11},{8,4},{9,5},... | collective-permute-start | bytes 196616 | tf_op jit(solution)/shard_map/ppermute | solution.py:143
  78.1 10.2 %collective-permute-start.35 = (bf16[16,16,128]{2,1,0:T(8,128)(2,1)}, bf16[16,16,128]{2,1,0:T(8,128)(2,1)S(1)}, u32[]{:S(2)}, u32[]{:S(2)}) collective-permute-start(bf16[16,16,128]{2,1,0:T(8,128)(2,1)} %level_block.1.refs_0_), channel_id=1, source_target_pairs={{0,10},{1,11},{2,8},{3,9},{4,14},{5,15},{6,12},{7,13},{8,2},{9,3},... | collective-permute-start | bytes 196616 | tf_op jit(solution)/shard_map/ppermute | solution.py:143
  80.7 9.1 %collective-permute-start.34 = (bf16[16,16,128]{2,1,0:T(8,128)(2,1)}, bf16[16,16,128]{2,1,0:T(8,128)(2,1)S(1)}, u32[]{:S(2)}, u32[]{:S(2)}) collective-permute-start(bf16[16,16,128]{2,1,0:T(8,128)(2,1)} %level_block.1.refs_0_), channel_id=1, source_target_pairs={{0,8},{1,9},{2,10},{3,11},{4,12},{5,13},{6,14},{7,15},{8,0},{9,1},... | collective-permute-start | bytes 196616 | tf_op jit(solution)/shard_map/ppermute | solution.py:143
  80.9 9.0 %collective-permute-start.33 = (bf16[16,16,128]{2,1,0:T(8,128)(2,1)}, bf16[16,16,128]{2,1,0:T(8,128)(2,1)S(1)}, u32[]{:S(2)}, u32[]{:S(2)}) collective-permute-start(bf16[16,16,128]{2,1,0:T(8,128)(2,1)} %level_block.1.refs_0_), channel_id=1, source_target_pairs={{0,6},{1,7},{2,4},{3,5},{4,2},{5,3},{6,0},{7,1},{8,14},{9,15},{10,... | collective-permute-start | bytes 196616 | tf_op jit(solution)/shard_map/ppermute | solution.py:143
  85.0 4.8 %collective-permute-start.32 = (bf16[16,16,128]{2,1,0:T(8,128)(2,1)}, bf16[16,16,128]{2,1,0:T(8,128)(2,1)S(1)}, u32[]{:S(2)}, u32[]{:S(2)}) collective-permute-start(bf16[16,16,128]{2,1,0:T(8,128)(2,1)} %level_block.1.refs_0_), channel_id=1, source_target_pairs={{0,4},{1,5},{2,6},{3,7},{4,0},{5,1},{6,2},{7,3},{8,12},{9,13},{10,... | collective-permute-start | bytes 196616 | tf_op jit(solution)/shard_map/ppermute | solution.py:143
  112.9 54.5 %all-to-all-start.1 = ((bf16[16,8,16,512]{3,2,1,0:T(8,128)(2,1)}), bf16[16,8,16,512]{3,2,1,0:T(8,128)(2,1)}, u32[]{:S(2)}, u32[]{:S(2)}) async-start(bf16[16,8,16,512]{3,2,1,0:T(8,128)(2,1)} %leaf_part.3), calls=%async_computation.1 | async-start | bytes 4194304 | tf_op jit(solution)/shard_map/all_to_all | solution.py:357
  167.5 52.4 %all-to-all-start = ((bf16[16,8,16,512]{3,2,1,0:T(8,128)(2,1)}), bf16[16,8,16,512]{3,2,1,0:T(8,128)(2,1)}, u32[]{:S(2)}, u32[]{:S(2)}) async-start(bf16[16,8,16,512]{3,2,1,0:T(8,128)(2,1)} %leaf_part.2), calls=%async_computation | async-start | bytes 4194304 | tf_op jit(solution)/shard_map/all_to_all | solution.py:357
  (50 other events, 851.6 us)

commit v3 on v2

--- a/solution.py
+++ b/solution.py
@@ -11,6 +11,7 @@
 ANY = pl.BlockSpec(memory_space=pltpu.HBM)
 SMEM = pl.BlockSpec(memory_space=pltpu.SMEM)
 VMEM_LIMIT = 60 * 2**20
+TOGETHER = 2
 SMALL = pl.CostEstimate(flops=1000, bytes_accessed=1000, transcendentals=0)
 
 
@@ -59,27 +60,26 @@
 def gather_root(piece):
     found = {}
 
-    def plane(dz, base):
-        found[0, dz, 0, 0] = base
-        for dx, dy in SIDES[1:]:
-            found[dx, dz, dy, 0] = flat_permute(base, dx=dx, dy=dy)
-        return [found[dx, dz, dy, 0] for dx, dy in SIDES]
-
-    def chip(dz):
-        for dx, dy in SIDES:
-            found[dx, dz, dy, 1] = flat_permute(found[dx, dz, dy, 0], dc=1)
+    def plane(dz, base, x_first):
+        from_x = flat_permute(base, dx=1)
+        from_y = flat_permute(base, dy=1)
+        if x_first:
+            corner = flat_permute(from_x, dy=1)
+        else:
+            corner = flat_permute(from_y, dx=1)
+        for (dx, dy), value in zip(SIDES, (base, from_x, from_y, corner)):
+            found[dx, dz, dy, 0] = value
+        return from_x, from_y
 
     near = flat_permute(piece, dz=1)
     far = flat_permute(piece, dz=2)
-    own_plane = plane(0, piece)
-    last = flat_permute(after(piece, near), dz=3)
-    near_plane = plane(1, after(near, own_plane))
-    chip(0)
-    plane(2, after(far, own_plane))
-    chip(1)
-    plane(3, after(last, near_plane))
-    chip(2)
-    chip(3)
+    sides = plane(0, piece, True)
+    last = flat_permute(after(piece, far), dz=3)
+    sides = plane(1, after(near, sides), False)
+    sides = plane(2, after(far, sides), True)
+    plane(3, after(last, sides), False)
+    for key in tuple(found):
+        found[key[:3] + (1,)] = flat_permute(found[key], dc=1)
     return found
 
 
@@ -157,7 +157,7 @@
     count = len(keys)
     pieces = refs[:count]
     level, sibling, rhs_hbm, inverse_hbm, panels_hbm = refs[count : count + 5]
-    out, source, rhs, inverse, panels, solved, sems, panel_sems, out_sems = refs[
+    out, source, rhs, inverse, panels, solved, sems, tile_sems, out_sems = refs[
         count + 5 :
     ]
     steps = out.shape[0]
@@ -167,12 +167,6 @@
 
     def tile_at(step, q):
         return order[0, step * 4 + q]
-
-    def panel_copy(step, q):
-        spot = step * 4 + q
-        return pltpu.make_async_copy(
-            panels_hbm.at[tile_at(step, q)], panels.at[spot], panel_sems.at[spot]
-        )
 
     groups, _, rows, width = source.shape
     half = (me_dev // groups) ^ part_index
@@ -182,55 +176,81 @@
         owner = first + (chip ^ i) * 2
         pairs.append((level.at[i, mine], source.at[:, owner + core]))
         pairs.append((sibling.at[i, mine], source.at[:, owner + 1 - core]))
-    pairs.append((rhs_hbm.at[half], rhs))
-    pairs.append((inverse_hbm, inverse))
+
+    def panel_copy(step, q):
+        spot = step * 4 + q
+        return pltpu.make_async_copy(
+            panels_hbm.at[tile_at(step, q)], panels.at[spot], tile_sems.at[spot]
+        )
+
     copies = [
         pltpu.make_async_copy(src, dst, sems.at[i]) for i, (src, dst) in enumerate(pairs)
     ]
     for copy in copies:
         copy.start()
 
-    @pl.loop(0, steps)
+    for step in range(TOGETHER):
+        for q in range(4):
+            panel_copy(step, q).start()
+    shared = [
+        pltpu.make_async_copy(rhs_hbm.at[half], rhs, sems.at[len(pairs)]),
+        pltpu.make_async_copy(inverse_hbm, inverse, sems.at[len(pairs) + 1]),
+    ]
+    for copy in shared:
+        copy.start()
+
+    @pl.loop(TOGETHER, steps)
     def _(step):
         for q in range(4):
             panel_copy(step, q).start()
 
-    for copy in copies:
+    for copy in copies + shared:
         copy.wait()
 
     depth = panels.shape[1]
 
-    @pl.loop(0, steps)
-    def _(step):
-        slot = lax.rem(step, 2)
-
-        @pl.when(step >= 2)
+    @pl.loop(0, steps // TOGETHER)
+    def _(turn):
+        slot = lax.rem(turn, 2)
+        spots = [(turn * TOGETHER + i, q) for i in range(TOGETHER) for q in range(4)]
+
+        def out_copy(turn):
+            return pltpu.make_async_copy(
+                solved.at[slot],
+                out.at[pl.ds(turn * TOGETHER, TOGETHER)],
+                out_sems.at[slot],
+            )
+
+        @pl.when(turn >= 2)
         def _():
-            pltpu.make_async_copy(
-                solved.at[slot], out.at[step], out_sems.at[slot]
-            ).wait()
-
-        for q in range(4):
+            out_copy(turn).wait()
+
+        for step, q in spots:
             panel_copy(step, q).wait()
-        tiles = [tile_at(step, q) for q in range(4)]
-        parts = [
-            pick_product(
-                source,
-                [columns[tile, k] for k in range(depth)],
-                [panels[step * 4 + q, k] for k in range(depth)],
+        parts = []
+        for step, q in spots:
+            tile = tile_at(step, q)
+            parts.append(
+                pick_product(
+                    source,
+                    [columns[0, tile * depth + k] for k in range(depth)],
+                    [panels[step * 4 + q, k] for k in range(depth)],
+                )
             )
-            for q, tile in enumerate(tiles)
-        ]
-        for q, tile in enumerate(tiles):
-            own = rhs[:, :, pl.ds(pl.multiple_of(tile * width, width), width)]
-            done = solve_block(own.reshape(parts[q].shape), parts[q], inverse[tile])
-            solved[slot, :, :, q * width : (q + 1) * width] = done.reshape(
+        for i, ((step, q), part) in enumerate(zip(spots, parts)):
+            tile = tile_at(step, q)
+            lanes = pl.ds(pl.multiple_of(tile * width, width), width)
+            own = rhs[:, :, lanes].reshape(part.shape)
+            done = solve_block(own, part, inverse[tile])
+            solved[slot, i // 4, :, :, q * width : (q + 1) * width] = done.reshape(
                 groups, rows, width
             )
-        pltpu.make_async_copy(solved.at[slot], out.at[step], out_sems.at[slot]).start()
+        out_copy(turn).start()
 
     for i in range(2):
-        pltpu.make_async_copy(solved.at[i], out.at[i], out_sems.at[i]).wait()
+        pltpu.make_async_copy(
+            solved.at[i], out.at[pl.ds(i * TOGETHER, TOGETHER)], out_sems.at[i]
+        ).wait()
 
 
 def leaf_part(
@@ -254,7 +274,7 @@
             pltpu.VMEM((groups, rows, tiles * width), jnp.bfloat16),
             pltpu.VMEM((tiles, width, width), jnp.bfloat16),
             pltpu.VMEM((tiles, depth, width, width), jnp.bfloat16),
-            pltpu.VMEM((2, groups, rows, 4 * width), jnp.bfloat16),
+            pltpu.VMEM((2, TOGETHER, groups, rows, 4 * width), jnp.bfloat16),
             pltpu.SemaphoreType.DMA((len(keys) + level_blocks + 2,)),
             pltpu.SemaphoreType.DMA((tiles,)),
             pltpu.SemaphoreType.DMA((2,)),
@@ -337,7 +357,8 @@
         root_inverse,
         preferred_element_type=jnp.float32,
     ).astype(jnp.bfloat16)
-    found = gather_root(piece)
+    leaf_columns = leaf_columns.reshape(1, -1)
+    found = gather_root(after(piece, leaf_columns))
     block = level_block(found, level_rhs, level_panels, level_inverse, level_columns)
     level = gather_level(block)
 

time: 223 us -> 210 us (0.942)
  waiting for transfers between devices: 122 us -> 110 us
  Pallas kernels: 44.3 us -> 37.8 us
  starting transfers between devices: 49.1 us -> 54.7 us
    ppermute x31, waiting for transfers between devices: 36 us -> 25.4 us  [flat_permute(): lax.ppermute(value, ('sub', 'dev'), [(i, i ^ step) for i in range(32)])]
    pallas_call x2, Pallas kernels: 31.2 us -> 24.7 us  [leaf_part(): pl.pallas_call(functools.partial(leaf_kernel, part_index, keys), out_shap...]
    ppermute x7, waiting for transfers between devices: 7.74 us -> 2.78 us  [gather_level(): found.append(lax.ppermute(block, 'dev', [(i, i ^ k) for i in range(16)]))]
    ppermute x7, starting transfers between devices: 7.18 us -> 10.6 us  [gather_level(): found.append(lax.ppermute(block, 'dev', [(i, i ^ k) for i in range(16)]))]
    all_to_all x2, waiting for transfers between devices: 76.9 us -> 80.1 us  [exchange(): return lax.all_to_all(value, 'dev', split_axis=0, concat_axis=0, tiled=True)]
    unnamed x83 -> x81, local copies, waits for them, and re-layouts: 4.95 us -> 4.1 us
  transfers between devices with their start and end apart: 41 -> 41, of which waited for: 19 -> 15; matrix products, arithmetic and copies ran while one was open for 0% -> 0% of each run, Pallas kernels for 8% -> 7%
where the time goes in v3:
time: 210 us
  waiting for transfers between devices  110 us (52%)
  starting transfers between devices  54.7 us (26%)
  Pallas kernels  37.8 us (18%)
  local copies, waits for them, and re-layouts  4.8 us (2%)
  matrix products  2.12 us (1%)
    all_to_all x2, waiting for transfers between devices, exchange(): return lax.all_to_all(value, 'dev', split_axis=0, concat_axis=0, tiled=True)  80.1 us
    ppermute x31, starting transfers between devices, flat_permute(): lax.ppermute(value, ('sub', 'dev'), [(i, i ^ step) for i in range(32)])  30 us
    ppermute x31, waiting for transfers between devices, flat_permute(): lax.ppermute(value, ('sub', 'dev'), [(i, i ^ step) for i in range(32)])  25.4 us
    pallas_call x2, Pallas kernels, leaf_part(): pl.pallas_call(functools.partial(leaf_kernel, part_index, keys), out_shap...  24.7 us
    all_to_all x2, starting transfers between devices, exchange(): return lax.all_to_all(value, 'dev', split_axis=0, concat_axis=0, tiled=True)  11.9 us
    ppermute x7, starting transfers between devices, gather_level(): found.append(lax.ppermute(block, 'dev', [(i, i ^ k) for i in range(16)]))  10.6 us
    pallas_call x1, Pallas kernels, level_block(): pl.pallas_call(functools.partial(level_kernel, keys), out_shape=jax.Shape...  6.03 us
    pallas_call x2, Pallas kernels, place_part(): pl.pallas_call(functools.partial(place_kernel, part_index), out_shape=jax...  5.14 us
  transfers between devices with their start and end apart: 41, of which 15 were waited for; matrix products, arithmetic and copies ran while one was open for 0% of the time, Pallas kernels for 7%

profile of v3, /device:TPU:13, one launch (start us, length us, event | category | flops | bytes accessed | tf_op | source)
XLA Modules:
  0.0 209.8 jit_solution(6069911029594257905)
XLA Ops:
  1.6 2.1 %convolution_convert_fusion.refs_0_ = bf16[64,16,128]{2,1,0:T(8,128)(2,1)S(1)} fusion(bf16[64,128,128]{2,1,0:T(8,128)(2,1)S(1)} %copy-done, bf16[16,8192]{1,0:T(8,128)(2,1)} %param.11), kind=kOutput, calls=%fused_computation | convolution fusion | flops 33685504 | bytes 2621440 | tf_op jit(solution)/shard_map/rnj,nij->nri/dot_general | solution.py:354
  5.4 2.3 %collective-permute-start = (bf16[64,16,128]{2,1,0:T(8,128)(2,1)S(1)}, bf16[64,16,128]{2,1,0:T(8,128)(2,1)S(1)}, u32[]{:S(2)}, u32[]{:S(2)}) collective-permute-start(bf16[64,16,128]{2,1,0:T(8,128)(2,1)S(1)} %convolution_convert_fusion.refs_0_), channel_id=1, source_target_pairs={{0,8},{1,9},{2,10},{3,11},{4,12},{5,13},{6,14},{7,15},{8,0},{9,1},... | collective-permute-start | bytes 786440 | tf_op jit(solution)/shard_map/ppermute | solution.py:50
  7.7 3.3 %collective-permute-done.3.refs_2_ = bf16[64,16,128]{2,1,0:T(8,128)(2,1)S(1)} collective-permute-done((bf16[64,16,128]{2,1,0:T(8,128)(2,1)S(1)}, bf16[64,16,128]{2,1,0:T(8,128)(2,1)S(1)}, u32[]{:S(2)}, u32[]{:S(2)}) %collective-permute-start.3) | collective-permute-done | bytes 262176 | tf_op jit(solution)/shard_map/ppermute | solution.py:50
  11.0 3.5 %collective-permute-done.1.refs_4_ = bf16[64,16,128]{2,1,0:T(8,128)(2,1)S(1)} collective-permute-done((bf16[64,16,128]{2,1,0:T(8,128)(2,1)S(1)}, bf16[64,16,128]{2,1,0:T(8,128)(2,1)S(1)}, u32[]{:S(2)}, u32[]{:S(2)}) %collective-permute-start.1) | collective-permute-done | bytes 262176 | tf_op jit(solution)/shard_map/ppermute | solution.py:50
  16.0 3.5 %collective-permute-start.21 = (bf16[64,16,128]{2,1,0:T(8,128)(2,1)S(1)}, bf16[64,16,128]{2,1,0:T(8,128)(2,1)S(1)}, u32[]{:S(2)}, u32[]{:S(2)}) collective-permute-start(bf16[64,16,128]{2,1,0:T(8,128)(2,1)S(1)} %convolution_convert_fusion.refs_0_), channel_id=1, source_target_pairs={{0,1},{1,0},{2,3},{3,2},{4,5},{5,4},{6,7},{7,6},{8,9},{9,8},{10,11... | collective-permute-start | bytes 786440 | tf_op jit(solution)/shard_map/ppermute | solution.py:50
  19.5 1.3 collective-permute-start.9
  23.6 2.8 %collective-permute-start.22 = (bf16[64,16,128]{2,1,0:T(8,128)(2,1)S(1)}, bf16[64,16,128]{2,1,0:T(8,128)(2,1)S(1)}, u32[]{:S(2)}, u32[]{:S(2)}) collective-permute-start(bf16[64,16,128]{2,1,0:T(8,128)(2,1)S(1)} %collective-permute-done.3.refs_2_), channel_id=1, source_target_pairs={{0,1},{1,0},{2,3},{3,2},{4,5},{5,4},{6,7},{7,6},{8,9},{9,8},{10,11... | collective-permute-start | bytes 786440 | tf_op jit(solution)/shard_map/ppermute | solution.py:50
  26.3 2.0 collective-permute-done.26.refs_18_.refs_10_
  28.3 2.0 collective-permute-start.25
  30.3 1.8 collective-permute-done.9.refs_12_.refs_4_
  32.1 1.8 collective-permute-start.23
  36.1 5.6 %collective-permute-done.29.refs_22_.refs_14_ = bf16[64,16,128]{2,1,0:T(8,128)(2,1)S(1)} collective-permute-done((bf16[64,16,128]{2,1,0:T(8,128)(2,1)S(1)}, bf16[64,16,128]{2,1,0:T(8,128)(2,1)S(1)}, u32[]{:S(2)}, u32[]{:S(2)}) %collective-permute-start.29) | collective-permute-done | bytes 262176 | tf_op jit(solution)/shard_map/ppermute | solution.py:50
  46.0 4.5 %collective-permute-done.12.refs_14_.refs_6_ = bf16[64,16,128]{2,1,0:T(8,128)(2,1)S(1)} collective-permute-done((bf16[64,16,128]{2,1,0:T(8,128)(2,1)S(1)}, bf16[64,16,128]{2,1,0:T(8,128)(2,1)S(1)}, u32[]{:S(2)}, u32[]{:S(2)}) %collective-permute-start.12) | collective-permute-done | bytes 262176 | tf_op jit(solution)/shard_map/ppermute | solution.py:50
  51.7 4.4 %collective-permute-done.15.refs_26_.refs_10_ = bf16[64,16,128]{2,1,0:T(8,128)(2,1)S(1)} collective-permute-done((bf16[64,16,128]{2,1,0:T(8,128)(2,1)S(1)}, bf16[64,16,128]{2,1,0:T(8,128)(2,1)S(1)}, u32[]{:S(2)}, u32[]{:S(2)}) %collective-permute-start.15) | collective-permute-done | bytes 262176 | tf_op jit(solution)/shard_map/ppermute | solution.py:50
  57.6 1.6 collective-permute-start.20
  60.9 6.0 %level_block.1.refs_0_ = bf16[16,16,128]{2,1,0:T(8,128)(2,1)} custom-call(s32[1,16]{1,0:T(1,128)} %columns.1, bf16[64,16,128]{2,1,0:T(8,128)(2,1)} %copy-done.1, bf16[64,16,128]{2,1,0:T(8,128)(2,1)} %copy-done.10, bf16[64,16,128]{2,1,0:T(8,128)(2,1)} %copy-done.4, bf16[64,16,128]{2,1,0:T(8,128)(2,1)} %copy-done.14, bf16[64,16,128]{2,1,0:T(8,128)(2,1)} %copy-done.6, ...), custom_call_target="tpu_custom_call" | custom-call | flops 1000 | bytes 1000 | tf_op jit(solution)/shard_map/level_block/pallas_call | solution.py:116
  66.9 1.3 collective-permute-start.37
  68.4 4.3 %collective-permute-start.35 = (bf16[16,16,128]{2,1,0:T(8,128)(2,1)}, bf16[16,16,128]{2,1,0:T(8,128)(2,1)S(1)}, u32[]{:S(2)}, u32[]{:S(2)}) collective-permute-start(bf16[16,16,128]{2,1,0:T(8,128)(2,1)} %level_block.1.refs_0_), channel_id=1, source_target_pairs={{0,10},{1,11},{2,8},{3,9},{4,14},{5,15},{6,12},{7,13},{8,2},{9,3},... | collective-permute-start | bytes 196616 | tf_op jit(solution)/shard_map/ppermute | solution.py:143
  72.8 1.7 collective-permute-start.33
  75.1 2.4 %collective-permute-start.31 = (bf16[16,16,128]{2,1,0:T(8,128)(2,1)}, bf16[16,16,128]{2,1,0:T(8,128)(2,1)S(1)}, u32[]{:S(2)}, u32[]{:S(2)}) collective-permute-start(bf16[16,16,128]{2,1,0:T(8,128)(2,1)} %level_block.1.refs_0_), channel_id=1, source_target_pairs={{0,2},{1,3},{2,0},{3,1},{4,6},{5,7},{6,4},{7,5},{8,10},{9,11},{10,... | collective-permute-start | bytes 196616 | tf_op jit(solution)/shard_map/ppermute | solution.py:143
  78.4 1.4 collective-permute-done.34.refs_4_
  81.2 1.9 stack_level.1.refs_16_
  83.2 2.2 %collective-permute-start.38 = (bf16[8,16,16,128]{3,2,1,0:T(8,128)(2,1)}, bf16[8,16,16,128]{3,2,1,0:T(8,128)(2,1)S(1)}, u32[]{:S(2)}, u32[]{:S(2)}) collective-permute-start(bf16[8,16,16,128]{3,2,1,0:T(8,128)(2,1)} %stack_level.1.refs_16_), channel_id=1, source_target_pairs={{0,1},{1,0},{2,3},{3,2},{4,5},{5,4},{6,7},{7,6},{8,9},{9,8},{10,11... | collective-permute-start | bytes 1572872 | tf_op jit(solution)/shard_map/ppermute | solution.py:132
  85.3 1.7 collective-permute-done.38.refs_17_
  87.9 12.4 %leaf_part.3 = bf16[16,8,16,512]{3,2,1,0:T(8,128)(2,1)} custom-call(s32[1,64]{1,0:T(1,128)} %order.3, s32[1,384]{1,0:T(1,128)} %reshape.13.columns, bf16[64,16,128]{2,1,0:T(8,128)(2,1)} %copy-done.1, bf16[64,16,128]{2,1,0:T(8,128)(2,1)} %copy-done.10, bf16[64,16,128]{2,1,0:T(8,128)(2,1)} %copy-done.4, bf16[64,16,128]{2,1,0:T(8,128)(2,1)} %copy-done.14, ...), custom_call_target="tpu_custom_call" | custom-call | flops 1000 | bytes 1000 | tf_op jit(solution)/shard_map/leaf_part/pallas_call | solution.py:265
  100.3 7.0 %all-to-all-start.1 = ((bf16[16,8,16,512]{3,2,1,0:T(8,128)(2,1)}), bf16[16,8,16,512]{3,2,1,0:T(8,128)(2,1)}, u32[]{:S(2)}, u32[]{:S(2)}) async-start(bf16[16,8,16,512]{3,2,1,0:T(8,128)(2,1)} %leaf_part.3), calls=%async_computation.1 | async-start | bytes 4194304 | tf_op jit(solution)/shard_map/all_to_all | solution.py:378
  107.3 12.4 %leaf_part.2 = bf16[16,8,16,512]{3,2,1,0:T(8,128)(2,1)} custom-call(s32[1,64]{1,0:T(1,128)} %order.3, s32[1,384]{1,0:T(1,128)} %reshape.13.columns, bf16[64,16,128]{2,1,0:T(8,128)(2,1)} %copy-done.3, bf16[64,16,128]{2,1,0:T(8,128)(2,1)} %copy-done.20, bf16[64,16,128]{2,1,0:T(8,128)(2,1)} %copy-done.12, bf16[64,16,128]{2,1,0:T(8,128)(2,1)} %copy-done.26, ...), custom_call_target="tpu_custom_call" | custom-call | flops 1000 | bytes 1000 | tf_op jit(solution)/shard_map/leaf_part/pallas_call | solution.py:265
  119.7 35.2 %all-to-all-done.1.arrived = bf16[16,8,16,512]{3,2,1,0:T(8,128)(2,1)} async-done(((bf16[16,8,16,512]{3,2,1,0:T(8,128)(2,1)}), bf16[16,8,16,512]{3,2,1,0:T(8,128)(2,1)}, u32[]{:S(2)}, u32[]{:S(2)}) %all-to-all-start.1) | async-done | bytes 2097184 | tf_op jit(solution)/shard_map/all_to_all | solution.py:378
  154.8 4.9 %all-to-all-start = ((bf16[16,8,16,512]{3,2,1,0:T(8,128)(2,1)}), bf16[16,8,16,512]{3,2,1,0:T(8,128)(2,1)}, u32[]{:S(2)}, u32[]{:S(2)}) async-start(bf16[16,8,16,512]{3,2,1,0:T(8,128)(2,1)} %leaf_part.2), calls=%async_computation | async-start | bytes 4194304 | tf_op jit(solution)/shard_map/all_to_all | solution.py:378
  159.7 2.6 %place_part.2.refs_0_ = bf16[2,8,16,8192]{3,2,1,0:T(8,128)(2,1)} custom-call(bf16[16,8,16,512]{3,2,1,0:T(8,128)(2,1)} %all-to-all-done.1.arrived), custom_call_target="tpu_custom_call" | custom-call | flops 1000 | bytes 1000 | tf_op jit(solution)/shard_map/place_part/pallas_call | solution.py:323
  162.3 44.9 %all-to-all-done.arrived = bf16[16,8,16,512]{3,2,1,0:T(8,128)(2,1)} async-done(((bf16[16,8,16,512]{3,2,1,0:T(8,128)(2,1)}), bf16[16,8,16,512]{3,2,1,0:T(8,128)(2,1)}, u32[]{:S(2)}, u32[]{:S(2)}) %all-to-all-start) | async-done | bytes 2097184 | tf_op jit(solution)/shard_map/all_to_all | solution.py:378
  207.2 2.6 %place_part.3 = bf16[2,8,16,8192]{3,2,1,0:T(8,128)(2,1)} custom-call(bf16[16,8,16,512]{3,2,1,0:T(8,128)(2,1)} %all-to-all-done.arrived, bf16[2,8,16,8192]{3,2,1,0:T(8,128)(2,1)} %place_part.2.refs_0_), custom_call_target="tpu_custom_call", output_to_operand_aliasing={{}: (1, {})} | custom-call | flops 1000 | bytes 1000 | tf_op jit(solution)/shard_map/place_part/pallas_call | solution.py:323
  (139 shorter events, 22.2 us)
Async XLA Ops:
  3.8 7.2 %collective-permute-start.3 = (bf16[64,16,128]{2,1,0:T(8,128)(2,1)S(1)}, bf16[64,16,128]{2,1,0:T(8,128)(2,1)S(1)}, u32[]{:S(2)}, u32[]{:S(2)}) collective-permute-start(bf16[64,16,128]{2,1,0:T(8,128)(2,1)S(1)} %convolution_convert_fusion.refs_0_), channel_id=1, source_target_pairs={{0,2},{1,3},{2,0},{3,1},{4,6},{5,7},{6,4},{7,5},{8,10},{9,11},{10,... | collective-permute-start | bytes 786440 | tf_op jit(solution)/shard_map/ppermute | solution.py:50
  4.0 7.0 %collective-permute-start.2 = (bf16[64,16,128]{2,1,0:T(8,128)(2,1)S(1)}, bf16[64,16,128]{2,1,0:T(8,128)(2,1)S(1)}, u32[]{:S(2)}, u32[]{:S(2)}) collective-permute-start(bf16[64,16,128]{2,1,0:T(8,128)(2,1)S(1)} %convolution_convert_fusion.refs_0_), channel_id=1, source_target_pairs={{0,16},{1,17},{2,18},{3,19},{4,20},{5,21},{6,22},{7,23},{8,24},{9,... | collective-permute-start | bytes 786440 | tf_op jit(solution)/shard_map/ppermute | solution.py:50
  5.2 9.3 %collective-permute-start.1 = (bf16[64,16,128]{2,1,0:T(8,128)(2,1)S(1)}, bf16[64,16,128]{2,1,0:T(8,128)(2,1)S(1)}, u32[]{:S(2)}, u32[]{:S(2)}) collective-permute-start(bf16[64,16,128]{2,1,0:T(8,128)(2,1)S(1)} %convolution_convert_fusion.refs_0_), channel_id=1, source_target_pairs={{0,4},{1,5},{2,6},{3,7},{4,0},{5,1},{6,2},{7,3},{8,12},{9,13},{10,... | collective-permute-start | bytes 786440 | tf_op jit(solution)/shard_map/ppermute | solution.py:50
  5.4 14.1 %collective-permute-start = (bf16[64,16,128]{2,1,0:T(8,128)(2,1)S(1)}, bf16[64,16,128]{2,1,0:T(8,128)(2,1)S(1)}, u32[]{:S(2)}, u32[]{:S(2)}) collective-permute-start(bf16[64,16,128]{2,1,0:T(8,128)(2,1)S(1)} %convolution_convert_fusion.refs_0_), channel_id=1, source_target_pairs={{0,8},{1,9},{2,10},{3,11},{4,12},{5,13},{6,14},{7,15},{8,0},{9,1},... | collective-permute-start | bytes 786440 | tf_op jit(solution)/shard_map/ppermute | solution.py:50
  14.5 6.5 %collective-permute-start.5 = (bf16[64,16,128]{2,1,0:T(8,128)(2,1)S(1)}, bf16[64,16,128]{2,1,0:T(8,128)(2,1)S(1)}, u32[]{:S(2)}, u32[]{:S(2)}) collective-permute-start(bf16[64,16,128]{2,1,0:T(8,128)(2,1)S(1)} %collective-permute-done.1.refs_4_), channel_id=1, source_target_pairs={{0,2},{1,3},{2,0},{3,1},{4,6},{5,7},{6,4},{7,5},{8,10},{9,11},{10,... | collective-permute-start | bytes 786440 | tf_op jit(solution)/shard_map/ppermute | solution.py:50
  15.8 5.5 %collective-permute-start.4 = (bf16[64,16,128]{2,1,0:T(8,128)(2,1)S(1)}, bf16[64,16,128]{2,1,0:T(8,128)(2,1)S(1)}, u32[]{:S(2)}, u32[]{:S(2)}) collective-permute-start(bf16[64,16,128]{2,1,0:T(8,128)(2,1)S(1)} %collective-permute-done.1.refs_4_), channel_id=1, source_target_pairs={{0,16},{1,17},{2,18},{3,19},{4,20},{5,21},{6,22},{7,23},{8,24},{9,... | collective-permute-start | bytes 786440 | tf_op jit(solution)/shard_map/ppermute | solution.py:50
  16.0 7.5 %collective-permute-start.21 = (bf16[64,16,128]{2,1,0:T(8,128)(2,1)S(1)}, bf16[64,16,128]{2,1,0:T(8,128)(2,1)S(1)}, u32[]{:S(2)}, u32[]{:S(2)}) collective-permute-start(bf16[64,16,128]{2,1,0:T(8,128)(2,1)S(1)} %convolution_convert_fusion.refs_0_), channel_id=1, source_target_pairs={{0,1},{1,0},{2,3},{3,2},{4,5},{5,4},{6,7},{7,6},{8,9},{9,8},{10,11... | collective-permute-start | bytes 786440 | tf_op jit(solution)/shard_map/ppermute | solution.py:50
  19.5 12.6 %collective-permute-start.9 = (bf16[64,16,128]{2,1,0:T(8,128)(2,1)S(1)}, bf16[64,16,128]{2,1,0:T(8,128)(2,1)S(1)}, u32[]{:S(2)}, u32[]{:S(2)}) collective-permute-start(bf16[64,16,128]{2,1,0:T(8,128)(2,1)S(1)} %convolution_convert_fusion.refs_0_), channel_id=1, source_target_pairs={{0,12},{1,13},{2,14},{3,15},{4,8},{5,9},{6,10},{7,11},{8,4},{9,5},... | collective-permute-start | bytes 786440 | tf_op jit(solution)/shard_map/ppermute | solution.py:50
  20.8 7.5 %collective-permute-start.26 = (bf16[64,16,128]{2,1,0:T(8,128)(2,1)S(1)}, bf16[64,16,128]{2,1,0:T(8,128)(2,1)S(1)}, u32[]{:S(2)}, u32[]{:S(2)}) collective-permute-start(bf16[64,16,128]{2,1,0:T(8,128)(2,1)S(1)} %collective-permute-done.2.refs_16_.refs_8_), channel_id=1, source_target_pairs={{0,2},{1,3},{2,0},{3,1},{4,6},{5,7},{6,4},{7,5},{8,10},{9,11},{10,... | collective-permute-start | bytes 786440 | tf_op jit(solution)/shard_map/ppermute | solution.py:50
  21.3 12.6 %collective-permute-start.10 = (bf16[64,16,128]{2,1,0:T(8,128)(2,1)S(1)}, bf16[64,16,128]{2,1,0:T(8,128)(2,1)S(1)}, u32[]{:S(2)}, u32[]{:S(2)}) collective-permute-start(bf16[64,16,128]{2,1,0:T(8,128)(2,1)S(1)} %collective-permute-done.refs_8_.refs_0_), channel_id=1, source_target_pairs={{0,16},{1,17},{2,18},{3,19},{4,20},{5,21},{6,22},{7,23},{8,24},{9,... | collective-permute-start | bytes 786440 | tf_op jit(solution)/shard_map/ppermute | solution.py:50
  22.3 12.8 %collective-permute-start.7 = (bf16[64,16,128]{2,1,0:T(8,128)(2,1)S(1)}, bf16[64,16,128]{2,1,0:T(8,128)(2,1)S(1)}, u32[]{:S(2)}, u32[]{:S(2)}) collective-permute-start(bf16[64,16,128]{2,1,0:T(8,128)(2,1)S(1)} %collective-permute-done.refs_8_.refs_0_), channel_id=1, source_target_pairs={{0,2},{1,3},{2,0},{3,1},{4,6},{5,7},{6,4},{7,5},{8,10},{9,11},{10,... | collective-permute-start | bytes 786440 | tf_op jit(solution)/shard_map/ppermute | solution.py:50
  23.6 11.9 %collective-permute-start.22 = (bf16[64,16,128]{2,1,0:T(8,128)(2,1)S(1)}, bf16[64,16,128]{2,1,0:T(8,128)(2,1)S(1)}, u32[]{:S(2)}, u32[]{:S(2)}) collective-permute-start(bf16[64,16,128]{2,1,0:T(8,128)(2,1)S(1)} %collective-permute-done.3.refs_2_), channel_id=1, source_target_pairs={{0,1},{1,0},{2,3},{3,2},{4,5},{5,4},{6,7},{7,6},{8,9},{9,8},{10,11... | collective-permute-start | bytes 786440 | tf_op jit(solution)/shard_map/ppermute | solution.py:50
  28.3 7.3 %collective-permute-start.25 = (bf16[64,16,128]{2,1,0:T(8,128)(2,1)S(1)}, bf16[64,16,128]{2,1,0:T(8,128)(2,1)S(1)}, u32[]{:S(2)}, u32[]{:S(2)}) collective-permute-start(bf16[64,16,128]{2,1,0:T(8,128)(2,1)S(1)} %collective-permute-done.2.refs_16_.refs_8_), channel_id=1, source_target_pairs={{0,1},{1,0},{2,3},{3,2},{4,5},{5,4},{6,7},{7,6},{8,9},{9,8},{10,11... | collective-permute-start | bytes 786440 | tf_op jit(solution)/shard_map/ppermute | solution.py:50
  33.8 7.9 %collective-permute-start.29 = (bf16[64,16,128]{2,1,0:T(8,128)(2,1)S(1)}, bf16[64,16,128]{2,1,0:T(8,128)(2,1)S(1)}, u32[]{:S(2)}, u32[]{:S(2)}) collective-permute-start(bf16[64,16,128]{2,1,0:T(8,128)(2,1)S(1)} %collective-permute-done.5.refs_6_), channel_id=1, source_target_pairs={{0,16},{1,17},{2,18},{3,19},{4,20},{5,21},{6,22},{7,23},{8,24},{9,... | collective-permute-start | bytes 786440 | tf_op jit(solution)/shard_map/ppermute | solution.py:50
  35.1 7.5 %collective-permute-start.27 = (bf16[64,16,128]{2,1,0:T(8,128)(2,1)S(1)}, bf16[64,16,128]{2,1,0:T(8,128)(2,1)S(1)}, u32[]{:S(2)}, u32[]{:S(2)}) collective-permute-start(bf16[64,16,128]{2,1,0:T(8,128)(2,1)S(1)} %collective-permute-done.26.refs_18_.refs_10_), channel_id=1, source_target_pairs={{0,1},{1,0},{2,3},{3,2},{4,5},{5,4},{6,7},{7,6},{8,9},{9,8},{10,11... | collective-permute-start | bytes 786440 | tf_op jit(solution)/shard_map/ppermute | solution.py:50
  35.4 7.4 %collective-permute-start.24 = (bf16[64,16,128]{2,1,0:T(8,128)(2,1)S(1)}, bf16[64,16,128]{2,1,0:T(8,128)(2,1)S(1)}, u32[]{:S(2)}, u32[]{:S(2)}) collective-permute-start(bf16[64,16,128]{2,1,0:T(8,128)(2,1)S(1)} %collective-permute-done.5.refs_6_), channel_id=1, source_target_pairs={{0,1},{1,0},{2,3},{3,2},{4,5},{5,4},{6,7},{7,6},{8,9},{9,8},{10,11... | collective-permute-start | bytes 786440 | tf_op jit(solution)/shard_map/ppermute | solution.py:50
  35.6 8.5 %collective-permute-start.28 = (bf16[64,16,128]{2,1,0:T(8,128)(2,1)S(1)}, bf16[64,16,128]{2,1,0:T(8,128)(2,1)S(1)}, u32[]{:S(2)}, u32[]{:S(2)}) collective-permute-start(bf16[64,16,128]{2,1,0:T(8,128)(2,1)S(1)} %collective-permute-done.4.refs_20_.refs_12_), channel_id=1, source_target_pairs={{0,1},{1,0},{2,3},{3,2},{4,5},{5,4},{6,7},{7,6},{8,9},{9,8},{10,11... | collective-permute-start | bytes 786440 | tf_op jit(solution)/shard_map/ppermute | solution.py:50
  36.0 8.8 %collective-permute-start.6 = (bf16[64,16,128]{2,1,0:T(8,128)(2,1)S(1)}, bf16[64,16,128]{2,1,0:T(8,128)(2,1)S(1)}, u32[]{:S(2)}, u32[]{:S(2)}) collective-permute-start(bf16[64,16,128]{2,1,0:T(8,128)(2,1)S(1)} %collective-permute-done.refs_8_.refs_0_), channel_id=1, source_target_pairs={{0,1},{1,0},{2,3},{3,2},{4,5},{5,4},{6,7},{7,6},{8,9},{9,8},{10,11... | collective-permute-start | bytes 786440 | tf_op jit(solution)/shard_map/ppermute | solution.py:50
  42.6 7.9 %collective-permute-start.12 = (bf16[64,16,128]{2,1,0:T(8,128)(2,1)S(1)}, bf16[64,16,128]{2,1,0:T(8,128)(2,1)S(1)}, u32[]{:S(2)}, u32[]{:S(2)}) collective-permute-start(bf16[64,16,128]{2,1,0:T(8,128)(2,1)S(1)} %collective-permute-done.9.refs_12_.refs_4_), channel_id=1, source_target_pairs={{0,2},{1,3},{2,0},{3,1},{4,6},{5,7},{6,4},{7,5},{8,10},{9,11},{10,... | collective-permute-start | bytes 786440 | tf_op jit(solution)/shard_map/ppermute | solution.py:50
  42.8 13.3 %collective-permute-start.15 = (bf16[64,16,128]{2,1,0:T(8,128)(2,1)S(1)}, bf16[64,16,128]{2,1,0:T(8,128)(2,1)S(1)}, u32[]{:S(2)}, u32[]{:S(2)}) collective-permute-start(bf16[64,16,128]{2,1,0:T(8,128)(2,1)S(1)} %collective-permute-done.10.refs_24_.refs_8_), channel_id=1, source_target_pairs={{0,2},{1,3},{2,0},{3,1},{4,6},{5,7},{6,4},{7,5},{8,10},{9,11},{10,... | collective-permute-start | bytes 786440 | tf_op jit(solution)/shard_map/ppermute | solution.py:50
  44.1 12.9 %collective-permute-start.14 = (bf16[64,16,128]{2,1,0:T(8,128)(2,1)S(1)}, bf16[64,16,128]{2,1,0:T(8,128)(2,1)S(1)}, u32[]{:S(2)}, u32[]{:S(2)}) collective-permute-start(bf16[64,16,128]{2,1,0:T(8,128)(2,1)S(1)} %collective-permute-done.10.refs_24_.refs_8_), channel_id=1, source_target_pairs={{0,1},{1,0},{2,3},{3,2},{4,5},{5,4},{6,7},{7,6},{8,9},{9,8},{10,11... | collective-permute-start | bytes 786440 | tf_op jit(solution)/shard_map/ppermute | solution.py:50
  44.7 12.3 %collective-permute-start.8 = (bf16[64,16,128]{2,1,0:T(8,128)(2,1)S(1)}, bf16[64,16,128]{2,1,0:T(8,128)(2,1)S(1)}, u32[]{:S(2)}, u32[]{:S(2)}) collective-permute-start(bf16[64,16,128]{2,1,0:T(8,128)(2,1)S(1)} %collective-permute-done.7.refs_10_.refs_2_), channel_id=1, source_target_pairs={{0,1},{1,0},{2,3},{3,2},{4,5},{5,4},{6,7},{7,6},{8,9},{9,8},{10,11... | collective-permute-start | bytes 786440 | tf_op jit(solution)/shard_map/ppermute | solution.py:50
  44.8 12.7 %collective-permute-start.17 = (bf16[64,16,128]{2,1,0:T(8,128)(2,1)S(1)}, bf16[64,16,128]{2,1,0:T(8,128)(2,1)S(1)}, u32[]{:S(2)}, u32[]{:S(2)}) collective-permute-start(bf16[64,16,128]{2,1,0:T(8,128)(2,1)S(1)} %collective-permute-done.9.refs_12_.refs_4_), channel_id=1, source_target_pairs={{0,16},{1,17},{2,18},{3,19},{4,20},{5,21},{6,22},{7,23},{8,24},{9,... | collective-permute-start | bytes 786440 | tf_op jit(solution)/shard_map/ppermute | solution.py:50
  50.5 7.1 %collective-permute-start.19 = (bf16[64,16,128]{2,1,0:T(8,128)(2,1)S(1)}, bf16[64,16,128]{2,1,0:T(8,128)(2,1)S(1)}, u32[]{:S(2)}, u32[]{:S(2)}) collective-permute-start(bf16[64,16,128]{2,1,0:T(8,128)(2,1)S(1)} %collective-permute-done.12.refs_14_.refs_6_), channel_id=1, source_target_pairs={{0,16},{1,17},{2,18},{3,19},{4,20},{5,21},{6,22},{7,23},{8,24},{9,... | collective-permute-start | bytes 786440 | tf_op jit(solution)/shard_map/ppermute | solution.py:50
  66.9 7.5 %collective-permute-start.37 = (bf16[16,16,128]{2,1,0:T(8,128)(2,1)}, bf16[16,16,128]{2,1,0:T(8,128)(2,1)S(1)}, u32[]{:S(2)}, u32[]{:S(2)}) collective-permute-start(bf16[16,16,128]{2,1,0:T(8,128)(2,1)} %level_block.1.refs_0_), channel_id=1, source_target_pairs={{0,14},{1,15},{2,12},{3,13},{4,10},{5,11},{6,8},{7,9},{8,6},{9,7},... | collective-permute-start | bytes 196616 | tf_op jit(solution)/shard_map/ppermute | solution.py:143
  68.2 6.9 %collective-permute-start.36 = (bf16[16,16,128]{2,1,0:T(8,128)(2,1)}, bf16[16,16,128]{2,1,0:T(8,128)(2,1)S(1)}, u32[]{:S(2)}, u32[]{:S(2)}) collective-permute-start(bf16[16,16,128]{2,1,0:T(8,128)(2,1)} %level_block.1.refs_0_), channel_id=1, source_target_pairs={{0,12},{1,13},{2,14},{3,15},{4,8},{5,9},{6,10},{7,11},{8,4},{9,5},... | collective-permute-start | bytes 196616 | tf_op jit(solution)/shard_map/ppermute | solution.py:143
  68.4 10.0 %collective-permute-start.35 = (bf16[16,16,128]{2,1,0:T(8,128)(2,1)}, bf16[16,16,128]{2,1,0:T(8,128)(2,1)S(1)}, u32[]{:S(2)}, u32[]{:S(2)}) collective-permute-start(bf16[16,16,128]{2,1,0:T(8,128)(2,1)} %level_block.1.refs_0_), channel_id=1, source_target_pairs={{0,10},{1,11},{2,8},{3,9},{4,14},{5,15},{6,12},{7,13},{8,2},{9,3},... | collective-permute-start | bytes 196616 | tf_op jit(solution)/shard_map/ppermute | solution.py:143
  72.7 7.2 %collective-permute-start.34 = (bf16[16,16,128]{2,1,0:T(8,128)(2,1)}, bf16[16,16,128]{2,1,0:T(8,128)(2,1)S(1)}, u32[]{:S(2)}, u32[]{:S(2)}) collective-permute-start(bf16[16,16,128]{2,1,0:T(8,128)(2,1)} %level_block.1.refs_0_), channel_id=1, source_target_pairs={{0,8},{1,9},{2,10},{3,11},{4,12},{5,13},{6,14},{7,15},{8,0},{9,1},... | collective-permute-start | bytes 196616 | tf_op jit(solution)/shard_map/ppermute | solution.py:143
  72.8 7.1 %collective-permute-start.33 = (bf16[16,16,128]{2,1,0:T(8,128)(2,1)}, bf16[16,16,128]{2,1,0:T(8,128)(2,1)S(1)}, u32[]{:S(2)}, u32[]{:S(2)}) collective-permute-start(bf16[16,16,128]{2,1,0:T(8,128)(2,1)} %level_block.1.refs_0_), channel_id=1, source_target_pairs={{0,6},{1,7},{2,4},{3,5},{4,2},{5,3},{6,0},{7,1},{8,14},{9,15},{10,... | collective-permute-start | bytes 196616 | tf_op jit(solution)/shard_map/ppermute | solution.py:143
  74.4 5.5 %collective-permute-start.32 = (bf16[16,16,128]{2,1,0:T(8,128)(2,1)}, bf16[16,16,128]{2,1,0:T(8,128)(2,1)S(1)}, u32[]{:S(2)}, u32[]{:S(2)}) collective-permute-start(bf16[16,16,128]{2,1,0:T(8,128)(2,1)} %level_block.1.refs_0_), channel_id=1, source_target_pairs={{0,4},{1,5},{2,6},{3,7},{4,0},{5,1},{6,2},{7,3},{8,12},{9,13},{10,... | collective-permute-start | bytes 196616 | tf_op jit(solution)/shard_map/ppermute | solution.py:143
  100.3 54.5 %all-to-all-start.1 = ((bf16[16,8,16,512]{3,2,1,0:T(8,128)(2,1)}), bf16[16,8,16,512]{3,2,1,0:T(8,128)(2,1)}, u32[]{:S(2)}, u32[]{:S(2)}) async-start(bf16[16,8,16,512]{3,2,1,0:T(8,128)(2,1)} %leaf_part.3), calls=%async_computation.1 | async-start | bytes 4194304 | tf_op jit(solution)/shard_map/all_to_all | solution.py:378
  154.8 52.4 %all-to-all-start = ((bf16[16,8,16,512]{3,2,1,0:T(8,128)(2,1)}), bf16[16,8,16,512]{3,2,1,0:T(8,128)(2,1)}, u32[]{:S(2)}, u32[]{:S(2)}) async-start(bf16[16,8,16,512]{3,2,1,0:T(8,128)(2,1)} %leaf_part.2), calls=%async_computation | async-start | bytes 4194304 | tf_op jit(solution)/shard_map/all_to_all | solution.py:378
  (49 other events, 704.3 us)

commit v4 on v3

--- a/solution.py
+++ b/solution.py
@@ -12,6 +12,7 @@
 SMEM = pl.BlockSpec(memory_space=pltpu.SMEM)
 VMEM_LIMIT = 60 * 2**20
 TOGETHER = 2
+PARTS = ((0, 1), (2, 3))
 SMALL = pl.CostEstimate(flops=1000, bytes_accessed=1000, transcendentals=0)
 
 
@@ -74,7 +75,7 @@
     near = flat_permute(piece, dz=1)
     far = flat_permute(piece, dz=2)
     sides = plane(0, piece, True)
-    last = flat_permute(after(piece, far), dz=3)
+    last = flat_permute(after(piece, sides), dz=3)
     sides = plane(1, after(near, sides), False)
     sides = plane(2, after(far, sides), True)
     plane(3, after(last, sides), False)
@@ -109,7 +110,7 @@
 
 
 def level_block(found, rhs, panels, inverse, columns):
-    keys = tuple(sorted(found))
+    keys = tuple(sorted(found, key=lambda key: key[1]))
     pieces = [found[key] for key in keys]
     blocks, rows, width = pieces[0].shape
     vmem = pl.BlockSpec(memory_space=pltpu.VMEM)
@@ -132,33 +133,20 @@
     return lax.ppermute(value, "dev", [(i, i ^ 1) for i in range(16)])
 
 
-def stack_kernel(*refs):
-    for i, ref in enumerate(refs[:-1]):
-        refs[-1][i] = ref[...]
-
-
 def gather_level(block):
-    found = [block]
+    mine = [block]
     for k in range(2, 16, 2):
-        found.append(lax.ppermute(block, "dev", [(i, i ^ k) for i in range(16)]))
-    vmem = pl.BlockSpec(memory_space=pltpu.VMEM)
-    mine = pl.pallas_call(
-        stack_kernel,
-        out_shape=jax.ShapeDtypeStruct((8,) + block.shape, block.dtype),
-        in_specs=[vmem] * 8,
-        out_specs=vmem,
-        cost_estimate=SMALL,
-        name="stack_level",
-    )(*found)
-    return mine, swap_cores(mine)
-
-
-def leaf_kernel(part_index, keys, order, columns, *refs):
+        mine.append(lax.ppermute(block, "dev", [(i, i ^ k) for i in range(16)]))
+    return mine + [swap_cores(value) for value in mine]
+
+
+def leaf_kernel(part, keys, order, columns, *refs):
     count = len(keys)
     pieces = refs[:count]
-    level, sibling, rhs_hbm, inverse_hbm, panels_hbm = refs[count : count + 5]
+    level = refs[count : count + 16]
+    rhs_hbm, inverse_hbm, panels_hbm = refs[count + 16 : count + 19]
     out, source, rhs, inverse, panels, solved, sems, tile_sems, out_sems = refs[
-        count + 5 :
+        count + 19 :
     ]
     steps = out.shape[0]
     me_dev = lax.axis_index("dev")
@@ -169,13 +157,19 @@
         return order[0, step * 4 + q]
 
     groups, _, rows, width = source.shape
-    half = (me_dev // groups) ^ part_index
-    mine = pl.ds(half * groups, groups)
-    pairs = piece_pairs(keys, pieces, source, groups)
-    for i in range(level.shape[0]):
-        owner = first + (chip ^ i) * 2
-        pairs.append((level.at[i, mine], source.at[:, owner + core]))
-        pairs.append((sibling.at[i, mine], source.at[:, owner + 1 - core]))
+    z = me_dev // 4
+    pairs = []
+    for (dx, dz, dy, dc), piece in zip(keys, pieces):
+        group = 4 * part.index(dz) + (me_dev ^ (2 * dy + dc)) % 4
+        blocks = piece.shape[0]
+        begin = (lax.axis_index("sub") ^ dx) * blocks
+        pairs.append((piece, source.at[group, pl.ds(begin, blocks)]))
+    for place, dz in enumerate(part):
+        spot, mine = pl.ds(4 * place, 4), pl.ds((z ^ dz) * 4, 4)
+        for i in range(8):
+            owner = first + (chip ^ i) * 2
+            pairs.append((level[i].at[mine], source.at[spot, owner + core]))
+            pairs.append((level[8 + i].at[mine], source.at[spot, owner + 1 - core]))
 
     def panel_copy(step, q):
         spot = step * 4 + q
@@ -193,8 +187,13 @@
         for q in range(4):
             panel_copy(step, q).start()
     shared = [
-        pltpu.make_async_copy(rhs_hbm.at[half], rhs, sems.at[len(pairs)]),
-        pltpu.make_async_copy(inverse_hbm, inverse, sems.at[len(pairs) + 1]),
+        pltpu.make_async_copy(inverse_hbm, inverse, sems.at[len(pairs)]),
+    ]
+    shared += [
+        pltpu.make_async_copy(
+            rhs_hbm.at[z ^ dz], rhs.at[pl.ds(4 * i, 4)], sems.at[len(pairs) + 1 + i]
+        )
+        for i, dz in enumerate(part)
     ]
     for copy in shared:
         copy.start()
@@ -227,21 +226,21 @@
 
         for step, q in spots:
             panel_copy(step, q).wait()
-        parts = []
+        sums = []
         for step, q in spots:
             tile = tile_at(step, q)
-            parts.append(
+            sums.append(
                 pick_product(
                     source,
-                    [columns[0, tile * depth + k] for k in range(depth)],
+                    [columns[k, tile] for k in range(depth)],
                     [panels[step * 4 + q, k] for k in range(depth)],
                 )
             )
-        for i, ((step, q), part) in enumerate(zip(spots, parts)):
+        for i, ((step, q), total) in enumerate(zip(spots, sums)):
             tile = tile_at(step, q)
             lanes = pl.ds(pl.multiple_of(tile * width, width), width)
-            own = rhs[:, :, lanes].reshape(part.shape)
-            done = solve_block(own, part, inverse[tile])
+            own = rhs[:, :, lanes].reshape(total.shape)
+            done = solve_block(own, total, inverse[tile])
             solved[slot, i // 4, :, :, q * width : (q + 1) * width] = done.reshape(
                 groups, rows, width
             )
@@ -254,20 +253,20 @@
 
 
 def leaf_part(
-    part_index, found, level, rhs, panels, inverse, order, columns
+    part, found, level, rhs, panels, inverse, order, columns
 ):
-    keys = tuple(sorted(key for key in found if key[1] // 2 == part_index))
+    keys = tuple(sorted(key for key in found if key[1] in part))
     pieces = [found[key] for key in keys]
     blocks, rows, width = pieces[0].shape
-    groups = 8
+    groups = 4 * len(part)
     tiles, depth = panels.shape[:2]
     level_blocks = 16
     return pl.pallas_call(
-        functools.partial(leaf_kernel, part_index, keys),
+        functools.partial(leaf_kernel, part, keys),
         out_shape=jax.ShapeDtypeStruct(
             (level_blocks, groups, rows, 4 * width), jnp.bfloat16
         ),
-        in_specs=[SMEM] * 2 + [ANY] * (len(keys) + 5),
+        in_specs=[SMEM] * 2 + [ANY] * (len(keys) + 19),
         out_specs=ANY,
         scratch_shapes=[
             pltpu.VMEM((groups, 2 * blocks + level_blocks, rows, width), jnp.bfloat16),
@@ -275,7 +274,7 @@
             pltpu.VMEM((tiles, width, width), jnp.bfloat16),
             pltpu.VMEM((tiles, depth, width, width), jnp.bfloat16),
             pltpu.VMEM((2, TOGETHER, groups, rows, 4 * width), jnp.bfloat16),
-            pltpu.SemaphoreType.DMA((len(keys) + level_blocks + 2,)),
+            pltpu.SemaphoreType.DMA((len(keys) + len(part) * (level_blocks + 1) + 1,)),
             pltpu.SemaphoreType.DMA((tiles,)),
             pltpu.SemaphoreType.DMA((2,)),
         ],
@@ -287,13 +286,13 @@
         columns,
         *pieces,
         *level,
-        rhs.reshape(2, groups, rows, tiles * width),
+        rhs.reshape(4, 4, rows, tiles * width),
         inverse,
         panels,
     )
 
 
-def place_kernel(part_index, arrived, *refs):
+def place_kernel(part, arrived, *refs):
     out, held, in_sems, out_sems = refs[-4:]
     count, groups, _, span = arrived.shape
     inward = [
@@ -302,33 +301,33 @@
     ]
     for copy in inward:
         copy.start()
-    outward = [
-        pltpu.make_async_copy(
-            held.at[k],
-            out.at[(k // groups) ^ part_index, :, :, pl.ds(k * span, span)],
-            out_sems.at[k],
-        )
-        for k in range(count)
-    ]
+    outward = []
     for k in range(count):
         inward[k].wait()
-        outward[k].start()
+        for i, dz in enumerate(part):
+            copy = pltpu.make_async_copy(
+                held.at[k, pl.ds(4 * i, 4)],
+                out.at[(k // 4) ^ dz, :, :, pl.ds(k * span, span)],
+                out_sems.at[len(part) * k + i],
+            )
+            copy.start()
+            outward.append(copy)
     for copy in outward:
         copy.wait()
 
 
-def place_part(part_index, arrived, before):
+def place_part(part, arrived, before):
     count, groups, rows, span = arrived.shape
     extra = [] if before is None else [before]
     return pl.pallas_call(
-        functools.partial(place_kernel, part_index),
-        out_shape=jax.ShapeDtypeStruct((2, groups, rows, count * span), jnp.bfloat16),
+        functools.partial(place_kernel, part),
+        out_shape=jax.ShapeDtypeStruct((4, 4, rows, count * span), jnp.bfloat16),
         in_specs=[ANY] * (1 + len(extra)),
         out_specs=ANY,
         scratch_shapes=[
             pltpu.VMEM((count, groups, rows, span), jnp.bfloat16),
             pltpu.SemaphoreType.DMA((count,)),
-            pltpu.SemaphoreType.DMA((count,)),
+            pltpu.SemaphoreType.DMA((count * len(part),)),
         ],
         input_output_aliases={} if before is None else {1: 0},
         compiler_params=pltpu.CompilerParams(vmem_limit_bytes=VMEM_LIMIT),
@@ -357,14 +356,14 @@
         root_inverse,
         preferred_element_type=jnp.float32,
     ).astype(jnp.bfloat16)
-    leaf_columns = leaf_columns.reshape(1, -1)
-    found = gather_root(after(piece, leaf_columns))
+    leaf_columns = leaf_columns.T
+    found = gather_root(piece)
     block = level_block(found, level_rhs, level_panels, level_inverse, level_columns)
     level = gather_level(block)
 
-    def leaf_of(part_index):
+    def leaf_of(part):
         return leaf_part(
-            part_index,
+            part,
             found,
             level,
             leaf_rhs,
@@ -378,8 +377,8 @@
         return lax.all_to_all(value, "dev", split_axis=0, concat_axis=0, tiled=True)
 
     out = None
-    for part_index in range(2):
-        out = place_part(part_index, exchange(leaf_of(part_index)), out)
+    for part in PARTS:
+        out = place_part(part, exchange(leaf_of(part)), out)
     return out.reshape(leaf_rhs.shape)
 
 

time: 210 us -> 208 us (level)
    ppermute x7, waiting for transfers between devices: 2.78 us -> 0.02 us  [gather_level(): mine.append(lax.ppermute(block, 'dev', [(i, i ^ k) for i in range(16)]))]
    ppermute x1 -> x8, starting transfers between devices: 2.17 us -> 4.89 us  [swap_cores(): return lax.ppermute(value, 'dev', [(i, i ^ 1) for i in range(16)])]
    pallas_call x5 -> x4, Pallas kernels: 31.8 us -> 30.4 us  [the longest x2 25 us: leaf_part(): pl.pallas_call(functools.partial(leaf_kernel, part, keys), out_shape=jax....]
  transfers between devices with their start and end apart: 41 -> 48, of which waited for: 15 -> 12; matrix products, arithmetic and copies ran while one was open for 0% -> 0% of each run, Pallas kernels for 7% -> 7%
where the time goes in v4:
time: 208 us
  waiting for transfers between devices  108 us (52%)
  starting transfers between devices  56.8 us (27%)
  Pallas kernels  36.4 us (18%)
  local copies, waits for them, and re-layouts  3.65 us (2%)
  matrix products  2.12 us (1%)
    all_to_all x2, waiting for transfers between devices, exchange(): return lax.all_to_all(value, 'dev', split_axis=0, concat_axis=0, tiled=True)  79.9 us
    ppermute x31, starting transfers between devices, flat_permute(): lax.ppermute(value, ('sub', 'dev'), [(i, i ^ step) for i in range(32)])  28.1 us
    ppermute x31, waiting for transfers between devices, flat_permute(): lax.ppermute(value, ('sub', 'dev'), [(i, i ^ step) for i in range(32)])  27.3 us
    pallas_call x2, Pallas kernels, leaf_part(): pl.pallas_call(functools.partial(leaf_kernel, part, keys), out_shape=jax....  25 us
    all_to_all x2, starting transfers between devices, exchange(): return lax.all_to_all(value, 'dev', split_axis=0, concat_axis=0, tiled=True)  12.2 us
    ppermute x7, starting transfers between devices, gather_level(): mine.append(lax.ppermute(block, 'dev', [(i, i ^ k) for i in range(16)]))  11.7 us
    pallas_call x1, Pallas kernels, level_block(): pl.pallas_call(functools.partial(level_kernel, keys), out_shape=jax.Shape...  6.01 us
    pallas_call x2, Pallas kernels, place_part(): pl.pallas_call(functools.partial(place_kernel, part), out_shape=jax.Shape...  5.4 us
  transfers between devices with their start and end apart: 48, of which 12 were waited for; matrix products, arithmetic and copies ran while one was open for 0% of the time, Pallas kernels for 7%

profile of v4, /device:TPU:13, one launch (start us, length us, event | category | flops | bytes accessed | tf_op | source)
XLA Modules:
  0.0 207.5 jit_solution(17223635074055668626)
XLA Ops:
  0.0 1.6 copy-done
  1.6 2.1 %convolution_convert_fusion.refs_0_ = bf16[64,16,128]{2,1,0:T(8,128)(2,1)S(1)} fusion(bf16[64,128,128]{2,1,0:T(8,128)(2,1)S(1)} %copy-done, bf16[16,8192]{1,0:T(8,128)(2,1)} %param.11), kind=kOutput, calls=%fused_computation | convolution fusion | flops 33685504 | bytes 2621440 | tf_op jit(solution)/shard_map/rnj,nij->nri/dot_general | solution.py:353
  5.4 2.3 %collective-permute-start = (bf16[64,16,128]{2,1,0:T(8,128)(2,1)S(1)}, bf16[64,16,128]{2,1,0:T(8,128)(2,1)S(1)}, u32[]{:S(2)}, u32[]{:S(2)}) collective-permute-start(bf16[64,16,128]{2,1,0:T(8,128)(2,1)S(1)} %convolution_convert_fusion.refs_0_), channel_id=1, source_target_pairs={{0,8},{1,9},{2,10},{3,11},{4,12},{5,13},{6,14},{7,15},{8,0},{9,1},... | collective-permute-start | bytes 786440 | tf_op jit(solution)/shard_map/ppermute | solution.py:51
  7.7 3.3 %collective-permute-done.3.refs_2_ = bf16[64,16,128]{2,1,0:T(8,128)(2,1)S(1)} collective-permute-done((bf16[64,16,128]{2,1,0:T(8,128)(2,1)S(1)}, bf16[64,16,128]{2,1,0:T(8,128)(2,1)S(1)}, u32[]{:S(2)}, u32[]{:S(2)}) %collective-permute-start.3) | collective-permute-done | bytes 262176 | tf_op jit(solution)/shard_map/ppermute | solution.py:51
  10.9 3.5 %collective-permute-done.1.refs_8_.refs_4_ = bf16[64,16,128]{2,1,0:T(8,128)(2,1)S(1)} collective-permute-done((bf16[64,16,128]{2,1,0:T(8,128)(2,1)S(1)}, bf16[64,16,128]{2,1,0:T(8,128)(2,1)S(1)}, u32[]{:S(2)}, u32[]{:S(2)}) %collective-permute-start.1) | collective-permute-done | bytes 262176 | tf_op jit(solution)/shard_map/ppermute | solution.py:51
  14.5 1.2 collective-permute-start.5
  16.0 3.5 %collective-permute-start.22 = (bf16[64,16,128]{2,1,0:T(8,128)(2,1)S(1)}, bf16[64,16,128]{2,1,0:T(8,128)(2,1)S(1)}, u32[]{:S(2)}, u32[]{:S(2)}) collective-permute-start(bf16[64,16,128]{2,1,0:T(8,128)(2,1)S(1)} %convolution_convert_fusion.refs_0_), channel_id=1, source_target_pairs={{0,1},{1,0},{2,3},{3,2},{4,5},{5,4},{6,7},{7,6},{8,9},{9,8},{10,11... | collective-permute-start | bytes 786440 | tf_op jit(solution)/shard_map/ppermute | solution.py:51
  19.4 1.3 collective-permute-start.9
  22.3 1.2 collective-permute-start.7
  23.5 2.8 %collective-permute-start.24 = (bf16[64,16,128]{2,1,0:T(8,128)(2,1)S(1)}, bf16[64,16,128]{2,1,0:T(8,128)(2,1)S(1)}, u32[]{:S(2)}, u32[]{:S(2)}) collective-permute-start(bf16[64,16,128]{2,1,0:T(8,128)(2,1)S(1)} %collective-permute-done.3.refs_2_), channel_id=1, source_target_pairs={{0,1},{1,0},{2,3},{3,2},{4,5},{5,4},{6,7},{7,6},{8,9},{9,8},{10,11... | collective-permute-start | bytes 786440 | tf_op jit(solution)/shard_map/ppermute | solution.py:51
  26.3 6.7 %collective-permute-done.9.refs_24_.refs_4_ = bf16[64,16,128]{2,1,0:T(8,128)(2,1)S(1)} collective-permute-done((bf16[64,16,128]{2,1,0:T(8,128)(2,1)S(1)}, bf16[64,16,128]{2,1,0:T(8,128)(2,1)S(1)}, u32[]{:S(2)}, u32[]{:S(2)}) %collective-permute-start.9) | collective-permute-done | bytes 262176 | tf_op jit(solution)/shard_map/ppermute | solution.py:51
  36.4 4.9 %collective-permute-done.26.refs_11_.refs_14_ = bf16[64,16,128]{2,1,0:T(8,128)(2,1)S(1)} collective-permute-done((bf16[64,16,128]{2,1,0:T(8,128)(2,1)S(1)}, bf16[64,16,128]{2,1,0:T(8,128)(2,1)S(1)}, u32[]{:S(2)}, u32[]{:S(2)}) %collective-permute-start.26) | collective-permute-done | bytes 262176 | tf_op jit(solution)/shard_map/ppermute | solution.py:51
  41.3 1.3 collective-permute-start.30
  42.7 1.4 collective-permute-start.15
  46.3 4.2 %collective-permute-done.12.refs_26_.refs_6_ = bf16[64,16,128]{2,1,0:T(8,128)(2,1)S(1)} collective-permute-done((bf16[64,16,128]{2,1,0:T(8,128)(2,1)S(1)}, bf16[64,16,128]{2,1,0:T(8,128)(2,1)S(1)}, u32[]{:S(2)}, u32[]{:S(2)}) %collective-permute-start.12) | collective-permute-done | bytes 262176 | tf_op jit(solution)/shard_map/ppermute | solution.py:51
  51.7 4.4 %collective-permute-done.15.refs_19_.refs_10_ = bf16[64,16,128]{2,1,0:T(8,128)(2,1)S(1)} collective-permute-done((bf16[64,16,128]{2,1,0:T(8,128)(2,1)S(1)}, bf16[64,16,128]{2,1,0:T(8,128)(2,1)S(1)}, u32[]{:S(2)}, u32[]{:S(2)}) %collective-permute-start.15) | collective-permute-done | bytes 262176 | tf_op jit(solution)/shard_map/ppermute | solution.py:51
  57.7 1.6 collective-permute-start.20
  60.9 6.0 %level_block.1.refs_16_ = bf16[16,16,128]{2,1,0:T(8,128)(2,1)} custom-call(s32[1,16]{1,0:T(1,128)} %columns.1, bf16[64,16,128]{2,1,0:T(8,128)(2,1)} %copy-done.1, bf16[64,16,128]{2,1,0:T(8,128)(2,1)} %copy-done.4, bf16[64,16,128]{2,1,0:T(8,128)(2,1)} %copy-done.3, bf16[64,16,128]{2,1,0:T(8,128)(2,1)} %copy-done.12, bf16[64,16,128]{2,1,0:T(8,128)(2,1)} %copy-done.9, ...), custom_call_target="tpu_custom_call" | custom-call | flops 1000 | bytes 1000 | tf_op jit(solution)/shard_map/level_block/pallas_call | solution.py:117
  67.2 1.2 collective-permute-start.37
  68.5 4.1 %collective-permute-start.35 = (bf16[16,16,128]{2,1,0:T(8,128)(2,1)}, bf16[16,16,128]{2,1,0:T(8,128)(2,1)S(1)}, u32[]{:S(2)}, u32[]{:S(2)}) collective-permute-start(bf16[16,16,128]{2,1,0:T(8,128)(2,1)} %level_block.1.refs_16_), channel_id=1, source_target_pairs={{0,10},{1,11},{2,8},{3,9},{4,14},{5,15},{6,12},{7,13},{8,2},{9,3},... | collective-permute-start | bytes 196616 | tf_op jit(solution)/shard_map/ppermute | solution.py:139
  74.0 1.3 collective-permute-start.32
  75.3 3.6 %collective-permute-start.31 = (bf16[16,16,128]{2,1,0:T(8,128)(2,1)}, bf16[16,16,128]{2,1,0:T(8,128)(2,1)S(1)}, u32[]{:S(2)}, u32[]{:S(2)}) collective-permute-start(bf16[16,16,128]{2,1,0:T(8,128)(2,1)} %level_block.1.refs_16_), channel_id=1, source_target_pairs={{0,2},{1,3},{2,0},{3,1},{4,6},{5,7},{6,4},{7,5},{8,10},{9,11},{10,... | collective-permute-start | bytes 196616 | tf_op jit(solution)/shard_map/ppermute | solution.py:139
  78.9 1.4 collective-permute-start.45
  81.5 1.6 collective-permute-start.41
  85.1 12.5 %leaf_part.3 = bf16[16,8,16,512]{3,2,1,0:T(8,128)(2,1)} custom-call(s32[1,64]{1,0:T(1,128)} %order.3, s32[6,64]{1,0:T(8,128)} %bitcast.13, bf16[64,16,128]{2,1,0:T(8,128)(2,1)} %copy-done.1, bf16[64,16,128]{2,1,0:T(8,128)(2,1)} %copy-done.9, bf16[64,16,128]{2,1,0:T(8,128)(2,1)} %copy-done.3, bf16[64,16,128]{2,1,0:T(8,128)(2,1)} %copy-done.13, ...), custom_call_target="tpu_custom_call" | custom-call | flops 1000 | bytes 1000 | tf_op jit(solution)/shard_map/leaf_part/pallas_call | solution.py:264
  97.6 7.2 %all-to-all-start.1 = ((bf16[16,8,16,512]{3,2,1,0:T(8,128)(2,1)}), bf16[16,8,16,512]{3,2,1,0:T(8,128)(2,1)}, u32[]{:S(2)}, u32[]{:S(2)}) async-start(bf16[16,8,16,512]{3,2,1,0:T(8,128)(2,1)} %leaf_part.3), calls=%async_computation.1 | async-start | bytes 4194304 | tf_op jit(solution)/shard_map/all_to_all | solution.py:377
  104.8 12.5 %leaf_part.2 = bf16[16,8,16,512]{3,2,1,0:T(8,128)(2,1)} custom-call(s32[1,64]{1,0:T(1,128)} %order.3, s32[6,64]{1,0:T(8,128)} %bitcast.14, bf16[64,16,128]{2,1,0:T(8,128)(2,1)} %copy-done.2, bf16[64,16,128]{2,1,0:T(8,128)(2,1)} %copy-done.19, bf16[64,16,128]{2,1,0:T(8,128)(2,1)} %copy-done.11, bf16[64,16,128]{2,1,0:T(8,128)(2,1)} %copy-done.28, ...), custom_call_target="tpu_custom_call" | custom-call | flops 1000 | bytes 1000 | tf_op jit(solution)/shard_map/leaf_part/pallas_call | solution.py:264
  117.3 35.0 %all-to-all-done.1.arrived = bf16[16,8,16,512]{3,2,1,0:T(8,128)(2,1)} async-done(((bf16[16,8,16,512]{3,2,1,0:T(8,128)(2,1)}), bf16[16,8,16,512]{3,2,1,0:T(8,128)(2,1)}, u32[]{:S(2)}, u32[]{:S(2)}) %all-to-all-start.1) | async-done | bytes 2097184 | tf_op jit(solution)/shard_map/all_to_all | solution.py:377
  152.4 4.9 %all-to-all-start = ((bf16[16,8,16,512]{3,2,1,0:T(8,128)(2,1)}), bf16[16,8,16,512]{3,2,1,0:T(8,128)(2,1)}, u32[]{:S(2)}, u32[]{:S(2)}) async-start(bf16[16,8,16,512]{3,2,1,0:T(8,128)(2,1)} %leaf_part.2), calls=%async_computation | async-start | bytes 4194304 | tf_op jit(solution)/shard_map/all_to_all | solution.py:377
  157.3 2.7 %place_part.2.refs_0_ = bf16[4,4,16,8192]{3,2,1,0:T(8,128)(2,1)} custom-call(bf16[16,8,16,512]{3,2,1,0:T(8,128)(2,1)} %all-to-all-done.1.arrived), custom_call_target="tpu_custom_call" | custom-call | flops 1000 | bytes 1000 | tf_op jit(solution)/shard_map/place_part/pallas_call | solution.py:322
  160.0 44.8 %all-to-all-done.arrived = bf16[16,8,16,512]{3,2,1,0:T(8,128)(2,1)} async-done(((bf16[16,8,16,512]{3,2,1,0:T(8,128)(2,1)}), bf16[16,8,16,512]{3,2,1,0:T(8,128)(2,1)}, u32[]{:S(2)}, u32[]{:S(2)}) %all-to-all-start) | async-done | bytes 2097184 | tf_op jit(solution)/shard_map/all_to_all | solution.py:377
  204.8 2.7 %place_part.3 = bf16[4,4,16,8192]{3,2,1,0:T(8,128)(2,1)} custom-call(bf16[16,8,16,512]{3,2,1,0:T(8,128)(2,1)} %all-to-all-done.arrived, bf16[4,4,16,8192]{3,2,1,0:T(8,128)(2,1)} %place_part.2.refs_0_), custom_call_target="tpu_custom_call", output_to_operand_aliasing={{}: (1, {})} | custom-call | flops 1000 | bytes 1000 | tf_op jit(solution)/shard_map/place_part/pallas_call | solution.py:322
  (164 shorter events, 18.2 us)
Async XLA Ops:
  3.7 7.2 %collective-permute-start.3 = (bf16[64,16,128]{2,1,0:T(8,128)(2,1)S(1)}, bf16[64,16,128]{2,1,0:T(8,128)(2,1)S(1)}, u32[]{:S(2)}, u32[]{:S(2)}) collective-permute-start(bf16[64,16,128]{2,1,0:T(8,128)(2,1)S(1)} %convolution_convert_fusion.refs_0_), channel_id=1, source_target_pairs={{0,2},{1,3},{2,0},{3,1},{4,6},{5,7},{6,4},{7,5},{8,10},{9,11},{10,... | collective-permute-start | bytes 786440 | tf_op jit(solution)/shard_map/ppermute | solution.py:51
  4.0 7.0 %collective-permute-start.2 = (bf16[64,16,128]{2,1,0:T(8,128)(2,1)S(1)}, bf16[64,16,128]{2,1,0:T(8,128)(2,1)S(1)}, u32[]{:S(2)}, u32[]{:S(2)}) collective-permute-start(bf16[64,16,128]{2,1,0:T(8,128)(2,1)S(1)} %convolution_convert_fusion.refs_0_), channel_id=1, source_target_pairs={{0,16},{1,17},{2,18},{3,19},{4,20},{5,21},{6,22},{7,23},{8,24},{9,... | collective-permute-start | bytes 786440 | tf_op jit(solution)/shard_map/ppermute | solution.py:51
  5.2 9.3 %collective-permute-start.1 = (bf16[64,16,128]{2,1,0:T(8,128)(2,1)S(1)}, bf16[64,16,128]{2,1,0:T(8,128)(2,1)S(1)}, u32[]{:S(2)}, u32[]{:S(2)}) collective-permute-start(bf16[64,16,128]{2,1,0:T(8,128)(2,1)S(1)} %convolution_convert_fusion.refs_0_), channel_id=1, source_target_pairs={{0,4},{1,5},{2,6},{3,7},{4,0},{5,1},{6,2},{7,3},{8,12},{9,13},{10,... | collective-permute-start | bytes 786440 | tf_op jit(solution)/shard_map/ppermute | solution.py:51
  5.4 15.4 %collective-permute-start = (bf16[64,16,128]{2,1,0:T(8,128)(2,1)S(1)}, bf16[64,16,128]{2,1,0:T(8,128)(2,1)S(1)}, u32[]{:S(2)}, u32[]{:S(2)}) collective-permute-start(bf16[64,16,128]{2,1,0:T(8,128)(2,1)S(1)} %convolution_convert_fusion.refs_0_), channel_id=1, source_target_pairs={{0,8},{1,9},{2,10},{3,11},{4,12},{5,13},{6,14},{7,15},{8,0},{9,1},... | collective-permute-start | bytes 786440 | tf_op jit(solution)/shard_map/ppermute | solution.py:51
  14.5 6.5 %collective-permute-start.5 = (bf16[64,16,128]{2,1,0:T(8,128)(2,1)S(1)}, bf16[64,16,128]{2,1,0:T(8,128)(2,1)S(1)}, u32[]{:S(2)}, u32[]{:S(2)}) collective-permute-start(bf16[64,16,128]{2,1,0:T(8,128)(2,1)S(1)} %collective-permute-done.1.refs_8_.refs_4_), channel_id=1, source_target_pairs={{0,2},{1,3},{2,0},{3,1},{4,6},{5,7},{6,4},{7,5},{8,10},{9,11},{10,... | collective-permute-start | bytes 786440 | tf_op jit(solution)/shard_map/ppermute | solution.py:51
  16.0 7.5 %collective-permute-start.22 = (bf16[64,16,128]{2,1,0:T(8,128)(2,1)S(1)}, bf16[64,16,128]{2,1,0:T(8,128)(2,1)S(1)}, u32[]{:S(2)}, u32[]{:S(2)}) collective-permute-start(bf16[64,16,128]{2,1,0:T(8,128)(2,1)S(1)} %convolution_convert_fusion.refs_0_), channel_id=1, source_target_pairs={{0,1},{1,0},{2,3},{3,2},{4,5},{5,4},{6,7},{7,6},{8,9},{9,8},{10,11... | collective-permute-start | bytes 786440 | tf_op jit(solution)/shard_map/ppermute | solution.py:51
  19.4 13.6 %collective-permute-start.9 = (bf16[64,16,128]{2,1,0:T(8,128)(2,1)S(1)}, bf16[64,16,128]{2,1,0:T(8,128)(2,1)S(1)}, u32[]{:S(2)}, u32[]{:S(2)}) collective-permute-start(bf16[64,16,128]{2,1,0:T(8,128)(2,1)S(1)} %convolution_convert_fusion.refs_0_), channel_id=1, source_target_pairs={{0,12},{1,13},{2,14},{3,15},{4,8},{5,9},{6,10},{7,11},{8,4},{9,5},... | collective-permute-start | bytes 786440 | tf_op jit(solution)/shard_map/ppermute | solution.py:51
  20.8 13.0 %collective-permute-start.21 = (bf16[64,16,128]{2,1,0:T(8,128)(2,1)S(1)}, bf16[64,16,128]{2,1,0:T(8,128)(2,1)S(1)}, u32[]{:S(2)}, u32[]{:S(2)}) collective-permute-start(bf16[64,16,128]{2,1,0:T(8,128)(2,1)S(1)} %collective-permute-done.2.refs_1_.refs_8_), channel_id=1, source_target_pairs={{0,2},{1,3},{2,0},{3,1},{4,6},{5,7},{6,4},{7,5},{8,10},{9,11},{10,... | collective-permute-start | bytes 786440 | tf_op jit(solution)/shard_map/ppermute | solution.py:51
  21.2 12.6 %collective-permute-start.10 = (bf16[64,16,128]{2,1,0:T(8,128)(2,1)S(1)}, bf16[64,16,128]{2,1,0:T(8,128)(2,1)S(1)}, u32[]{:S(2)}, u32[]{:S(2)}) collective-permute-start(bf16[64,16,128]{2,1,0:T(8,128)(2,1)S(1)} %collective-permute-done.refs_16_.refs_0_), channel_id=1, source_target_pairs={{0,16},{1,17},{2,18},{3,19},{4,20},{5,21},{6,22},{7,23},{8,24},{9,... | collective-permute-start | bytes 786440 | tf_op jit(solution)/shard_map/ppermute | solution.py:51
  22.3 12.8 %collective-permute-start.7 = (bf16[64,16,128]{2,1,0:T(8,128)(2,1)S(1)}, bf16[64,16,128]{2,1,0:T(8,128)(2,1)S(1)}, u32[]{:S(2)}, u32[]{:S(2)}) collective-permute-start(bf16[64,16,128]{2,1,0:T(8,128)(2,1)S(1)} %collective-permute-done.refs_16_.refs_0_), channel_id=1, source_target_pairs={{0,2},{1,3},{2,0},{3,1},{4,6},{5,7},{6,4},{7,5},{8,10},{9,11},{10,... | collective-permute-start | bytes 786440 | tf_op jit(solution)/shard_map/ppermute | solution.py:51
  23.5 12.3 %collective-permute-start.24 = (bf16[64,16,128]{2,1,0:T(8,128)(2,1)S(1)}, bf16[64,16,128]{2,1,0:T(8,128)(2,1)S(1)}, u32[]{:S(2)}, u32[]{:S(2)}) collective-permute-start(bf16[64,16,128]{2,1,0:T(8,128)(2,1)S(1)} %collective-permute-done.3.refs_2_), channel_id=1, source_target_pairs={{0,1},{1,0},{2,3},{3,2},{4,5},{5,4},{6,7},{7,6},{8,9},{9,8},{10,11... | collective-permute-start | bytes 786440 | tf_op jit(solution)/shard_map/ppermute | solution.py:51
  33.9 7.5 %collective-permute-start.26 = (bf16[64,16,128]{2,1,0:T(8,128)(2,1)S(1)}, bf16[64,16,128]{2,1,0:T(8,128)(2,1)S(1)}, u32[]{:S(2)}, u32[]{:S(2)}) collective-permute-start(bf16[64,16,128]{2,1,0:T(8,128)(2,1)S(1)} %collective-permute-done.5.refs_10_.refs_6_), channel_id=1, source_target_pairs={{0,16},{1,17},{2,18},{3,19},{4,20},{5,21},{6,22},{7,23},{8,24},{9,... | collective-permute-start | bytes 786440 | tf_op jit(solution)/shard_map/ppermute | solution.py:51
  35.1 7.5 %collective-permute-start.25 = (bf16[64,16,128]{2,1,0:T(8,128)(2,1)S(1)}, bf16[64,16,128]{2,1,0:T(8,128)(2,1)S(1)}, u32[]{:S(2)}, u32[]{:S(2)}) collective-permute-start(bf16[64,16,128]{2,1,0:T(8,128)(2,1)S(1)} %collective-permute-done.21.refs_3_.refs_10_), channel_id=1, source_target_pairs={{0,1},{1,0},{2,3},{3,2},{4,5},{5,4},{6,7},{7,6},{8,9},{9,8},{10,11... | collective-permute-start | bytes 786440 | tf_op jit(solution)/shard_map/ppermute | solution.py:51
  35.8 6.9 %collective-permute-start.29 = (bf16[64,16,128]{2,1,0:T(8,128)(2,1)S(1)}, bf16[64,16,128]{2,1,0:T(8,128)(2,1)S(1)}, u32[]{:S(2)}, u32[]{:S(2)}) collective-permute-start(bf16[64,16,128]{2,1,0:T(8,128)(2,1)S(1)} %collective-permute-done.5.refs_10_.refs_6_), channel_id=1, source_target_pairs={{0,1},{1,0},{2,3},{3,2},{4,5},{5,4},{6,7},{7,6},{8,9},{9,8},{10,11... | collective-permute-start | bytes 786440 | tf_op jit(solution)/shard_map/ppermute | solution.py:51
  35.9 8.2 %collective-permute-start.28 = (bf16[64,16,128]{2,1,0:T(8,128)(2,1)S(1)}, bf16[64,16,128]{2,1,0:T(8,128)(2,1)S(1)}, u32[]{:S(2)}, u32[]{:S(2)}) collective-permute-start(bf16[64,16,128]{2,1,0:T(8,128)(2,1)S(1)} %collective-permute-done.4.refs_9_.refs_12_), channel_id=1, source_target_pairs={{0,1},{1,0},{2,3},{3,2},{4,5},{5,4},{6,7},{7,6},{8,9},{9,8},{10,11... | collective-permute-start | bytes 786440 | tf_op jit(solution)/shard_map/ppermute | solution.py:51
  36.3 8.4 %collective-permute-start.6 = (bf16[64,16,128]{2,1,0:T(8,128)(2,1)S(1)}, bf16[64,16,128]{2,1,0:T(8,128)(2,1)S(1)}, u32[]{:S(2)}, u32[]{:S(2)}) collective-permute-start(bf16[64,16,128]{2,1,0:T(8,128)(2,1)S(1)} %collective-permute-done.refs_16_.refs_0_), channel_id=1, source_target_pairs={{0,1},{1,0},{2,3},{3,2},{4,5},{5,4},{6,7},{7,6},{8,9},{9,8},{10,11... | collective-permute-start | bytes 786440 | tf_op jit(solution)/shard_map/ppermute | solution.py:51
  42.6 7.9 %collective-permute-start.12 = (bf16[64,16,128]{2,1,0:T(8,128)(2,1)S(1)}, bf16[64,16,128]{2,1,0:T(8,128)(2,1)S(1)}, u32[]{:S(2)}, u32[]{:S(2)}) collective-permute-start(bf16[64,16,128]{2,1,0:T(8,128)(2,1)S(1)} %collective-permute-done.9.refs_24_.refs_4_), channel_id=1, source_target_pairs={{0,2},{1,3},{2,0},{3,1},{4,6},{5,7},{6,4},{7,5},{8,10},{9,11},{10,... | collective-permute-start | bytes 786440 | tf_op jit(solution)/shard_map/ppermute | solution.py:51
  42.7 13.4 %collective-permute-start.15 = (bf16[64,16,128]{2,1,0:T(8,128)(2,1)S(1)}, bf16[64,16,128]{2,1,0:T(8,128)(2,1)S(1)}, u32[]{:S(2)}, u32[]{:S(2)}) collective-permute-start(bf16[64,16,128]{2,1,0:T(8,128)(2,1)S(1)} %collective-permute-done.10.refs_17_.refs_8_), channel_id=1, source_target_pairs={{0,2},{1,3},{2,0},{3,1},{4,6},{5,7},{6,4},{7,5},{8,10},{9,11},{10,... | collective-permute-start | bytes 786440 | tf_op jit(solution)/shard_map/ppermute | solution.py:51
  44.1 12.9 %collective-permute-start.14 = (bf16[64,16,128]{2,1,0:T(8,128)(2,1)S(1)}, bf16[64,16,128]{2,1,0:T(8,128)(2,1)S(1)}, u32[]{:S(2)}, u32[]{:S(2)}) collective-permute-start(bf16[64,16,128]{2,1,0:T(8,128)(2,1)S(1)} %collective-permute-done.10.refs_17_.refs_8_), channel_id=1, source_target_pairs={{0,1},{1,0},{2,3},{3,2},{4,5},{5,4},{6,7},{7,6},{8,9},{9,8},{10,11... | collective-permute-start | bytes 786440 | tf_op jit(solution)/shard_map/ppermute | solution.py:51
  44.7 12.3 %collective-permute-start.17 = (bf16[64,16,128]{2,1,0:T(8,128)(2,1)S(1)}, bf16[64,16,128]{2,1,0:T(8,128)(2,1)S(1)}, u32[]{:S(2)}, u32[]{:S(2)}) collective-permute-start(bf16[64,16,128]{2,1,0:T(8,128)(2,1)S(1)} %collective-permute-done.9.refs_24_.refs_4_), channel_id=1, source_target_pairs={{0,16},{1,17},{2,18},{3,19},{4,20},{5,21},{6,22},{7,23},{8,24},{9,... | collective-permute-start | bytes 786440 | tf_op jit(solution)/shard_map/ppermute | solution.py:51
  46.0 11.5 %collective-permute-start.11 = (bf16[64,16,128]{2,1,0:T(8,128)(2,1)S(1)}, bf16[64,16,128]{2,1,0:T(8,128)(2,1)S(1)}, u32[]{:S(2)}, u32[]{:S(2)}) collective-permute-start(bf16[64,16,128]{2,1,0:T(8,128)(2,1)S(1)} %collective-permute-done.9.refs_24_.refs_4_), channel_id=1, source_target_pairs={{0,1},{1,0},{2,3},{3,2},{4,5},{5,4},{6,7},{7,6},{8,9},{9,8},{10,11... | collective-permute-start | bytes 786440 | tf_op jit(solution)/shard_map/ppermute | solution.py:51
  50.5 7.2 %collective-permute-start.19 = (bf16[64,16,128]{2,1,0:T(8,128)(2,1)S(1)}, bf16[64,16,128]{2,1,0:T(8,128)(2,1)S(1)}, u32[]{:S(2)}, u32[]{:S(2)}) collective-permute-start(bf16[64,16,128]{2,1,0:T(8,128)(2,1)S(1)} %collective-permute-done.12.refs_26_.refs_6_), channel_id=1, source_target_pairs={{0,16},{1,17},{2,18},{3,19},{4,20},{5,21},{6,22},{7,23},{8,24},{9,... | collective-permute-start | bytes 786440 | tf_op jit(solution)/shard_map/ppermute | solution.py:51
  66.9 5.9 %collective-permute-start.38 = (bf16[16,16,128]{2,1,0:T(8,128)(2,1)}, bf16[16,16,128]{2,1,0:T(8,128)(2,1)S(1)}, u32[]{:S(2)}, u32[]{:S(2)}) collective-permute-start(bf16[16,16,128]{2,1,0:T(8,128)(2,1)} %level_block.1.refs_16_), channel_id=1, source_target_pairs={{0,1},{1,0},{2,3},{3,2},{4,5},{5,4},{6,7},{7,6},{8,9},{9,8},{10,11... | collective-permute-start | bytes 196616 | tf_op jit(solution)/shard_map/ppermute | solution.py:133
  67.2 6.8 %collective-permute-start.37 = (bf16[16,16,128]{2,1,0:T(8,128)(2,1)}, bf16[16,16,128]{2,1,0:T(8,128)(2,1)S(1)}, u32[]{:S(2)}, u32[]{:S(2)}) collective-permute-start(bf16[16,16,128]{2,1,0:T(8,128)(2,1)} %level_block.1.refs_16_), channel_id=1, source_target_pairs={{0,14},{1,15},{2,12},{3,13},{4,10},{5,11},{6,8},{7,9},{8,6},{9,7},... | collective-permute-start | bytes 196616 | tf_op jit(solution)/shard_map/ppermute | solution.py:139
  68.4 6.8 %collective-permute-start.36 = (bf16[16,16,128]{2,1,0:T(8,128)(2,1)}, bf16[16,16,128]{2,1,0:T(8,128)(2,1)S(1)}, u32[]{:S(2)}, u32[]{:S(2)}) collective-permute-start(bf16[16,16,128]{2,1,0:T(8,128)(2,1)} %level_block.1.refs_16_), channel_id=1, source_target_pairs={{0,12},{1,13},{2,14},{3,15},{4,8},{5,9},{6,10},{7,11},{8,4},{9,5},... | collective-permute-start | bytes 196616 | tf_op jit(solution)/shard_map/ppermute | solution.py:139
  68.5 10.4 %collective-permute-start.35 = (bf16[16,16,128]{2,1,0:T(8,128)(2,1)}, bf16[16,16,128]{2,1,0:T(8,128)(2,1)S(1)}, u32[]{:S(2)}, u32[]{:S(2)}) collective-permute-start(bf16[16,16,128]{2,1,0:T(8,128)(2,1)} %level_block.1.refs_16_), channel_id=1, source_target_pairs={{0,10},{1,11},{2,8},{3,9},{4,14},{5,15},{6,12},{7,13},{8,2},{9,3},... | collective-permute-start | bytes 196616 | tf_op jit(solution)/shard_map/ppermute | solution.py:139
  72.6 7.8 %collective-permute-start.34 = (bf16[16,16,128]{2,1,0:T(8,128)(2,1)}, bf16[16,16,128]{2,1,0:T(8,128)(2,1)S(1)}, u32[]{:S(2)}, u32[]{:S(2)}) collective-permute-start(bf16[16,16,128]{2,1,0:T(8,128)(2,1)} %level_block.1.refs_16_), channel_id=1, source_target_pairs={{0,8},{1,9},{2,10},{3,11},{4,12},{5,13},{6,14},{7,15},{8,0},{9,1},... | collective-permute-start | bytes 196616 | tf_op jit(solution)/shard_map/ppermute | solution.py:139
  72.8 8.1 %collective-permute-start.33 = (bf16[16,16,128]{2,1,0:T(8,128)(2,1)}, bf16[16,16,128]{2,1,0:T(8,128)(2,1)S(1)}, u32[]{:S(2)}, u32[]{:S(2)}) collective-permute-start(bf16[16,16,128]{2,1,0:T(8,128)(2,1)} %level_block.1.refs_16_), channel_id=1, source_target_pairs={{0,6},{1,7},{2,4},{3,5},{4,2},{5,3},{6,0},{7,1},{8,14},{9,15},{10,... | collective-permute-start | bytes 196616 | tf_op jit(solution)/shard_map/ppermute | solution.py:139
  74.0 7.0 %collective-permute-start.32 = (bf16[16,16,128]{2,1,0:T(8,128)(2,1)}, bf16[16,16,128]{2,1,0:T(8,128)(2,1)S(1)}, u32[]{:S(2)}, u32[]{:S(2)}) collective-permute-start(bf16[16,16,128]{2,1,0:T(8,128)(2,1)} %level_block.1.refs_16_), channel_id=1, source_target_pairs={{0,4},{1,5},{2,6},{3,7},{4,0},{5,1},{6,2},{7,3},{8,12},{9,13},{10,... | collective-permute-start | bytes 196616 | tf_op jit(solution)/shard_map/ppermute | solution.py:139
  75.3 6.2 %collective-permute-start.31 = (bf16[16,16,128]{2,1,0:T(8,128)(2,1)}, bf16[16,16,128]{2,1,0:T(8,128)(2,1)S(1)}, u32[]{:S(2)}, u32[]{:S(2)}) collective-permute-start(bf16[16,16,128]{2,1,0:T(8,128)(2,1)} %level_block.1.refs_16_), channel_id=1, source_target_pairs={{0,2},{1,3},{2,0},{3,1},{4,6},{5,7},{6,4},{7,5},{8,10},{9,11},{10,... | collective-permute-start | bytes 196616 | tf_op jit(solution)/shard_map/ppermute | solution.py:139
  97.6 54.8 %all-to-all-start.1 = ((bf16[16,8,16,512]{3,2,1,0:T(8,128)(2,1)}), bf16[16,8,16,512]{3,2,1,0:T(8,128)(2,1)}, u32[]{:S(2)}, u32[]{:S(2)}) async-start(bf16[16,8,16,512]{3,2,1,0:T(8,128)(2,1)} %leaf_part.3), calls=%async_computation.1 | async-start | bytes 4194304 | tf_op jit(solution)/shard_map/all_to_all | solution.py:377
  152.4 52.4 %all-to-all-start = ((bf16[16,8,16,512]{3,2,1,0:T(8,128)(2,1)}), bf16[16,8,16,512]{3,2,1,0:T(8,128)(2,1)}, u32[]{:S(2)}, u32[]{:S(2)}) async-start(bf16[16,8,16,512]{3,2,1,0:T(8,128)(2,1)} %leaf_part.2), calls=%async_computation | async-start | bytes 4194304 | tf_op jit(solution)/shard_map/all_to_all | solution.py:377
  (63 other events, 748.3 us)

commit v5 on v4

--- a/solution.py
+++ b/solution.py
@@ -336,6 +336,57 @@
     )(arrived, *extra)
 
 
+def place_each_kernel(part, *refs):
+    count = 16
+    arrived = refs[:count]
+    out, held, in_sems, out_sems = refs[-4:]
+    span = held.shape[4]
+    me_dev = lax.axis_index("dev")
+    inward = [
+        pltpu.make_async_copy(arrived[k], held.at[k], in_sems.at[k])
+        for k in range(count)
+    ]
+    for copy in inward:
+        copy.start()
+    outward = []
+    for k in range(count):
+        inward[k].wait()
+        owner = me_dev ^ k
+        columns = pl.ds(pl.multiple_of(owner * span, span), span)
+        for i, dz in enumerate(part):
+            copy = pltpu.make_async_copy(
+                held.at[k, 0, pl.ds(4 * i, 4)],
+                out.at[(owner // 4) ^ dz, :, :, columns],
+                out_sems.at[len(part) * k + i],
+            )
+            copy.start()
+            outward.append(copy)
+    for copy in outward:
+        copy.wait()
+
+
+def place_each(part, arrived, before):
+    count = len(arrived)
+    return pl.pallas_call(
+        functools.partial(place_each_kernel, part),
+        out_shape=jax.ShapeDtypeStruct(before.shape, jnp.bfloat16),
+        in_specs=[ANY] * (count + 1),
+        out_specs=ANY,
+        scratch_shapes=[
+            pltpu.VMEM((count,) + arrived[0].shape, jnp.bfloat16),
+            pltpu.SemaphoreType.DMA((count,)),
+            pltpu.SemaphoreType.DMA((count * len(part),)),
+        ],
+        input_output_aliases={count: 0},
+        compiler_params=pltpu.CompilerParams(vmem_limit_bytes=VMEM_LIMIT),
+        cost_estimate=SMALL,
+        name="place_each",
+    )(*arrived, before)
+
+
+SEND_ORDER = (12, 3, 13, 4, 14, 2, 15, 5, 8, 1, 9, 6, 10, 7, 11)
+
+
 def on_device_pairs(
     root_rhs,
     root_inverse,
@@ -376,9 +427,14 @@
     def exchange(value):
         return lax.all_to_all(value, "dev", split_axis=0, concat_axis=0, tiled=True)
 
-    out = None
-    for part in PARTS:
-        out = place_part(part, exchange(leaf_of(part)), out)
+    out = place_part(PARTS[0], exchange(leaf_of(PARTS[0])), None)
+    solved = leaf_of(PARTS[1])
+    me_dev = lax.axis_index("dev")
+    arrived = [lax.dynamic_slice_in_dim(solved, me_dev, 1)] + [None] * 15
+    for k in SEND_ORDER:
+        value = lax.dynamic_slice_in_dim(solved, me_dev ^ k, 1)
+        arrived[k] = lax.ppermute(value, "dev", [(i, i ^ k) for i in range(16)])
+    out = place_each(PARTS[1], arrived, out)
     return out.reshape(leaf_rhs.shape)
 
 

time: 208 us -> 201 us (0.966)
  waiting for transfers between devices: 108 us -> 79.7 us
  starting transfers between devices: 56.8 us -> 74.4 us
  local copies, waits for them, and re-layouts: 3.65 us -> 6.35 us
    all_to_all x2 -> x1, waiting for transfers between devices: 79.9 us -> 0.01 us  [exchange(): return lax.all_to_all(value, 'dev', split_axis=0, concat_axis=0, tiled=True)]
    ppermute x0 -> x15, waiting for transfers between devices: none -> 50.3 us  [on_device_pairs(): arrived[k] = lax.ppermute(value, 'dev', [(i, i ^ k) for i in range(16)])]
    ppermute x0 -> x15, starting transfers between devices: none -> 25.3 us  [on_device_pairs(): arrived[k] = lax.ppermute(value, 'dev', [(i, i ^ k) for i in range(16)])]
    all_to_all x2 -> x1, starting transfers between devices: 12.2 us -> 4.79 us  [exchange(): return lax.all_to_all(value, 'dev', split_axis=0, concat_axis=0, tiled=True)]
    ppermute x7, starting transfers between devices: 11.7 us -> 7.46 us  [gather_level(): mine.append(lax.ppermute(block, 'dev', [(i, i ^ k) for i in range(16)]))]
    ppermute x7, waiting for transfers between devices: 0.02 us -> 3.03 us  [gather_level(): mine.append(lax.ppermute(block, 'dev', [(i, i ^ k) for i in range(16)]))]
    ppermute x8, starting transfers between devices: 4.89 us -> 7.9 us  [swap_cores(): return lax.ppermute(value, 'dev', [(i, i ^ 1) for i in range(16)])]
    pallas_call x0 -> x1, Pallas kernels: none -> 2.7 us  [place_each(): pl.pallas_call(functools.partial(place_each_kernel, part), out_shape=jax....]
  transfers between devices with their start and end apart: 48 -> 62, of which waited for: 12 -> 30; matrix products, arithmetic and copies ran while one was open for 0% -> 1% of each run, Pallas kernels for 7% -> 8%
where the time goes in v5:
time: 201 us; the launch traced here: 199 us
  waiting for transfers between devices  79.7 us (40%)
  starting transfers between devices  74.4 us (37%)
  Pallas kernels  36.3 us (18%)
  local copies, waits for them, and re-layouts  6.35 us (3%)
  matrix products  2.12 us (1%)
    ppermute x15, waiting for transfers between devices, on_device_pairs(): arrived[k] = lax.ppermute(value, 'dev', [(i, i ^ k) for i in range(16)])  50.3 us
    ppermute x31, starting transfers between devices, flat_permute(): lax.ppermute(value, ('sub', 'dev'), [(i, i ^ step) for i in range(32)])  28.9 us
    ppermute x15, starting transfers between devices, on_device_pairs(): arrived[k] = lax.ppermute(value, 'dev', [(i, i ^ k) for i in range(16)])  25.3 us
    ppermute x31, waiting for transfers between devices, flat_permute(): lax.ppermute(value, ('sub', 'dev'), [(i, i ^ step) for i in range(32)])  25.2 us
    pallas_call x2, Pallas kernels, leaf_part(): pl.pallas_call(functools.partial(leaf_kernel, part, keys), out_shape=jax....  24.9 us
    ppermute x8, starting transfers between devices, swap_cores(): return lax.ppermute(value, 'dev', [(i, i ^ 1) for i in range(16)])  7.9 us
    ppermute x7, starting transfers between devices, gather_level(): mine.append(lax.ppermute(block, 'dev', [(i, i ^ k) for i in range(16)]))  7.46 us
    pallas_call x1, Pallas kernels, level_block(): pl.pallas_call(functools.partial(level_kernel, keys), out_shape=jax.Shape...  6.01 us
  transfers between devices with their start and end apart: 62, of which 30 were waited for; matrix products, arithmetic and copies ran while one was open for 1% of the time, Pallas kernels for 8%

profile of v5, /device:TPU:13, one launch (start us, length us, event | category | flops | bytes accessed | tf_op | source)
XLA Modules:
  0.0 199.3 jit_solution(14285293485670591282)
XLA Ops:
  1.6 2.1 %convolution_convert_fusion.refs_0_ = bf16[64,16,128]{2,1,0:T(8,128)(2,1)S(1)} fusion(bf16[64,128,128]{2,1,0:T(8,128)(2,1)S(1)} %copy-done, bf16[16,8192]{1,0:T(8,128)(2,1)} %param.11), kind=kOutput, calls=%fused_computation | convolution fusion | flops 33685504 | bytes 2621440 | tf_op jit(solution)/shard_map/rnj,nij->nri/dot_general | solution.py:404
  5.4 2.3 %collective-permute-start = (bf16[64,16,128]{2,1,0:T(8,128)(2,1)S(1)}, bf16[64,16,128]{2,1,0:T(8,128)(2,1)S(1)}, u32[]{:S(2)}, u32[]{:S(2)}) collective-permute-start(bf16[64,16,128]{2,1,0:T(8,128)(2,1)S(1)} %convolution_convert_fusion.refs_0_), channel_id=1, source_target_pairs={{0,8},{1,9},{2,10},{3,11},{4,12},{5,13},{6,14},{7,15},{8,0},{9,1},... | collective-permute-start | bytes 786440 | tf_op jit(solution)/shard_map/ppermute | solution.py:51
  7.7 3.3 %collective-permute-done.2.refs_1_.refs_8_ = bf16[64,16,128]{2,1,0:T(8,128)(2,1)S(1)} collective-permute-done((bf16[64,16,128]{2,1,0:T(8,128)(2,1)S(1)}, bf16[64,16,128]{2,1,0:T(8,128)(2,1)S(1)}, u32[]{:S(2)}, u32[]{:S(2)}) %collective-permute-start.2) | collective-permute-done | bytes 262176 | tf_op jit(solution)/shard_map/ppermute | solution.py:51
  11.8 2.6 %collective-permute-done.1.refs_8_.refs_4_ = bf16[64,16,128]{2,1,0:T(8,128)(2,1)S(1)} collective-permute-done((bf16[64,16,128]{2,1,0:T(8,128)(2,1)S(1)}, bf16[64,16,128]{2,1,0:T(8,128)(2,1)S(1)}, u32[]{:S(2)}, u32[]{:S(2)}) %collective-permute-start.1) | collective-permute-done | bytes 262176 | tf_op jit(solution)/shard_map/ppermute | solution.py:51
  16.0 3.5 %collective-permute-start.22 = (bf16[64,16,128]{2,1,0:T(8,128)(2,1)S(1)}, bf16[64,16,128]{2,1,0:T(8,128)(2,1)S(1)}, u32[]{:S(2)}, u32[]{:S(2)}) collective-permute-start(bf16[64,16,128]{2,1,0:T(8,128)(2,1)S(1)} %convolution_convert_fusion.refs_0_), channel_id=1, source_target_pairs={{0,1},{1,0},{2,3},{3,2},{4,5},{5,4},{6,7},{7,6},{8,9},{9,8},{10,11... | collective-permute-start | bytes 786440 | tf_op jit(solution)/shard_map/ppermute | solution.py:51
  23.6 8.2 %collective-permute-done.9.refs_24_.refs_4_ = bf16[64,16,128]{2,1,0:T(8,128)(2,1)S(1)} collective-permute-done((bf16[64,16,128]{2,1,0:T(8,128)(2,1)S(1)}, bf16[64,16,128]{2,1,0:T(8,128)(2,1)S(1)}, u32[]{:S(2)}, u32[]{:S(2)}) %collective-permute-start.9) | collective-permute-done | bytes 262176 | tf_op jit(solution)/shard_map/ppermute | solution.py:51
  31.8 2.1 %collective-permute-start.23 = (bf16[64,16,128]{2,1,0:T(8,128)(2,1)S(1)}, bf16[64,16,128]{2,1,0:T(8,128)(2,1)S(1)}, u32[]{:S(2)}, u32[]{:S(2)}) collective-permute-start(bf16[64,16,128]{2,1,0:T(8,128)(2,1)S(1)} %collective-permute-done.2.refs_1_.refs_8_), channel_id=1, source_target_pairs={{0,1},{1,0},{2,3},{3,2},{4,5},{5,4},{6,7},{7,6},{8,9},{9,8},{10,11... | collective-permute-start | bytes 786440 | tf_op jit(solution)/shard_map/ppermute | solution.py:51
  37.3 5.0 %collective-permute-done.26.refs_11_.refs_14_ = bf16[64,16,128]{2,1,0:T(8,128)(2,1)S(1)} collective-permute-done((bf16[64,16,128]{2,1,0:T(8,128)(2,1)S(1)}, bf16[64,16,128]{2,1,0:T(8,128)(2,1)S(1)}, u32[]{:S(2)}, u32[]{:S(2)}) %collective-permute-start.26) | collective-permute-done | bytes 262176 | tf_op jit(solution)/shard_map/ppermute | solution.py:51
  45.8 3.4 %collective-permute-done.17.refs_25_.refs_12_ = bf16[64,16,128]{2,1,0:T(8,128)(2,1)S(1)} collective-permute-done((bf16[64,16,128]{2,1,0:T(8,128)(2,1)S(1)}, bf16[64,16,128]{2,1,0:T(8,128)(2,1)S(1)}, u32[]{:S(2)}, u32[]{:S(2)}) %collective-permute-start.17) | collective-permute-done | bytes 262176 | tf_op jit(solution)/shard_map/ppermute | solution.py:51
  50.5 2.0 %collective-permute-start.30 = (bf16[64,16,128]{2,1,0:T(8,128)(2,1)S(1)}, bf16[64,16,128]{2,1,0:T(8,128)(2,1)S(1)}, u32[]{:S(2)}, u32[]{:S(2)}) collective-permute-start(bf16[64,16,128]{2,1,0:T(8,128)(2,1)S(1)} %collective-permute-done.26.refs_11_.refs_14_), channel_id=1, source_target_pairs={{0,1},{1,0},{2,3},{3,2},{4,5},{5,4},{6,7},{7,6},{8,9},{9,8},{10,11... | collective-permute-start | bytes 786440 | tf_op jit(solution)/shard_map/ppermute | solution.py:51
  55.3 2.7 %collective-permute-start.20 = (bf16[64,16,128]{2,1,0:T(8,128)(2,1)S(1)}, bf16[64,16,128]{2,1,0:T(8,128)(2,1)}, u32[]{:S(2)}, u32[]{:S(2)}) collective-permute-start(bf16[64,16,128]{2,1,0:T(8,128)(2,1)S(1)} %collective-permute-done.19.refs_27_.refs_14_), channel_id=1, source_target_pairs={{0,1},{1,0},{2,3},{3,2},{4,5},{5,4},{6,7},{7,6},{8,9},{9,8},{10,11... | collective-permute-start | bytes 786440 | tf_op jit(solution)/shard_map/ppermute | solution.py:51
  59.6 6.0 %level_block.1.refs_16_ = bf16[16,16,128]{2,1,0:T(8,128)(2,1)} custom-call(s32[1,16]{1,0:T(1,128)} %columns.1, bf16[64,16,128]{2,1,0:T(8,128)(2,1)} %copy-done.1, bf16[64,16,128]{2,1,0:T(8,128)(2,1)} %copy-done.14, bf16[64,16,128]{2,1,0:T(8,128)(2,1)} %copy-done.15, bf16[64,16,128]{2,1,0:T(8,128)(2,1)} %copy-done.24, bf16[64,16,128]{2,1,0:T(8,128)(2,1)} %copy-done.22, ...), custom_call_target="tpu_custom_call" | custom-call | flops 1000 | bytes 1000 | tf_op jit(solution)/shard_map/level_block/pallas_call | solution.py:117
  66.1 2.2 %collective-permute-start.33 = (bf16[16,16,128]{2,1,0:T(8,128)(2,1)}, bf16[16,16,128]{2,1,0:T(8,128)(2,1)S(1)}, u32[]{:S(2)}, u32[]{:S(2)}) collective-permute-start(bf16[16,16,128]{2,1,0:T(8,128)(2,1)} %level_block.1.refs_16_), channel_id=1, source_target_pairs={{0,6},{1,7},{2,4},{3,5},{4,2},{5,3},{6,0},{7,1},{8,14},{9,15},{10,... | collective-permute-start | bytes 196616 | tf_op jit(solution)/shard_map/ppermute | solution.py:139
  73.1 2.0 %collective-permute-start.38 = (bf16[16,16,128]{2,1,0:T(8,128)(2,1)}, bf16[16,16,128]{2,1,0:T(8,128)(2,1)S(1)}, u32[]{:S(2)}, u32[]{:S(2)}) collective-permute-start(bf16[16,16,128]{2,1,0:T(8,128)(2,1)} %level_block.1.refs_16_), channel_id=1, source_target_pairs={{0,1},{1,0},{2,3},{3,2},{4,5},{5,4},{6,7},{7,6},{8,9},{9,8},{10,11... | collective-permute-start | bytes 196616 | tf_op jit(solution)/shard_map/ppermute | solution.py:133
  77.6 2.0 %collective-permute-start.40 = (bf16[16,16,128]{2,1,0:T(8,128)(2,1)S(1)}, bf16[16,16,128]{2,1,0:T(8,128)(2,1)S(1)}, u32[]{:S(2)}, u32[]{:S(2)}) collective-permute-start(bf16[16,16,128]{2,1,0:T(8,128)(2,1)S(1)} %collective-permute-done.32.refs_18_), channel_id=1, source_target_pairs={{0,1},{1,0},{2,3},{3,2},{4,5},{5,4},{6,7},{7,6},{8,9},{9,8},{10,11... | collective-permute-start | bytes 196616 | tf_op jit(solution)/shard_map/ppermute | solution.py:133
  85.8 12.5 %leaf_part.3 = bf16[16,8,16,512]{3,2,1,0:T(8,128)(2,1)} custom-call(s32[1,64]{1,0:T(1,128)} %order.3, s32[6,64]{1,0:T(8,128)} %bitcast.13, bf16[64,16,128]{2,1,0:T(8,128)(2,1)} %copy-done.1, bf16[64,16,128]{2,1,0:T(8,128)(2,1)} %copy-done.22, bf16[64,16,128]{2,1,0:T(8,128)(2,1)} %copy-done.15, bf16[64,16,128]{2,1,0:T(8,128)(2,1)} %copy-done.26, ...), custom_call_target="tpu_custom_call" | custom-call | flops 1000 | bytes 1000 | tf_op jit(solution)/shard_map/leaf_part/pallas_call | solution.py:264
  98.3 4.8 %all-to-all-start = ((bf16[16,8,16,512]{3,2,1,0:T(8,128)(2,1)}), bf16[16,8,16,512]{3,2,1,0:T(8,128)(2,1)}, u32[]{:S(2)}, u32[]{:S(2)}) async-start(bf16[16,8,16,512]{3,2,1,0:T(8,128)(2,1)} %leaf_part.3), calls=%async_computation | async-start | bytes 4194304 | tf_op jit(solution)/shard_map/all_to_all | solution.py:428
  103.1 12.5 %leaf_part.2 = bf16[16,8,16,512]{3,2,1,0:T(8,128)(2,1)} custom-call(s32[1,64]{1,0:T(1,128)} %order.3, s32[6,64]{1,0:T(8,128)} %bitcast.14, bf16[64,16,128]{2,1,0:T(8,128)(2,1)} %copy-done.2, bf16[64,16,128]{2,1,0:T(8,128)(2,1)} %copy-done.6, bf16[64,16,128]{2,1,0:T(8,128)(2,1)} %copy-done.5, bf16[64,16,128]{2,1,0:T(8,128)(2,1)} %copy-done.12, ...), custom_call_target="tpu_custom_call" | custom-call | flops 1000 | bytes 1000 | tf_op jit(solution)/shard_map/leaf_part/pallas_call | solution.py:264
  115.6 2.6 %constant_dynamic-slice_fusion = (bf16[1,8,16,512]{3,2,1,0:T(8,128)(2,1)}, bf16[1,8,16,512]{3,2,1,0:T(8,128)(2,1)}, bf16[1,8,16,512]{3,2,1,0:T(8,128)(2,1)}, bf1...) fusion(bf16[16,8,16,512]{3,2,1,0:T(8,128)(2,1)} %leaf_part.2, ...), kind=kLoop, calls=%fused_computation.3 | loop fusion | bytes 4194368 | tf_op jit(solution)/shard_map/dynamic_slice | solution.py:435
  122.3 2.2 %collective-permute-done.47.refs_2_ = bf16[1,8,16,512]{3,2,1,0:T(8,128)(2,1)S(1)} collective-permute-done((bf16[1,8,16,512]{3,2,1,0:T(8,128)(2,1)S(1)}, bf16[1,8,16,512]{3,2,1,0:T(8,128)(2,1)S(1)}, u32[]{:S(2)}, u32[]{:S(2)}) %collective-permute-start.47) | collective-permute-done | bytes 131104 | tf_op jit(solution)/shard_map/ppermute | solution.py:436
  124.5 4.2 %collective-permute-start.52 = (bf16[1,8,16,512]{3,2,1,0:T(8,128)(2,1)S(1)}, bf16[1,8,16,512]{3,2,1,0:T(8,128)(2,1)S(1)}, u32[]{:S(2)}, u32[]{:S(2)}) collective-permute-start(bf16[1,8,16,512]{3,2,1,0:T(8,128)(2,1)S(1)} %get-tuple-element.21), channel_id=1, source_target_pairs={{0,7},{1,6},{2,5},{3,4},{4,3},{5,2},{6,1},{7,0},{8,15},{9,14},{10,... | collective-permute-start | bytes 393224 | tf_op jit(solution)/shard_map/ppermute | solution.py:436
  132.1 9.3 %collective-permute-done.49.refs_4_ = bf16[1,8,16,512]{3,2,1,0:T(8,128)(2,1)S(1)} collective-permute-done((bf16[1,8,16,512]{3,2,1,0:T(8,128)(2,1)S(1)}, bf16[1,8,16,512]{3,2,1,0:T(8,128)(2,1)S(1)}, u32[]{:S(2)}, u32[]{:S(2)}) %collective-permute-start.49) | collective-permute-done | bytes 131104 | tf_op jit(solution)/shard_map/ppermute | solution.py:436
  141.4 2.1 %collective-permute-start.54 = (bf16[1,8,16,512]{3,2,1,0:T(8,128)(2,1)S(1)}, bf16[1,8,16,512]{3,2,1,0:T(8,128)(2,1)S(1)}, u32[]{:S(2)}, u32[]{:S(2)}) collective-permute-start(bf16[1,8,16,512]{3,2,1,0:T(8,128)(2,1)S(1)} %get-tuple-element.19), channel_id=1, source_target_pairs={{0,9},{1,8},{2,11},{3,10},{4,13},{5,12},{6,15},{7,14},{8,1},{9,0},... | collective-permute-start | bytes 393224 | tf_op jit(solution)/shard_map/ppermute | solution.py:436
  146.8 3.8 %collective-permute-start.56 = (bf16[1,8,16,512]{3,2,1,0:T(8,128)(2,1)}, bf16[1,8,16,512]{3,2,1,0:T(8,128)(2,1)S(1)}, u32[]{:S(2)}, u32[]{:S(2)}) collective-permute-start(bf16[1,8,16,512]{3,2,1,0:T(8,128)(2,1)} %get-tuple-element.17), channel_id=1, source_target_pairs={{0,11},{1,10},{2,9},{3,8},{4,15},{5,14},{6,13},{7,12},{8,3},{9,2},... | collective-permute-start | bytes 393224 | tf_op jit(solution)/shard_map/ppermute | solution.py:436
  152.2 14.2 %collective-permute-done.53.refs_8_ = bf16[1,8,16,512]{3,2,1,0:T(8,128)(2,1)S(1)} collective-permute-done((bf16[1,8,16,512]{3,2,1,0:T(8,128)(2,1)S(1)}, bf16[1,8,16,512]{3,2,1,0:T(8,128)(2,1)S(1)}, u32[]{:S(2)}, u32[]{:S(2)}) %collective-permute-start.53) | collective-permute-done | bytes 131104 | tf_op jit(solution)/shard_map/ppermute | solution.py:436
  166.4 2.4 %collective-permute-start.58 = (bf16[1,8,16,512]{3,2,1,0:T(8,128)(2,1)}, bf16[1,8,16,512]{3,2,1,0:T(8,128)(2,1)}, u32[]{:S(2)}, u32[]{:S(2)}) collective-permute-start(bf16[1,8,16,512]{3,2,1,0:T(8,128)(2,1)} %get-tuple-element.15), channel_id=1, source_target_pairs={{0,13},{1,12},{2,15},{3,14},{4,9},{5,8},{6,11},{7,10},{8,5},{9,4},... | collective-permute-start | bytes 393224 | tf_op jit(solution)/shard_map/ppermute | solution.py:436
  172.0 5.1 %collective-permute-start.60 = (bf16[1,8,16,512]{3,2,1,0:T(8,128)(2,1)}, bf16[1,8,16,512]{3,2,1,0:T(8,128)(2,1)}, u32[]{:S(2)}, u32[]{:S(2)}) collective-permute-start(bf16[1,8,16,512]{3,2,1,0:T(8,128)(2,1)} %get-tuple-element.13), channel_id=1, source_target_pairs={{0,15},{1,14},{2,13},{3,12},{4,11},{5,10},{6,9},{7,8},{8,7},{9,6},... | collective-permute-start | bytes 393224 | tf_op jit(solution)/shard_map/ppermute | solution.py:436
  177.2 2.7 %place_part.1.refs_16_ = bf16[4,4,16,8192]{3,2,1,0:T(8,128)(2,1)} custom-call(bf16[16,8,16,512]{3,2,1,0:T(8,128)(2,1)} %all-to-all-done.arrived), custom_call_target="tpu_custom_call" | custom-call | flops 1000 | bytes 1000 | tf_op jit(solution)/shard_map/place_part/pallas_call | solution.py:322
  180.7 4.7 %collective-permute-done.57.refs_12_ = bf16[1,8,16,512]{3,2,1,0:T(8,128)(2,1)} collective-permute-done((bf16[1,8,16,512]{3,2,1,0:T(8,128)(2,1)}, bf16[1,8,16,512]{3,2,1,0:T(8,128)(2,1)}, u32[]{:S(2)}, u32[]{:S(2)}) %collective-permute-start.57) | collective-permute-done | bytes 131104 | tf_op jit(solution)/shard_map/ppermute | solution.py:436
  185.4 6.6 %collective-permute-done.58.refs_13_ = bf16[1,8,16,512]{3,2,1,0:T(8,128)(2,1)} collective-permute-done((bf16[1,8,16,512]{3,2,1,0:T(8,128)(2,1)}, bf16[1,8,16,512]{3,2,1,0:T(8,128)(2,1)}, u32[]{:S(2)}, u32[]{:S(2)}) %collective-permute-start.58) | collective-permute-done | bytes 131104 | tf_op jit(solution)/shard_map/ppermute | solution.py:436
  193.7 3.0 %collective-permute-done.60.refs_15_ = bf16[1,8,16,512]{3,2,1,0:T(8,128)(2,1)} collective-permute-done((bf16[1,8,16,512]{3,2,1,0:T(8,128)(2,1)}, bf16[1,8,16,512]{3,2,1,0:T(8,128)(2,1)}, u32[]{:S(2)}, u32[]{:S(2)}) %collective-permute-start.60) | collective-permute-done | bytes 131104 | tf_op jit(solution)/shard_map/ppermute | solution.py:436
  196.6 2.7 %place_each.1 = bf16[4,4,16,8192]{3,2,1,0:T(8,128)(2,1)} custom-call(bf16[1,8,16,512]{3,2,1,0:T(8,128)(2,1)} %get-tuple-element.28.refs_0_, bf16[1,8,16,512]{3,2,1,0:T(8,128)(2,1)} %copy-done.47, bf16[1,8,16,512]{3,2,1,0:T(8,128)(2,1)} %copy-done.48, bf16[1,8,16,512]{3,2,1,0:T(8,128)(2,1)} %copy-done.49, ...), custom_call_target="tpu_custom_call", output_to_operand_aliasing={{}: (16, {})} | custom-call | flops 1000 | bytes 1000 | tf_op jit(solution)/shard_map/place_each/pallas_call | solution.py:370
  (215 shorter events, 54.1 us)
Async XLA Ops:
  5.2 9.3 %collective-permute-start.1 = (bf16[64,16,128]{2,1,0:T(8,128)(2,1)S(1)}, bf16[64,16,128]{2,1,0:T(8,128)(2,1)S(1)}, u32[]{:S(2)}, u32[]{:S(2)}) collective-permute-start(bf16[64,16,128]{2,1,0:T(8,128)(2,1)S(1)} %convolution_convert_fusion.refs_0_), channel_id=1, source_target_pairs={{0,4},{1,5},{2,6},{3,7},{4,0},{5,1},{6,2},{7,3},{8,12},{9,13},{10,... | collective-permute-start | bytes 786440 | tf_op jit(solution)/shard_map/ppermute | solution.py:51
  5.4 14.1 %collective-permute-start = (bf16[64,16,128]{2,1,0:T(8,128)(2,1)S(1)}, bf16[64,16,128]{2,1,0:T(8,128)(2,1)S(1)}, u32[]{:S(2)}, u32[]{:S(2)}) collective-permute-start(bf16[64,16,128]{2,1,0:T(8,128)(2,1)S(1)} %convolution_convert_fusion.refs_0_), channel_id=1, source_target_pairs={{0,8},{1,9},{2,10},{3,11},{4,12},{5,13},{6,14},{7,15},{8,0},{9,1},... | collective-permute-start | bytes 786440 | tf_op jit(solution)/shard_map/ppermute | solution.py:51
  19.4 14.4 %collective-permute-start.27 = (bf16[64,16,128]{2,1,0:T(8,128)(2,1)S(1)}, bf16[64,16,128]{2,1,0:T(8,128)(2,1)S(1)}, u32[]{:S(2)}, u32[]{:S(2)}) collective-permute-start(bf16[64,16,128]{2,1,0:T(8,128)(2,1)S(1)} %collective-permute-done.1.refs_8_.refs_4_), channel_id=1, source_target_pairs={{0,1},{1,0},{2,3},{3,2},{4,5},{5,4},{6,7},{7,6},{8,9},{9,8},{10,11... | collective-permute-start | bytes 786440 | tf_op jit(solution)/shard_map/ppermute | solution.py:51
  19.5 12.4 %collective-permute-start.9 = (bf16[64,16,128]{2,1,0:T(8,128)(2,1)S(1)}, bf16[64,16,128]{2,1,0:T(8,128)(2,1)S(1)}, u32[]{:S(2)}, u32[]{:S(2)}) collective-permute-start(bf16[64,16,128]{2,1,0:T(8,128)(2,1)S(1)} %convolution_convert_fusion.refs_0_), channel_id=1, source_target_pairs={{0,12},{1,13},{2,14},{3,15},{4,8},{5,9},{6,10},{7,11},{8,4},{9,5},... | collective-permute-start | bytes 786440 | tf_op jit(solution)/shard_map/ppermute | solution.py:51
  21.2 12.7 %collective-permute-start.10 = (bf16[64,16,128]{2,1,0:T(8,128)(2,1)S(1)}, bf16[64,16,128]{2,1,0:T(8,128)(2,1)S(1)}, u32[]{:S(2)}, u32[]{:S(2)}) collective-permute-start(bf16[64,16,128]{2,1,0:T(8,128)(2,1)S(1)} %collective-permute-done.refs_16_.refs_0_), channel_id=1, source_target_pairs={{0,16},{1,17},{2,18},{3,19},{4,20},{5,21},{6,22},{7,23},{8,24},{9,... | collective-permute-start | bytes 786440 | tf_op jit(solution)/shard_map/ppermute | solution.py:51
  22.1 12.3 %collective-permute-start.7 = (bf16[64,16,128]{2,1,0:T(8,128)(2,1)S(1)}, bf16[64,16,128]{2,1,0:T(8,128)(2,1)S(1)}, u32[]{:S(2)}, u32[]{:S(2)}) collective-permute-start(bf16[64,16,128]{2,1,0:T(8,128)(2,1)S(1)} %collective-permute-done.refs_16_.refs_0_), channel_id=1, source_target_pairs={{0,2},{1,3},{2,0},{3,1},{4,6},{5,7},{6,4},{7,5},{8,10},{9,11},{10,... | collective-permute-start | bytes 786440 | tf_op jit(solution)/shard_map/ppermute | solution.py:51
  22.4 13.3 %collective-permute-start.21 = (bf16[64,16,128]{2,1,0:T(8,128)(2,1)S(1)}, bf16[64,16,128]{2,1,0:T(8,128)(2,1)S(1)}, u32[]{:S(2)}, u32[]{:S(2)}) collective-permute-start(bf16[64,16,128]{2,1,0:T(8,128)(2,1)S(1)} %collective-permute-done.2.refs_1_.refs_8_), channel_id=1, source_target_pairs={{0,2},{1,3},{2,0},{3,1},{4,6},{5,7},{6,4},{7,5},{8,10},{9,11},{10,... | collective-permute-start | bytes 786440 | tf_op jit(solution)/shard_map/ppermute | solution.py:51
  36.5 8.2 %collective-permute-start.28 = (bf16[64,16,128]{2,1,0:T(8,128)(2,1)S(1)}, bf16[64,16,128]{2,1,0:T(8,128)(2,1)S(1)}, u32[]{:S(2)}, u32[]{:S(2)}) collective-permute-start(bf16[64,16,128]{2,1,0:T(8,128)(2,1)S(1)} %collective-permute-done.4.refs_9_.refs_12_), channel_id=1, source_target_pairs={{0,1},{1,0},{2,3},{3,2},{4,5},{5,4},{6,7},{7,6},{8,9},{9,8},{10,11... | collective-permute-start | bytes 786440 | tf_op jit(solution)/shard_map/ppermute | solution.py:51
  36.6 8.4 %collective-permute-start.25 = (bf16[64,16,128]{2,1,0:T(8,128)(2,1)S(1)}, bf16[64,16,128]{2,1,0:T(8,128)(2,1)S(1)}, u32[]{:S(2)}, u32[]{:S(2)}) collective-permute-start(bf16[64,16,128]{2,1,0:T(8,128)(2,1)S(1)} %collective-permute-done.21.refs_3_.refs_10_), channel_id=1, source_target_pairs={{0,1},{1,0},{2,3},{3,2},{4,5},{5,4},{6,7},{7,6},{8,9},{9,8},{10,11... | collective-permute-start | bytes 786440 | tf_op jit(solution)/shard_map/ppermute | solution.py:51
  37.0 8.4 %collective-permute-start.12 = (bf16[64,16,128]{2,1,0:T(8,128)(2,1)S(1)}, bf16[64,16,128]{2,1,0:T(8,128)(2,1)S(1)}, u32[]{:S(2)}, u32[]{:S(2)}) collective-permute-start(bf16[64,16,128]{2,1,0:T(8,128)(2,1)S(1)} %collective-permute-done.9.refs_24_.refs_4_), channel_id=1, source_target_pairs={{0,2},{1,3},{2,0},{3,1},{4,6},{5,7},{6,4},{7,5},{8,10},{9,11},{10,... | collective-permute-start | bytes 786440 | tf_op jit(solution)/shard_map/ppermute | solution.py:51
  44.7 8.0 %collective-permute-start.15 = (bf16[64,16,128]{2,1,0:T(8,128)(2,1)S(1)}, bf16[64,16,128]{2,1,0:T(8,128)(2,1)S(1)}, u32[]{:S(2)}, u32[]{:S(2)}) collective-permute-start(bf16[64,16,128]{2,1,0:T(8,128)(2,1)S(1)} %collective-permute-done.10.refs_17_.refs_8_), channel_id=1, source_target_pairs={{0,2},{1,3},{2,0},{3,1},{4,6},{5,7},{6,4},{7,5},{8,10},{9,11},{10,... | collective-permute-start | bytes 786440 | tf_op jit(solution)/shard_map/ppermute | solution.py:51
  45.0 8.5 %collective-permute-start.14 = (bf16[64,16,128]{2,1,0:T(8,128)(2,1)S(1)}, bf16[64,16,128]{2,1,0:T(8,128)(2,1)S(1)}, u32[]{:S(2)}, u32[]{:S(2)}) collective-permute-start(bf16[64,16,128]{2,1,0:T(8,128)(2,1)S(1)} %collective-permute-done.10.refs_17_.refs_8_), channel_id=1, source_target_pairs={{0,1},{1,0},{2,3},{3,2},{4,5},{5,4},{6,7},{7,6},{8,9},{9,8},{10,11... | collective-permute-start | bytes 786440 | tf_op jit(solution)/shard_map/ppermute | solution.py:51
  45.4 8.2 %collective-permute-start.8 = (bf16[64,16,128]{2,1,0:T(8,128)(2,1)S(1)}, bf16[64,16,128]{2,1,0:T(8,128)(2,1)S(1)}, u32[]{:S(2)}, u32[]{:S(2)}) collective-permute-start(bf16[64,16,128]{2,1,0:T(8,128)(2,1)S(1)} %collective-permute-done.7.refs_18_.refs_2_), channel_id=1, source_target_pairs={{0,1},{1,0},{2,3},{3,2},{4,5},{5,4},{6,7},{7,6},{8,9},{9,8},{10,11... | collective-permute-start | bytes 786440 | tf_op jit(solution)/shard_map/ppermute | solution.py:51
  69.7 7.9 %collective-permute-start.35 = (bf16[16,16,128]{2,1,0:T(8,128)(2,1)}, bf16[16,16,128]{2,1,0:T(8,128)(2,1)S(1)}, u32[]{:S(2)}, u32[]{:S(2)}) collective-permute-start(bf16[16,16,128]{2,1,0:T(8,128)(2,1)} %level_block.1.refs_16_), channel_id=1, source_target_pairs={{0,10},{1,11},{2,8},{3,9},{4,14},{5,15},{6,12},{7,13},{8,2},{9,3},... | collective-permute-start | bytes 196616 | tf_op jit(solution)/shard_map/ppermute | solution.py:139
  70.6 10.2 %collective-permute-start.36 = (bf16[16,16,128]{2,1,0:T(8,128)(2,1)}, bf16[16,16,128]{2,1,0:T(8,128)(2,1)S(1)}, u32[]{:S(2)}, u32[]{:S(2)}) collective-permute-start(bf16[16,16,128]{2,1,0:T(8,128)(2,1)} %level_block.1.refs_16_), channel_id=1, source_target_pairs={{0,12},{1,13},{2,14},{3,15},{4,8},{5,9},{6,10},{7,11},{8,4},{9,5},... | collective-permute-start | bytes 196616 | tf_op jit(solution)/shard_map/ppermute | solution.py:139
  71.3 11.7 %collective-permute-start.37 = (bf16[16,16,128]{2,1,0:T(8,128)(2,1)}, bf16[16,16,128]{2,1,0:T(8,128)(2,1)S(1)}, u32[]{:S(2)}, u32[]{:S(2)}) collective-permute-start(bf16[16,16,128]{2,1,0:T(8,128)(2,1)} %level_block.1.refs_16_), channel_id=1, source_target_pairs={{0,14},{1,15},{2,12},{3,13},{4,10},{5,11},{6,8},{7,9},{8,6},{9,7},... | collective-permute-start | bytes 196616 | tf_op jit(solution)/shard_map/ppermute | solution.py:139
  73.1 10.3 %collective-permute-start.38 = (bf16[16,16,128]{2,1,0:T(8,128)(2,1)}, bf16[16,16,128]{2,1,0:T(8,128)(2,1)S(1)}, u32[]{:S(2)}, u32[]{:S(2)}) collective-permute-start(bf16[16,16,128]{2,1,0:T(8,128)(2,1)} %level_block.1.refs_16_), channel_id=1, source_target_pairs={{0,1},{1,0},{2,3},{3,2},{4,5},{5,4},{6,7},{7,6},{8,9},{9,8},{10,11... | collective-permute-start | bytes 196616 | tf_op jit(solution)/shard_map/ppermute | solution.py:133
  75.1 8.4 %collective-permute-start.39 = (bf16[16,16,128]{2,1,0:T(8,128)(2,1)S(1)}, bf16[16,16,128]{2,1,0:T(8,128)(2,1)S(1)}, u32[]{:S(2)}, u32[]{:S(2)}) collective-permute-start(bf16[16,16,128]{2,1,0:T(8,128)(2,1)S(1)} %collective-permute-done.31.refs_17_), channel_id=1, source_target_pairs={{0,1},{1,0},{2,3},{3,2},{4,5},{5,4},{6,7},{7,6},{8,9},{9,8},{10,11... | collective-permute-start | bytes 196616 | tf_op jit(solution)/shard_map/ppermute | solution.py:133
  98.3 78.9 %all-to-all-start = ((bf16[16,8,16,512]{3,2,1,0:T(8,128)(2,1)}), bf16[16,8,16,512]{3,2,1,0:T(8,128)(2,1)}, u32[]{:S(2)}, u32[]{:S(2)}) async-start(bf16[16,8,16,512]{3,2,1,0:T(8,128)(2,1)} %leaf_part.3), calls=%async_computation | async-start | bytes 4194304 | tf_op jit(solution)/shard_map/all_to_all | solution.py:428
  119.1 11.0 %collective-permute-start.48 = (bf16[1,8,16,512]{3,2,1,0:T(8,128)(2,1)S(1)}, bf16[1,8,16,512]{3,2,1,0:T(8,128)(2,1)S(1)}, u32[]{:S(2)}, u32[]{:S(2)}) collective-permute-start(bf16[1,8,16,512]{3,2,1,0:T(8,128)(2,1)S(1)} %get-tuple-element.25), channel_id=1, source_target_pairs={{0,3},{1,2},{2,1},{3,0},{4,7},{5,6},{6,5},{7,4},{8,11},{9,10},{10,... | collective-permute-start | bytes 393224 | tf_op jit(solution)/shard_map/ppermute | solution.py:436
  120.4 21.1 %collective-permute-start.49 = (bf16[1,8,16,512]{3,2,1,0:T(8,128)(2,1)S(1)}, bf16[1,8,16,512]{3,2,1,0:T(8,128)(2,1)S(1)}, u32[]{:S(2)}, u32[]{:S(2)}) collective-permute-start(bf16[1,8,16,512]{3,2,1,0:T(8,128)(2,1)S(1)} %get-tuple-element.24), channel_id=1, source_target_pairs={{0,4},{1,5},{2,6},{3,7},{4,0},{5,1},{6,2},{7,3},{8,12},{9,13},{10,... | collective-permute-start | bytes 393224 | tf_op jit(solution)/shard_map/ppermute | solution.py:436
  120.7 24.5 %collective-permute-start.50 = (bf16[1,8,16,512]{3,2,1,0:T(8,128)(2,1)S(1)}, bf16[1,8,16,512]{3,2,1,0:T(8,128)(2,1)S(1)}, u32[]{:S(2)}, u32[]{:S(2)}) collective-permute-start(bf16[1,8,16,512]{3,2,1,0:T(8,128)(2,1)S(1)} %get-tuple-element.23), channel_id=1, source_target_pairs={{0,5},{1,4},{2,7},{3,6},{4,1},{5,0},{6,3},{7,2},{8,13},{9,12},{10,... | collective-permute-start | bytes 393224 | tf_op jit(solution)/shard_map/ppermute | solution.py:436
  122.1 24.8 %collective-permute-start.51 = (bf16[1,8,16,512]{3,2,1,0:T(8,128)(2,1)S(1)}, bf16[1,8,16,512]{3,2,1,0:T(8,128)(2,1)S(1)}, u32[]{:S(2)}, u32[]{:S(2)}) collective-permute-start(bf16[1,8,16,512]{3,2,1,0:T(8,128)(2,1)S(1)} %get-tuple-element.22), channel_id=1, source_target_pairs={{0,6},{1,7},{2,4},{3,5},{4,2},{5,3},{6,0},{7,1},{8,14},{9,15},{10,... | collective-permute-start | bytes 393224 | tf_op jit(solution)/shard_map/ppermute | solution.py:436
  124.5 27.0 %collective-permute-start.52 = (bf16[1,8,16,512]{3,2,1,0:T(8,128)(2,1)S(1)}, bf16[1,8,16,512]{3,2,1,0:T(8,128)(2,1)S(1)}, u32[]{:S(2)}, u32[]{:S(2)}) collective-permute-start(bf16[1,8,16,512]{3,2,1,0:T(8,128)(2,1)S(1)} %get-tuple-element.21), channel_id=1, source_target_pairs={{0,7},{1,6},{2,5},{3,4},{4,3},{5,2},{6,1},{7,0},{8,15},{9,14},{10,... | collective-permute-start | bytes 393224 | tf_op jit(solution)/shard_map/ppermute | solution.py:436
  130.2 36.2 %collective-permute-start.53 = (bf16[1,8,16,512]{3,2,1,0:T(8,128)(2,1)S(1)}, bf16[1,8,16,512]{3,2,1,0:T(8,128)(2,1)S(1)}, u32[]{:S(2)}, u32[]{:S(2)}) collective-permute-start(bf16[1,8,16,512]{3,2,1,0:T(8,128)(2,1)S(1)} %get-tuple-element.20), channel_id=1, source_target_pairs={{0,8},{1,9},{2,10},{3,11},{4,12},{5,13},{6,14},{7,15},{8,0},{9,1},... | collective-permute-start | bytes 393224 | tf_op jit(solution)/shard_map/ppermute | solution.py:436
  141.4 27.9 %collective-permute-start.54 = (bf16[1,8,16,512]{3,2,1,0:T(8,128)(2,1)S(1)}, bf16[1,8,16,512]{3,2,1,0:T(8,128)(2,1)S(1)}, u32[]{:S(2)}, u32[]{:S(2)}) collective-permute-start(bf16[1,8,16,512]{3,2,1,0:T(8,128)(2,1)S(1)} %get-tuple-element.19), channel_id=1, source_target_pairs={{0,9},{1,8},{2,11},{3,10},{4,13},{5,12},{6,15},{7,14},{8,1},{9,0},... | collective-permute-start | bytes 393224 | tf_op jit(solution)/shard_map/ppermute | solution.py:436
  145.2 26.8 %collective-permute-start.55 = (bf16[1,8,16,512]{3,2,1,0:T(8,128)(2,1)S(1)}, bf16[1,8,16,512]{3,2,1,0:T(8,128)(2,1)S(1)}, u32[]{:S(2)}, u32[]{:S(2)}) collective-permute-start(bf16[1,8,16,512]{3,2,1,0:T(8,128)(2,1)S(1)} %get-tuple-element.18), channel_id=1, source_target_pairs={{0,10},{1,11},{2,8},{3,9},{4,14},{5,15},{6,12},{7,13},{8,2},{9,3},... | collective-permute-start | bytes 393224 | tf_op jit(solution)/shard_map/ppermute | solution.py:436
  146.8 33.9 %collective-permute-start.56 = (bf16[1,8,16,512]{3,2,1,0:T(8,128)(2,1)}, bf16[1,8,16,512]{3,2,1,0:T(8,128)(2,1)S(1)}, u32[]{:S(2)}, u32[]{:S(2)}) collective-permute-start(bf16[1,8,16,512]{3,2,1,0:T(8,128)(2,1)} %get-tuple-element.17), channel_id=1, source_target_pairs={{0,11},{1,10},{2,9},{3,8},{4,15},{5,14},{6,13},{7,12},{8,3},{9,2},... | collective-permute-start | bytes 393224 | tf_op jit(solution)/shard_map/ppermute | solution.py:436
  151.5 33.8 %collective-permute-start.57 = (bf16[1,8,16,512]{3,2,1,0:T(8,128)(2,1)}, bf16[1,8,16,512]{3,2,1,0:T(8,128)(2,1)}, u32[]{:S(2)}, u32[]{:S(2)}) collective-permute-start(bf16[1,8,16,512]{3,2,1,0:T(8,128)(2,1)} %get-tuple-element.16), channel_id=1, source_target_pairs={{0,12},{1,13},{2,14},{3,15},{4,8},{5,9},{6,10},{7,11},{8,4},{9,5},... | collective-permute-start | bytes 393224 | tf_op jit(solution)/shard_map/ppermute | solution.py:436
  166.4 25.5 %collective-permute-start.58 = (bf16[1,8,16,512]{3,2,1,0:T(8,128)(2,1)}, bf16[1,8,16,512]{3,2,1,0:T(8,128)(2,1)}, u32[]{:S(2)}, u32[]{:S(2)}) collective-permute-start(bf16[1,8,16,512]{3,2,1,0:T(8,128)(2,1)} %get-tuple-element.15), channel_id=1, source_target_pairs={{0,13},{1,12},{2,15},{3,14},{4,9},{5,8},{6,11},{7,10},{8,5},{9,4},... | collective-permute-start | bytes 393224 | tf_op jit(solution)/shard_map/ppermute | solution.py:436
  169.3 24.3 %collective-permute-start.59 = (bf16[1,8,16,512]{3,2,1,0:T(8,128)(2,1)}, bf16[1,8,16,512]{3,2,1,0:T(8,128)(2,1)}, u32[]{:S(2)}, u32[]{:S(2)}) collective-permute-start(bf16[1,8,16,512]{3,2,1,0:T(8,128)(2,1)} %get-tuple-element.14), channel_id=1, source_target_pairs={{0,14},{1,15},{2,12},{3,13},{4,10},{5,11},{6,8},{7,9},{8,6},{9,7},... | collective-permute-start | bytes 393224 | tf_op jit(solution)/shard_map/ppermute | solution.py:436
  172.0 24.6 %collective-permute-start.60 = (bf16[1,8,16,512]{3,2,1,0:T(8,128)(2,1)}, bf16[1,8,16,512]{3,2,1,0:T(8,128)(2,1)}, u32[]{:S(2)}, u32[]{:S(2)}) collective-permute-start(bf16[1,8,16,512]{3,2,1,0:T(8,128)(2,1)} %get-tuple-element.13), channel_id=1, source_target_pairs={{0,15},{1,14},{2,13},{3,12},{4,11},{5,10},{6,9},{7,8},{8,7},{9,6},... | collective-permute-start | bytes 393224 | tf_op jit(solution)/shard_map/ppermute | solution.py:436
  (88 other events, 1093.5 us)
